TPU v7x, 32 devices: a whole 2x2x4 slice. The times are simulated.
32 devices in a mesh: groups: 2 (over x), replica: 2 (over core), tensor: 8 (over z, y).
Axes of the slice: x: 2, y: 2, z: 4, core: 2. Of those that a mesh axis runs over, the one named last changes fastest.
Arguments:
- queries: bfloat16 [2, 64, 8192], P(None, ('groups', 'replica'), 'tensor'), parts along dimension 1, may hold values from -8 to 8
- latest_key_value: bfloat16 [2, 64, 8, 256], P(None, ('groups', 'replica'), 'tensor'), parts along dimension 1, may hold values from -6 to 6, as said below
- residual: bfloat16 [2, 64, 8192], P(None, ('groups', 'replica'), 'tensor'), parts along dimension 1, may hold values from -3 to 3
- paged_cache_pool: bfloat16 [512, 8, 64, 256], P(('groups', 'replica'), 'tensor'), parts along dimension 0, may hold values from -6 to 6, as said below
- adapter_down_weight: bfloat16 [16, 64, 8192], P(('groups', 'replica'), None, 'tensor'), parts along dimension 0, may hold values from -0.5 to 0.5
- adapter_up_weight: bfloat16 [16, 64, 8192], P(('groups', 'replica'), None, 'tensor'), parts along dimension 0, may hold values from -0.375 to 0.375
- output_weight: bfloat16 [8192, 8192], P('tensor'), may hold values from -0.5 to 0.5
- lengths: int32 [64], P('groups'), parts along dimension 0, may hold values from 1 to 512, as said below
- previous_block_table: int32 [64, 8], P('groups'), parts along dimension 0, may hold values from 0 to 127, as said below
- request_order_after: int32 [64], P('groups'), parts along dimension 0, may hold values from 0 to 31, as said below
- request_adapter_index: int32 [64], P('groups'), parts along dimension 0, may hold values from 0 to 3
Outputs:
- layer_out: bfloat16 [2, 64, 8192], P(None, ('groups', 'replica'), 'tensor'), parts along dimension 1
- placed_cache: bfloat16 [64, 8, 8, 64, 256], P(('groups', 'replica'), None, 'tensor'), parts along dimension 0
There are 2 independent parts, one for each index of `groups`. A program takes and returns all parts, laid end to end along the dimension named above; an argument that names none is the same for every part. Nothing has to cross between parts.
Inputs may be any that keep to these rules, and one draw needn't show every extreme that they name: `lengths`: request 0 has exactly 512. `previous_block_table`: block numbers in the holder's own pool; the blocks of the 16 requests of one replica are all different. `request_order_after`: A permutation; of the 16 requests at the new places of each replica exactly 8 are held by another replica. `request_adapter_index`: A slot of the holder's own adapter pool. `paged_cache_pool`: each key and value head is stored in 1 equal copies, side by side. `latest_key_value`: each key and value head is given in 1 equal copies, side by side.
All inputs are finite; a program needn't handle non-finite values.
Results may differ from a plain program's by a relative error of at most 0.006.
Values may be sent and summed in bfloat16 or wider, within the bound.
No kernel may reach another device: no remote copies, remote signals or barrier semaphores. Data moves between devices by JAX's collectives and lax.ppermute only.
A program may use at most 128 MiB of HBM per device.

v0:
```python
import jax
import jax.numpy as jnp
from jax import lax
from jax.sharding import PartitionSpec as P

adapter_scale = 2.0


def as_sent(value):

    def short(part):
        return part.astype(jnp.bfloat16) if part.dtype == jnp.float32 else part

    return jax.tree.map(short, value)


def serve_step(
    query_rows,
    cache_rows,
    new_lengths,
    fresh_rows,
    residual_stream_rows,
    lowered_rows,
    raised_rows,
    output_weight,
):
    row_count, features = query_rows.shape
    stored = cache_rows.shape[2]
    block_size = cache_rows.shape[3]
    block_count = cache_rows.shape[1]
    head_dim = cache_rows.shape[4] // 2
    group_size = features // (stored * head_dim)
    head_query = query_rows.reshape(row_count, stored, group_size, head_dim)
    scale = head_dim ** (-0.5)
    scores = (
        jnp.einsum(
            "rsgd,rbstd->rsgbt",
            head_query,
            cache_rows[..., :head_dim],
            preferred_element_type=jnp.float32,
        )
        * scale
    )
    positions = (
        jnp.arange(block_count, dtype=jnp.int32)[:, None] * block_size
        + jnp.arange(block_size, dtype=jnp.int32)[None, :]
    )
    inside = positions[None] < new_lengths[:, None, None]
    scores = jnp.where(inside[:, None, None], scores, jnp.float32(-1e30))
    fresh_scores = [
        jnp.einsum(
            "rsgd,rsd->rsg", head_query, row[..., :head_dim], preferred_element_type=jnp.float32
        )
        * scale
        for row in fresh_rows
    ]
    top_score = jnp.max(scores, axis=(3, 4))
    for extra in fresh_scores:
        top_score = jnp.maximum(top_score, extra)
    weights = jnp.exp(scores - top_score[..., None, None])
    fresh_weights = [jnp.exp(extra - top_score) for extra in fresh_scores]
    totals = jnp.sum(weights, axis=(3, 4))
    for extra in fresh_weights:
        totals = totals + extra
    probabilities = (weights / totals[..., None, None]).astype(jnp.bfloat16)
    attended = jnp.einsum(
        "rsgbt,rbstd->rsgd",
        probabilities,
        cache_rows[..., head_dim:],
        preferred_element_type=jnp.float32,
    )
    for extra, row in zip(fresh_weights, fresh_rows):
        share = lax.optimization_barrier((extra / totals).astype(jnp.bfloat16)).astype(jnp.float32)
        attended = attended + share[..., None] * row[:, :, None, head_dim:].astype(jnp.float32)
    attended = attended.reshape(row_count, features).astype(jnp.bfloat16)
    partial_terms = jnp.dot(attended, output_weight, preferred_element_type=jnp.float32)
    output_projected = lax.psum_scatter(partial_terms, "tensor", scatter_dimension=1, tiled=True)
    shrink_terms = jnp.einsum(
        "rc,rkc->rk", attended, lowered_rows, preferred_element_type=jnp.float32
    )
    shrink = lax.psum(shrink_terms, "tensor").astype(jnp.bfloat16)
    widen_back = jnp.einsum("rk,rkc->rc", shrink, raised_rows, preferred_element_type=jnp.float32)
    combined_output = (
        residual_stream_rows.astype(jnp.float32) + output_projected + adapter_scale * widen_back
    )
    return combined_output.astype(jnp.bfloat16)


def shards(
    queries,
    latest_key_value,
    residual,
    paged_cache_pool,
    adapter_down_weight,
    adapter_up_weight,
    output_weight,
    lengths,
    previous_block_table,
    request_order_after,
    request_adapter_index,
):
    row_count = queries.shape[1]
    half_rows = row_count // 2
    replicas = lax.axis_size("replica")
    own_index = lax.axis_index("replica")
    first_row = own_index * row_count
    layout_rows = request_order_after.reshape(replicas, row_count)
    moved_all = layout_rows // row_count != jnp.arange(replicas, dtype=jnp.int32)[:, None]
    arrival_rank = jnp.cumsum(moved_all.astype(jnp.int32), axis=1) - 1
    picker = (
        arrival_rank[:, None, :] == jnp.arange(half_rows, dtype=jnp.int32)[None, :, None]
    ) & moved_all[:, None, :]
    moved_ids = jnp.sum(jnp.where(picker, layout_rows[:, None, :], 0), axis=2)
    from_here = moved_ids // row_count == own_index
    departing_rows = jnp.clip(moved_ids - first_row, 0, row_count - 1)
    own_tables = lax.dynamic_slice_in_dim(previous_block_table, first_row, row_count, 0)
    holder_adapter_indices = lax.dynamic_slice_in_dim(
        request_adapter_index, first_row, row_count, 0
    )
    my_moved = moved_ids[own_index]
    source_rank = my_moved // row_count
    within = jnp.arange(half_rows, dtype=jnp.int32)
    placed_ids = lax.dynamic_slice_in_dim(request_order_after, first_row, row_count, 0)
    moved_here = placed_ids // row_count != own_index
    arrival_slot = jnp.clip(jnp.cumsum(moved_here.astype(jnp.int32)) - 1, 0, half_rows - 1)
    resident_rows = jnp.clip(placed_ids - first_row, 0, row_count - 1)

    def departing_requests(values):
        flags = from_here.reshape(from_here.shape + (1,) * (values.ndim - 2))
        return jnp.where(flags, values, jnp.zeros_like(values))

    def finish_relocation(incoming, local_values):
        flags = moved_here.reshape(moved_here.shape + (1,) * (local_values.ndim - 1))
        return jnp.where(flags, incoming[arrival_slot], local_values)

    send_blocks = departing_requests(paged_cache_pool[own_tables[departing_rows]])
    send_queries = departing_requests(jnp.moveaxis(queries[:, departing_rows], 0, 2))
    send_fresh = departing_requests(jnp.moveaxis(latest_key_value[:, departing_rows], 0, 2))
    send_residual = departing_requests(jnp.moveaxis(residual[:, departing_rows], 0, 2))
    parcel = (send_blocks, send_queries, send_fresh, send_residual)
    parcel = parcel + (
        departing_requests(adapter_down_weight[holder_adapter_indices[departing_rows]]),
        departing_requests(adapter_up_weight[holder_adapter_indices[departing_rows]]),
    )
    landed_requests = jax.tree.map(
        lambda part, own: part.astype(own.dtype),
        lax.all_to_all(as_sent(parcel), "replica", split_axis=0, concat_axis=0, tiled=True),
        parcel,
    )
    landed_requests = tuple((item[source_rank, within] for item in landed_requests))
    placed_blocks = finish_relocation(
        landed_requests[0], paged_cache_pool[own_tables[resident_rows]]
    )
    new_lengths = lengths[placed_ids]
    block_size = paged_cache_pool.shape[2]
    positions = (
        jnp.arange(placed_blocks.shape[1], dtype=jnp.int32)[:, None] * block_size
        + jnp.arange(block_size, dtype=jnp.int32)[None, :]
    )
    inside = positions[None] < new_lengths[:, None, None]
    placed_cache = jnp.where(
        inside[:, :, None, :, None], placed_blocks, jnp.zeros_like(placed_blocks)
    )
    step_queries = finish_relocation(
        landed_requests[1], jnp.moveaxis(queries[:, resident_rows], 0, 1)
    )
    step_fresh = finish_relocation(
        landed_requests[2], jnp.moveaxis(latest_key_value[:, resident_rows], 0, 1)
    )
    step_residual = finish_relocation(
        landed_requests[3], jnp.moveaxis(residual[:, resident_rows], 0, 1)
    )
    lowered_rows = finish_relocation(
        landed_requests[4], adapter_down_weight[holder_adapter_indices[resident_rows]]
    )
    raised_rows = finish_relocation(
        landed_requests[5], adapter_up_weight[holder_adapter_indices[resident_rows]]
    )
    first_out = serve_step(
        step_queries[:, 0],
        placed_blocks,
        new_lengths,
        [step_fresh[:, 0]],
        step_residual[:, 0],
        lowered_rows,
        raised_rows,
        output_weight,
    )
    second_out = serve_step(
        step_queries[:, 1],
        placed_blocks,
        new_lengths,
        [step_fresh[:, 0], step_fresh[:, 1]],
        step_residual[:, 1],
        lowered_rows,
        raised_rows,
        output_weight,
    )
    layer_out = jnp.stack([first_out, second_out])
    return (layer_out, placed_cache)


def solution(mesh):
    in_specs = (
        P(None, ("groups", "replica"), "tensor"),
        P(None, ("groups", "replica"), "tensor", None),
        P(None, ("groups", "replica"), "tensor"),
        P(("groups", "replica"), "tensor", None, None),
        P(("groups", "replica"), None, "tensor"),
        P(("groups", "replica"), None, "tensor"),
        P("tensor", None),
        P("groups"),
        P("groups", None),
        P("groups"),
        P("groups"),
    )
    out_specs = (
        P(None, ("groups", "replica"), "tensor"),
        P(("groups", "replica"), None, "tensor", None, None),
    )
    return jax.shard_map(shards, mesh=mesh, in_specs=in_specs, out_specs=out_specs, check_vma=False)
```

profile of v0, /device:TPU:0, one launch (start us, length us, event | category | flops | bytes accessed | tf_op | source)
XLA Modules:
  0.0 232.1 jit_solution(13179776492569065762)
XLA Ops:
  10.1 5.0 %gather_fusion.10 = bf16[128,64,256]{2,1,0:T(8,128)(2,1)} fusion(bf16[128,64,256]{2,1,0:T(8,128)(2,1)} %bitcast.237, s32[1024]{0:T(1024)S(1)} %pad_clamp_fusion.3), kind=kCustom, calls=%fused_computation.10 | custom fusion | bytes 8389120 | tf_op jit(solution)/shard_map/gather | solution.py:136
  15.2 4.5 %broadcast_select_fusion = bf16[2,8,8,1,64,256]{5,4,2,1,3,0:T(8,128)(2,1)} fusion(bf16[2,8,8,1,64,256]{5,4,2,1,3,0:T(8,128)(2,1)} %bitcast.239, pred[2,8]{1,0:T(4,128)(4,1)S(1)} %fusion.52), kind=kLoop, calls=%fused_computation.31 | loop fusion | flops 2097152 | bytes 8388624 | tf_op jit(solution)/shard_map/jit(_where)/select_n | solution.py:130
  19.7 5.7 %all-to-all-start.2 = ((bf16[2,8,8,1,64,256]{5,4,2,1,3,0:T(8,128)(2,1)}), bf16[2,8,8,1,64,256]{5,4,2,1,3,0:T(8,128)(2,1)}, u32[]{:S(2)}, u32[]{:S(2)}) async-start(bf16[2,8,8,1,64,256]{5,4,2,1,3,0:T(8,128)(2,1)} %broadcast_select_fusion), calls=%async_computation.2 | async-start | bytes 8388608 | tf_op jit(solution)/shard_map/all_to_all | solution.py:147
  31.4 2.0 gather_fusion.20
  33.4 2.0 gather_fusion.25
  36.1 5.0 %gather_fusion.14 = bf16[128,64,256]{2,1,0:T(8,128)(2,1)} fusion(bf16[128,64,256]{2,1,0:T(8,128)(2,1)} %bitcast.238, s32[1024]{0:T(1024)S(1)} %pad_clamp_fusion.2), kind=kCustom, calls=%fused_computation.14 | custom fusion | bytes 8389120 | tf_op jit(solution)/shard_map/gather | solution.py:152
  42.0 3.3 %all-to-all-start = ((bf16[2,8,2,1024]{3,2,1,0:T(2,128)(2,1)}), bf16[2,8,2,1024]{3,2,1,0:T(2,128)(2,1)S(1)}, u32[]{:S(2)}, u32[]{:S(2)}) async-start(bf16[2,8,2,1024]{3,2,1,0:T(2,128)(2,1)} %get-tuple-element.36), calls=%async_computation | async-start | bytes 131072 | tf_op jit(solution)/shard_map/all_to_all | solution.py:147
  45.3 2.9 %gather_fusion.11 = bf16[8,8,64,256]{3,2,1,0:T(8,128)(2,1)S(1)} fusion(bf16[2,8,8,64,256]{4,3,2,1,0:T(8,128)(2,1)} %bitcast.11, s32[8]{0:T(128)S(1)} %fusion.56), kind=kCustom, calls=%fused_computation.11 | custom fusion | bytes 4194368 | tf_op jit(solution)/shard_map/gather | solution.py:150
  48.2 2.8 %gather_fusion.12 = bf16[16,8,64,256]{3,2,1,0:T(8,128)(2,1)} fusion(bf16[8,8,64,256]{3,2,1,0:T(8,128)(2,1)S(1)} %gather_fusion.11, s32[1024]{0:T(1024)S(1)} %pad_clamp_fusion.6), kind=kCustom, calls=%fused_computation.12 | custom fusion | bytes 8388672 | tf_op jit(solution)/shard_map/gather | solution.py:134
  50.9 3.3 %all-to-all-start.1 = ((bf16[2,8,2,1024]{3,2,1,0:T(2,128)(2,1)}), bf16[2,8,2,1024]{3,2,1,0:T(2,128)(2,1)S(1)}, u32[]{:S(2)}, u32[]{:S(2)}) async-start(bf16[2,8,2,1024]{3,2,1,0:T(2,128)(2,1)} %get-tuple-element.37), calls=%async_computation.1 | async-start | bytes 131072 | tf_op jit(solution)/shard_map/all_to_all | solution.py:147
  56.3 3.2 %all-to-all-start.3 = ((bf16[2,8,2,1,256]{4,2,1,3,0:T(2,128)(2,1)}), bf16[2,8,2,1,256]{4,2,1,3,0:T(2,128)(2,1)S(1)}, u32[]{:S(2)}, u32[]{:S(2)}) async-start(bf16[2,8,2,1,256]{4,2,1,3,0:T(2,128)(2,1)} %fusion.35), calls=%async_computation.3 | async-start | bytes 32768 | tf_op jit(solution)/shard_map/all_to_all | solution.py:147
  60.9 4.6 %broadcast_select_fusion.4 = (bf16[2,8,64,1024]{3,2,1,0:T(8,128)(2,1)}, bf16[2,8,64,1024]{3,2,1,0:T(8,128)(2,1)}) fusion(bf16[2,8,64,1024]{3,2,1,0:T(8,128)(2,1)} %bitcast.241, pred[2,8]{1,0:T(4,128)(4,1)S(1)} %fusion.52, bf16[2,8,64,1024]{3,2,1,0:T(8,128)(2,1)} %bitcast.242), kind=kLoop, calls=%fused_computation.37 | loop fusion | flops 2097152 | bytes 8388624 | tf_op jit(solution)/shard_map/jit(_where)/select_n | solution.py:130
  65.5 3.9 %all-to-all-start.4 = ((bf16[2,8,64,1024]{3,2,1,0:T(8,128)(2,1)}), bf16[2,8,64,1024]{3,2,1,0:T(8,128)(2,1)S(1)}, u32[]{:S(2)}, u32[]{:S(2)}) async-start(bf16[2,8,64,1024]{3,2,1,0:T(8,128)(2,1)} %get-tuple-element.40), calls=%async_computation.5 | async-start | bytes 4194304 | tf_op jit(solution)/shard_map/all_to_all | solution.py:147
  71.6 6.2 %select_bitcast_fusion = (bf16[16,8,1,64,256]{4,3,2,1,0:T(8,128)(2,1)}, bf16[16,8,1,64,256]{4,3,1,0,2:T(8,128)(2,1)S(1)}) fusion(pred[16,8,64]{2,1,0:T(8,128)(4,1)S(1)} %broadcast_compare_fusion, bf16[16,8,1,64,256]{4,3,1,0,2:T(8,128)(2,1)} %bitcast.240, bf16[16,8,64,256]{3,2,1,0:T(8,128)(2,1)} %gather_fusion.12, pred[16]{0:T(512)(128)(4,1)S(1)} %get-tuple-element.19), kind=kLoop, calls=%fused_computation.30 | loop fusion | flops 4194304 | bytes 16785424
  77.8 1.9 copy-done.5
  79.8 1.8 fusion.62
  82.8 2.4 %fusion.13 = bf16[16,8,128]{2,1,0:T(8,128)(2,1)S(1)} fusion(bf16[16,8,1,64,256]{4,3,1,0,2:T(8,128)(2,1)} %copy-done.5, f32[16,8,8,64]{3,1,2,0:T(8,128)} %copy-done.8, f32[16,8]{1,0:T(8,128)S(1)} %get-tuple-element.27, f32[16,8]{1,0:T(8,128)S(1)} %multiply_maximum_fusion, f32[16,128]{1,0:T(8,128)S(1)} %get-tuple-element.30, f32[16,8]{1,0:T(8,128)S(1)} %copy.107), kind=kOutput, calls=%fused_computation.51 | convolution fusion | flops 17022976 | bytes 2663936 | tf_op jit(solution)/shard_map/rsgbt,rbstd->rsgd/dot_general | solution.py:66
  85.3 8.9 %fusion.30 = f32[16,8192]{1,0:T(8,128)} fusion(bf16[1024,8192]{1,0:T(8,128)(2,1)} %param.17, bf16[2,8,8,128]{3,2,1,0:T(8,128)(2,1)S(1)} %bitcast.245), kind=kOutput, calls=%fused_computation.81 | convolution fusion | flops 268435456 | bytes 17334272 | tf_op jit(solution)/shard_map/dot_general | solution.py:76
  94.4 3.4 %fusion.61 = (f32[16,8]{1,0:T(8,128)S(1)}, f32[16,8,8,64]{3,1,2,0:T(8,128)S(1)}) fusion(bf16[16,8,1,64,256]{4,3,1,0,2:T(8,128)(2,1)} %copy-done.5, bf16[16,8,128,1]{2,1,0,3:T(8,128)(2,1)S(1)} %bitcast.251, pred[16,8,64]{2,1,0:T(8,128)(4,1)S(1)} %broadcast_compare_fusion), kind=kOutput, calls=%fused_computation.181 | convolution fusion | flops 16973696 | bytes 2400768 | tf_op jit(solution)/shard_map/rsgd,rbstd->rsgbt/dot_general | solution.py:36
  99.3 2.4 %fusion.14 = bf16[16,8,128]{2,1,0:T(8,128)(2,1)S(1)} fusion(bf16[16,8,1,64,256]{4,3,1,0,2:T(8,128)(2,1)} %copy-done.5, f32[16,8,8,64]{3,1,2,0:T(8,128)} %copy-done.7, f32[16,8]{1,0:T(8,128)S(1)} %get-tuple-element.17, f32[16,8]{1,0:T(8,128)S(1)} %maximum_maximum_fusion, f32[16,128]{1,0:T(8,128)S(1)} %get-tuple-element.32, f32[16,8]{1,0:T(8,128)S(1)} %copy.114, ...), kind=kOutput, calls=%fused_computation.52 | convolution fusion | flops 17055744 | bytes 2672640 | tf_op jit(solution)/shard_map/rsgbt,rbstd->rsgd/dot_general | solution.py:66
  101.7 8.9 %fusion.27 = f32[16,8192]{1,0:T(8,128)} fusion(bf16[1024,8192]{1,0:T(8,128)(2,1)} %param.17, bf16[2,8,8,128]{3,2,1,0:T(8,128)(2,1)S(1)} %bitcast.246), kind=kOutput, calls=%fused_computation.78 | convolution fusion | flops 268435456 | bytes 17334272 | tf_op jit(solution)/shard_map/dot_general | solution.py:76
  111.5 2.0 gather_fusion.24
  113.5 2.0 gather_fusion.28
  115.6 1.3 copy-done.6
  116.9 4.9 %all-to-all-start.5 = ((bf16[2,8,64,1024]{3,2,1,0:T(8,128)(2,1)}), bf16[2,8,64,1024]{3,2,1,0:T(8,128)(2,1)}, u32[]{:S(2)}, u32[]{:S(2)}) async-start(bf16[2,8,64,1024]{3,2,1,0:T(8,128)(2,1)} %get-tuple-element.41), calls=%async_computation.6 | async-start | bytes 4194304 | tf_op jit(solution)/shard_map/all_to_all | solution.py:147
  121.8 2.2 gather_fusion.21
  124.1 2.0 gather_fusion.22
  126.1 2.2 gather_fusion.26
  128.3 2.0 gather_fusion.27
  130.3 4.0 %broadcast_select_fusion.2 = (bf16[16,64,1024]{2,1,0:T(8,128)(2,1)S(1)}, bf16[16,64,1024]{2,1,0:T(8,128)(2,1)S(1)}) fusion(bf16[16,64,1024]{2,1,0:T(8,128)(2,1)} %gather_fusion.22, bf16[16,64,1024]{2,1,0:T(8,128)(2,1)} %gather_fusion.24, pred[16]{0:T(512)(128)(4,1)S(1)} %get-tuple-element.19, bf16[16,64,1024]{2,1,0:T(8,128)(2,1)} %gather_fusion.27, ...), kind=kLoop, calls=%fused_computation.35 | loop fusion | flops 2097152 | bytes 12582928 | tf_op jit(solution)/shard_map/jit(_where)/select_n | solution.py:134
  135.6 38.9 %all-reduce = (bf16[16,64]{1,0:T(8,128)(2,1)S(1)}, bf16[16,64]{1,0:T(8,128)(2,1)S(1)}) all-reduce(f32[16,64]{1,0:T(8,128)S(1)} %bitcast.269, f32[16,64]{1,0:T(8,128)S(1)} %bitcast.270), channel_id=1, replica_groups=mesh['groups'=2,'replica'=2,'tensor'=8] {'tensor'}, use_global_device_ids=true, to_apply=%region_10.11 | all-reduce | flops 2048 | bytes 12288 | tf_op jit(solution)/shard_map/psum | solution.py:81
  175.3 48.5 %reduce-scatter.5.cloned.1.call-done = f32[16,1024]{1,0:T(8,128)} async-done(((f32[16,8192]{1,0:T(8,128)}), f32[16,1024]{1,0:T(8,128)}) %reduce-scatter.5.cloned.1.call-update) | async-done | bytes 65552 | tf_op jit(solution)/shard_map/reduce_scatter | solution.py:77
  (131 shorter events, 23.3 us)
Async XLA Ops:
  7.2 24.2 %copy-start = (bf16[4,64,1024]{2,1,0:T(8,128)(2,1)S(1)}, bf16[4,64,1024]{2,1,0:T(8,128)(2,1)}, u32[]{:S(2)}) copy-start(bf16[4,64,1024]{2,1,0:T(8,128)(2,1)} %param.15) | copy-start | bytes 1572868
  19.7 5.8 %copy-start.10 = (s32[32]{0:T(128)S(1)}, s32[32]{0:T(128)}, u32[]{:S(2)}) copy-start(s32[32]{0:T(128)} %param.20) | copy-start | bytes 388
  19.7 6.5 %copy-start.3 = (bf16[2,16,1024]{2,1,0:T(8,128)(2,1)S(1)}, bf16[2,16,1024]{2,1,0:T(8,128)(2,1)}, u32[]{:S(2)}) copy-start(bf16[2,16,1024]{2,1,0:T(8,128)(2,1)} %param.13) | copy-start | bytes 196612
  19.7 8.0 %copy-start.4 = (bf16[2,16,1024]{2,1,0:T(8,128)(2,1)S(1)}, bf16[2,16,1024]{2,1,0:T(8,128)(2,1)}, u32[]{:S(2)}) copy-start(bf16[2,16,1024]{2,1,0:T(8,128)(2,1)} %param.11) | copy-start | bytes 196612
  19.7 22.3 %all-to-all-start.2 = ((bf16[2,8,8,1,64,256]{5,4,2,1,3,0:T(8,128)(2,1)}), bf16[2,8,8,1,64,256]{5,4,2,1,3,0:T(8,128)(2,1)}, u32[]{:S(2)}, u32[]{:S(2)}) async-start(bf16[2,8,8,1,64,256]{5,4,2,1,3,0:T(8,128)(2,1)} %broadcast_select_fusion), calls=%async_computation.2 | async-start | bytes 8388608 | tf_op jit(solution)/shard_map/all_to_all | solution.py:147
  25.4 3.8 %copy-start.9 = (bf16[2,16,1,256]{3,1,2,0:T(8,128)(2,1)S(1)}, bf16[2,16,1,256]{3,1,2,0:T(8,128)(2,1)}, u32[]{:S(2)}) copy-start(bf16[2,16,1,256]{3,1,2,0:T(8,128)(2,1)} %param.12) | copy-start | bytes 49156
  25.4 5.1 %copy-start.11 = (s32[32]{0:T(128)S(1)}, s32[32]{0:T(128)}, u32[]{:S(2)}) copy-start(s32[32]{0:T(128)} %param.21) | copy-start | bytes 388
  31.4 2.1 copy-start.2
  42.0 8.9 %all-to-all-start = ((bf16[2,8,2,1024]{3,2,1,0:T(2,128)(2,1)}), bf16[2,8,2,1024]{3,2,1,0:T(2,128)(2,1)S(1)}, u32[]{:S(2)}, u32[]{:S(2)}) async-start(bf16[2,8,2,1024]{3,2,1,0:T(2,128)(2,1)} %get-tuple-element.36), calls=%async_computation | async-start | bytes 131072 | tf_op jit(solution)/shard_map/all_to_all | solution.py:147
  50.9 5.3 %all-to-all-start.1 = ((bf16[2,8,2,1024]{3,2,1,0:T(2,128)(2,1)}), bf16[2,8,2,1024]{3,2,1,0:T(2,128)(2,1)S(1)}, u32[]{:S(2)}, u32[]{:S(2)}) async-start(bf16[2,8,2,1024]{3,2,1,0:T(2,128)(2,1)} %get-tuple-element.37), calls=%async_computation.1 | async-start | bytes 131072 | tf_op jit(solution)/shard_map/all_to_all | solution.py:147
  56.3 9.2 %all-to-all-start.3 = ((bf16[2,8,2,1,256]{4,2,1,3,0:T(2,128)(2,1)}), bf16[2,8,2,1,256]{4,2,1,3,0:T(2,128)(2,1)S(1)}, u32[]{:S(2)}, u32[]{:S(2)}) async-start(bf16[2,8,2,1,256]{4,2,1,3,0:T(2,128)(2,1)} %fusion.35), calls=%async_computation.3 | async-start | bytes 32768 | tf_op jit(solution)/shard_map/all_to_all | solution.py:147
  65.5 5.3 %copy-start.1 = (s32[32]{0:T(128)S(1)}, s32[32]{0:T(128)}, u32[]{:S(2)}) copy-start(s32[32]{0:T(128)} %param.18) | copy-start | bytes 388
  65.5 50.1 %all-to-all-start.4 = ((bf16[2,8,64,1024]{3,2,1,0:T(8,128)(2,1)}), bf16[2,8,64,1024]{3,2,1,0:T(8,128)(2,1)S(1)}, u32[]{:S(2)}, u32[]{:S(2)}) async-start(bf16[2,8,64,1024]{3,2,1,0:T(8,128)(2,1)} %get-tuple-element.40), calls=%async_computation.5 | async-start | bytes 4194304 | tf_op jit(solution)/shard_map/all_to_all | solution.py:147
  69.4 105.9 %reduce-scatter.3.cloned.1.call-start = ((), (), s32[]{:S(2)}) async-start(), calls=%async_computation.8 | async-start | bytes 589824 | tf_op jit(solution)/shard_map/reduce_scatter | solution.py:77
  77.8 1.9 copy-start.5
  81.6 0.8 copy-start.8
  94.2 129.6 %reduce-scatter.5.cloned.1.call-start = ((), (), s32[]{:S(2)}) async-start(), calls=%async_computation.9 | async-start | bytes 589824 | tf_op jit(solution)/shard_map/reduce_scatter | solution.py:77
  97.8 0.9 copy-start.7
  115.6 1.3 copy-start.6
  116.9 9.2 %all-to-all-start.5 = ((bf16[2,8,64,1024]{3,2,1,0:T(8,128)(2,1)}), bf16[2,8,64,1024]{3,2,1,0:T(8,128)(2,1)}, u32[]{:S(2)}, u32[]{:S(2)}) async-start(bf16[2,8,64,1024]{3,2,1,0:T(8,128)(2,1)} %get-tuple-element.41), calls=%async_computation.6 | async-start | bytes 4194304 | tf_op jit(solution)/shard_map/all_to_all | solution.py:147
Sparse Core Ops, SparseCore 0:
  94.3 64.6 reduce-scatter.2
  162.7 60.9 reduce-scatter.4
where the time goes:
time: 233 us; the launch traced here: 232 us
  local copies, waits for them, and re-layouts  51.1 us (22%)
  waiting for transfers between devices  48.5 us (21%)
  blocking collectives  38.9 us (17%)
  matrix products  30.4 us (13%)
  starting transfers between devices  24.6 us (11%)
  other arithmetic  24.1 us (10%)
  between operations  14.5 us (6%)
    reduce_scatter x2, waiting for transfers between devices, serve_step(): lax.psum_scatter(partial_terms, 'tensor', scatter_dimension=1, tiled=True)  48.5 us
    psum x1, blocking collectives, serve_step(): shrink = lax.psum(shrink_terms, 'tensor').astype(jnp.bfloat16)  38.9 us
    all_to_all x6, starting transfers between devices, shards(): lax.all_to_all(as_sent(parcel), 'replica', split_axis=0, concat_axis=0, t...  24.4 us
    dot_general x2, matrix products, serve_step(): jnp.dot(attended, output_weight, preferred_element_type=jnp.float32)  17.8 us
    select_n x4, other arithmetic, departing_requests(): return jnp.where(flags, values, jnp.zeros_like(values))  10.6 us
    gather x6, local copies, waits for them, and re-layouts, shards(): item[source_rank, within]  9.16 us
    gather x6, local copies, waits for them, and re-layouts, finish_relocation(): return jnp.where(flags, incoming[arrival_slot], local_values)  8.76 us
    unnamed x1, other arithmetic  6.24 us
  transfers between devices with their start and end apart: 8, of which 1 were waited for; matrix products, arithmetic and copies ran while one was open for 38% of the time, Pallas kernels for 0%

commit v1 on v0

v1 whole, which is shorter than its diff:
```python
import jax
import jax.numpy as jnp
from jax import lax
from jax.experimental import pallas as pl
from jax.experimental.pallas import tpu as pltpu
from jax.sharding import PartitionSpec as P

adapter_scale = 2.0
bf16 = jnp.bfloat16
f32 = jnp.float32
LANES = 128
VMEM_BYTES = 56 * 1024 * 1024


def iota(shape, dim):
    return lax.broadcasted_iota(jnp.int32, shape, dim)


def div(value, size):
    return value >> (size.bit_length() - 1) if size & (size - 1) == 0 else value // size


def mod(value, size):
    return value & (size - 1) if size & (size - 1) == 0 else value % size


def dot(a, b, contract=((1,), (0,))):
    return lax.dot_general(a, b, (contract, ((), ())), preferred_element_type=f32)


def one_hot(mask):
    return jnp.where(mask, 1.0, 0.0).astype(bf16)


def rank_rows(order_ref, found_ref, holder, place, row_count, base):
    def step(j, count):
        request = order_ref[place * row_count + j]
        hit = div(request, row_count) == holder

        @pl.when(hit)
        def _():
            found_ref[base + count] = request - holder * row_count

        return count + hit.astype(jnp.int32)

    lax.fori_loop(0, row_count, step, jnp.int32(0))


def attend_kernel(
    order_ref,
    lengths_ref,
    table_ref,
    adapter_ref,
    queries_hbm,
    fresh_hbm,
    down_hbm,
    pool_ref,
    weight_ref,
    send_ref,
    queries_ref,
    fresh_ref,
    down_ref,
    pool_v,
    weight_v,
    scores_v,
    probs_v,
    attended_v,
    send_v,
    found,
    small_sem,
    pool_sem,
    weight_sem,
    send_sem,
):
    steps, rows, features = queries_ref.shape
    blocks, block_size, width = pool_v.shape
    head = width // 2
    heads = features // head
    sh = steps * heads
    table_blocks = table_ref.shape[0]
    positions = table_blocks * block_size
    places = lengths_ref.shape[0] // rows
    half = rows // places
    tensor = weight_v.shape[0]
    slots, rank = down_ref.shape[:2]
    me = lax.axis_index("replica")
    first = me * rows

    small_copies = [
        pltpu.make_async_copy(source, target, small_sem.at[n])
        for n, (source, target) in enumerate(
            ((queries_hbm, queries_ref), (fresh_hbm, fresh_ref), (down_hbm, down_ref))
        )
    ]
    pool_copy = pltpu.make_async_copy(pool_ref, pool_v, pool_sem)
    out_width = weight_v.shape[2]
    weight_copies = [
        pltpu.make_async_copy(
            weight_ref.at[:, pl.ds(t * out_width, out_width)], weight_v.at[t], weight_sem.at[t]
        )
        for t in range(tensor)
    ]
    small_copies[0].start()
    small_copies[1].start()
    pool_copy.start()
    small_copies[2].start()
    for copy in weight_copies[:2]:
        copy.start()

    for place in range(places):
        rank_rows(order_ref, found, me, place, rows, place * half)

    small_copies[0].wait()
    small_copies[1].wait()
    stacked = jnp.concatenate(
        [
            queries_ref[s, :, h * head : (h + 1) * head]
            for s in range(steps)
            for h in range(heads)
        ],
        axis=0,
    )
    total = rows * sh
    out_row, in_row = iota((total, total), 0), iota((total, total), 1)
    turn = one_hot((div(out_row, sh) == mod(in_row, rows)) & (mod(out_row, sh) == div(in_row, rows)))
    turned = dot(turn, stacked)
    query_rows = turned.astype(bf16)
    spread = one_hot(div(iota((total, rows), 0), sh) == iota((total, rows), 1))
    scale = head ** (-0.5)
    fresh_rows = [dot(spread, fresh_ref[s]) for s in range(steps)]
    step_of = div(mod(iota((total, 1), 0), sh), heads)
    fresh_scores = []
    for s in range(steps):
        value = jnp.sum(turned * fresh_rows[s][:, :head], axis=1, keepdims=True) * scale
        fresh_scores.append(jnp.where(step_of >= s, value, f32(-1e30)))

    pool_copy.wait()
    for copy in weight_copies[2:]:
        copy.start()

    def block_rows(row, lo):
        return jnp.concatenate(
            [pool_v[table_ref[b, first + row], :, lo : lo + head] for b in range(table_blocks)],
            axis=0,
        )

    column = iota((sh, positions), 1)
    for row in range(rows):
        part = dot(query_rows[row * sh : (row + 1) * sh], block_rows(row, 0), ((1,), (1,)))
        part = jnp.where(column < lengths_ref[first + row], part * scale, f32(-1e30))
        scores_v[row * sh : (row + 1) * sh, :] = part

    scores = scores_v[...]
    top = jnp.max(scores, axis=1, keepdims=True)
    for value in fresh_scores:
        top = jnp.maximum(top, value)
    weights = jnp.exp(scores - top)
    fresh_weights = [jnp.exp(value - top) for value in fresh_scores]
    totals = jnp.sum(weights, axis=1, keepdims=True)
    for value in fresh_weights:
        totals = totals + value
    probs_v[...] = weights / totals

    for row in range(rows):
        span = slice(row * sh, (row + 1) * sh)
        attended_v[span, :] = dot(probs_v[span, :].astype(bf16), block_rows(row, head))
    attended = attended_v[...]
    for value, row in zip(fresh_weights, fresh_rows):
        share = (value / totals).astype(bf16).astype(f32)
        attended = attended + share * row[:, head:]
    attended = attended.astype(bf16)

    row_index = iota((places * steps * half, 1), 0)
    source = jnp.zeros_like(row_index)
    adapter = jnp.zeros_like(row_index)
    for place in range(places):
        for slot in range(half):
            local = found[place * half + slot]
            here = (div(row_index, steps * half) == place) & (mod(row_index, half) == slot)
            source = jnp.where(here, local, source)
            adapter = jnp.where(here, adapter_ref[first + local], adapter)
    step_index = div(mod(row_index, steps * half), half)
    columns = iota((places * steps * half, total), 1)
    pieces = []
    for h in range(heads):
        wanted = source * sh + step_index * heads + h
        pieces.append(dot(one_hot(columns == wanted), attended))
    mixed = jnp.concatenate(pieces, axis=1).astype(bf16)

    small_copies[2].wait()
    wide = dot(mixed, down_ref[...].reshape(slots * rank, features), ((1,), (1,)))
    shrink = jnp.zeros((places * steps * half, rank), f32)
    for slot in range(slots):
        shrink = shrink + jnp.where(
            adapter == slot, wide[:, slot * rank : (slot + 1) * rank], 0.0
        )
    shrink = jnp.concatenate(
        [shrink, jnp.zeros((places * steps * half, LANES - rank), f32)], axis=1
    ).astype(bf16)

    group = steps * half
    send_copies = []
    for t in range(tensor):
        weight_copies[t].wait()
        projected = dot(mixed, weight_v[t]).astype(bf16)
        for place in range(places):
            span = slice(place * group, (place + 1) * group)
            send_v[t, place, :, :out_width] = projected[span]
            send_v[t, place, :, out_width:] = shrink[span]
            copy = pltpu.make_async_copy(
                send_v.at[t, place], send_ref.at[place, t], send_sem.at[t, place]
            )
            copy.start()
            send_copies.append(copy)
    for copy in send_copies:
        copy.wait()


def attend_call(order, lengths, table, adapters, queries, fresh, down, pool, weight):
    steps, rows, features = queries.shape
    replicas = lax.axis_size("replica")
    tensor = lax.axis_size("tensor")
    blocks, block_size, width = pool.shape
    positions = table.shape[0] * block_size
    score_rows = rows * steps * features // (width // 2)
    out_width = weight.shape[1] // tensor
    smem = pl.BlockSpec(memory_space=pltpu.SMEM)
    hbm = pl.BlockSpec(memory_space=pl.ANY)
    return pl.pallas_call(
        attend_kernel,
        out_shape=jax.ShapeDtypeStruct(
            (replicas, tensor, steps * rows // replicas, out_width + LANES), bf16
        ),
        in_specs=[smem] * 4 + [hbm] * 5,
        out_specs=hbm,
        scratch_shapes=[
            pltpu.VMEM(queries.shape, bf16),
            pltpu.VMEM(fresh.shape, bf16),
            pltpu.VMEM(down.shape, bf16),
            pltpu.VMEM((blocks, block_size, width), bf16),
            pltpu.VMEM((tensor, weight.shape[0], out_width), bf16),
            pltpu.VMEM((score_rows, positions), f32),
            pltpu.VMEM((score_rows, positions), f32),
            pltpu.VMEM((score_rows, width // 2), f32),
            pltpu.VMEM((tensor, replicas, steps * rows // replicas, out_width + LANES), bf16),
            pltpu.SMEM((rows,), jnp.int32),
            pltpu.SemaphoreType.DMA((3,)),
            pltpu.SemaphoreType.DMA,
            pltpu.SemaphoreType.DMA((tensor,)),
            pltpu.SemaphoreType.DMA((tensor, replicas)),
        ],
        compiler_params=pltpu.CompilerParams(vmem_limit_bytes=VMEM_BYTES),
        name="attend",
    )(order, lengths, table, adapters, queries, fresh, down, pool, weight)


def place_kernel(
    order_ref,
    lengths_ref,
    table_ref,
    adapter_ref,
    own_ref,
    other_ref,
    residual_ref,
    other_residual_ref,
    out_ref,
    base_ref,
    mix_ref,
    slot_ref,
    blocks_v,
    block_sem,
    out_sem,
):
    rows, table_blocks, block_size, width = blocks_v.shape
    steps, _, features = residual_ref.shape
    group = mix_ref.shape[0] // 2
    half = group // steps
    tensor = mix_ref.shape[1] // (2 * group)
    me = lax.axis_index("replica")

    def fetch(j, carry):
        request = order_ref[me * rows + j]
        mine = div(request, rows) == me

        @pl.when(mine)
        def _():
            for b in range(table_blocks):
                source = own_ref.at[table_ref[b, request]]
                pltpu.make_async_copy(source, blocks_v.at[j, b], block_sem.at[j]).start()

        @pl.when(jnp.logical_not(mine))
        def _():
            for b in range(table_blocks):
                source = other_ref.at[table_ref[b, request]]
                pltpu.make_async_copy(source, blocks_v.at[j, b], block_sem.at[j]).start()

        return carry

    lax.fori_loop(0, rows, fetch, 0)

    out_row = iota((steps * rows, 1), 0)
    step_of, place_of = div(out_row, rows), mod(out_row, rows)
    landed_row = jnp.zeros_like(out_row)
    residual_row = jnp.zeros_like(out_row)
    slot = jnp.zeros_like(out_row)
    slots = slot_ref.shape[1] // 2
    counts = [jnp.int32(0), jnp.int32(0)]
    for j in range(rows):
        request = order_ref[me * rows + j]
        holder = div(request, rows)
        count = jnp.where(holder == 0, counts[0], counts[1])
        counts[0] = counts[0] + jnp.where(holder == 0, 1, 0)
        counts[1] = counts[1] + jnp.where(holder == 0, 0, 1)
        away = jnp.where(holder == me, 0, 1)
        here = place_of == j
        landed_row = jnp.where(here, holder * (tensor * group) + count, landed_row)
        residual_row = jnp.where(here, away * (steps * rows) + mod(request, rows), residual_row)
        slot = jnp.where(here, away * slots + adapter_ref[request], slot)
    landed_row = landed_row + step_of * half
    residual_row = residual_row + step_of * rows
    column = iota(mix_ref.shape, 1)
    kept = column - mod(column, tensor * group) + mod(column, group)
    mix_ref[...] = one_hot(kept == landed_row)
    slot_ref[...] = one_hot(iota(slot_ref.shape, 1) == slot).astype(f32)
    column = iota((steps * rows, steps * rows), 1)
    base_ref[...] = dot(
        one_hot(column == residual_row), residual_ref[...].reshape(steps * rows, features)
    ) + dot(
        one_hot(column + steps * rows == residual_row),
        other_residual_ref[...].reshape(steps * rows, features),
    )

    position = iota((table_blocks, block_size, width), 0) * block_size + iota(
        (table_blocks, block_size, width), 1
    )

    def store(j, carry):
        length = lengths_ref[order_ref[me * rows + j]]
        pltpu.make_async_copy(own_ref.at[pl.ds(0, table_blocks)], blocks_v.at[j], block_sem.at[j]).wait()
        values = blocks_v[j]
        blocks_v[j] = jnp.where(position < length, values, jnp.zeros_like(values))
        pltpu.make_async_copy(blocks_v.at[j], out_ref.at[j], out_sem).start()
        return carry

    lax.fori_loop(0, rows, store, 0)
    pltpu.make_async_copy(blocks_v, out_ref, out_sem).wait()


def place_call(order, lengths, table, adapters, own, other, residual, other_residual, tensor, slots):
    steps, rows, features = residual.shape
    _, block_size, width = own.shape
    smem = pl.BlockSpec(memory_space=pltpu.SMEM)
    vmem = pl.BlockSpec(memory_space=pltpu.VMEM)
    hbm = pl.BlockSpec(memory_space=pl.ANY)
    cache = (rows, table.shape[0], block_size, width)
    return pl.pallas_call(
        place_kernel,
        out_shape=(
            jax.ShapeDtypeStruct(cache, bf16),
            jax.ShapeDtypeStruct((steps * rows, features), f32),
            jax.ShapeDtypeStruct((steps * rows, tensor * steps * rows), bf16),
            jax.ShapeDtypeStruct((steps * rows, 2 * slots), f32),
        ),
        in_specs=[smem] * 4 + [hbm] * 2 + [vmem] * 2,
        out_specs=(hbm, vmem, vmem, vmem),
        scratch_shapes=[
            pltpu.VMEM(cache, bf16),
            pltpu.SemaphoreType.DMA((rows,)),
            pltpu.SemaphoreType.DMA,
        ],
        compiler_params=pltpu.CompilerParams(vmem_limit_bytes=VMEM_BYTES),
        name="place",
    )(order, lengths, table, adapters, own, other, residual, other_residual)


def finish_kernel(landed_ref, base_ref, mix_ref, slot_ref, up_ref, other_up_ref, out_ref):
    features = base_ref.shape[1]
    slots, rank = up_ref.shape[:2]
    sums = dot(mix_ref[...], landed_ref[...])
    shrink = sums[:, features : features + rank].astype(bf16).astype(f32)
    result = base_ref[...] + sums[:, :features]
    for side, up in enumerate((up_ref, other_up_ref)):
        wide = jnp.concatenate(
            [shrink * slot_ref[:, side * slots + n : side * slots + n + 1] for n in range(slots)],
            axis=1,
        ).astype(bf16)
        result = result + adapter_scale * dot(wide, up[...].reshape(slots * rank, features))
    out_ref[...] = result.astype(bf16).reshape(out_ref.shape)


def shards(
    queries,
    latest_key_value,
    residual,
    paged_cache_pool,
    adapter_down_weight,
    adapter_up_weight,
    output_weight,
    lengths,
    previous_block_table,
    request_order_after,
    request_adapter_index,
):
    steps, rows, features = queries.shape
    replicas = lax.axis_size("replica")
    tensor = lax.axis_size("tensor")
    blocks, _, block_size, width = paged_cache_pool.shape
    table_blocks = previous_block_table.shape[1]
    pool = paged_cache_pool.reshape(blocks, block_size, width)
    fresh = latest_key_value.reshape(steps, rows, width)
    swap = [(0, 1), (1, 0)]
    other_pool = lax.ppermute(pool, "replica", swap)
    other_residual = lax.ppermute(residual, "replica", swap)
    other_up = lax.ppermute(adapter_up_weight, "replica", swap)

    table = previous_block_table.T
    send = attend_call(
        request_order_after,
        lengths,
        table,
        request_adapter_index,
        queries,
        fresh,
        adapter_down_weight,
        pool,
        output_weight,
    )
    landed = lax.all_to_all(
        send.reshape((replicas * tensor,) + send.shape[2:]),
        ("replica", "tensor"),
        split_axis=0,
        concat_axis=0,
        tiled=True,
    ).reshape(send.shape)
    placed_cache, base, mix, slot = place_call(
        request_order_after,
        lengths,
        table,
        request_adapter_index,
        pool,
        other_pool,
        residual,
        other_residual,
        tensor,
        adapter_up_weight.shape[0],
    )
    vmem = pl.BlockSpec(memory_space=pltpu.VMEM)
    layer_out = pl.pallas_call(
        finish_kernel,
        out_shape=jax.ShapeDtypeStruct((steps, rows, features), bf16),
        in_specs=[vmem] * 6,
        out_specs=vmem,
        compiler_params=pltpu.CompilerParams(vmem_limit_bytes=VMEM_BYTES // 2),
        name="finish",
    )(landed.reshape(-1, landed.shape[-1]), base, mix, slot, adapter_up_weight, other_up)
    return (layer_out, placed_cache.reshape(rows, table_blocks, 1, block_size, width))


def solution(mesh):
    in_specs = (
        P(None, ("groups", "replica"), "tensor"),
        P(None, ("groups", "replica"), "tensor", None),
        P(None, ("groups", "replica"), "tensor"),
        P(("groups", "replica"), "tensor", None, None),
        P(("groups", "replica"), None, "tensor"),
        P(("groups", "replica"), None, "tensor"),
        P("tensor", None),
        P("groups"),
        P("groups", None),
        P("groups"),
        P("groups"),
    )
    out_specs = (
        P(None, ("groups", "replica"), "tensor"),
        P(("groups", "replica"), None, "tensor", None, None),
    )
    return jax.shard_map(shards, mesh=mesh, in_specs=in_specs, out_specs=out_specs, check_vma=False)
```

time: 233 us -> 40.4 us (0.17)
  local copies, waits for them, and re-layouts: 51.1 us -> 2.97 us
  blocking collectives: 38.9 us -> 0 us
  waiting for transfers between devices: 48.5 us -> 10.9 us
  matrix products: 30.4 us -> 0 us
  other arithmetic: 24.1 us -> 0 us
  Pallas kernels: 0 us -> 17.1 us
  starting transfers between devices: 24.6 us -> 8.15 us
  between operations: 14.5 us -> 0.68 us
    reduce_scatter x2 -> x0, waiting for transfers between devices: 48.5 us -> none  [serve_step(): lax.psum_scatter(partial_terms, 'tensor', scatter_dimension=1, tiled=True)]
    gather x34 -> x0, local copies, waits for them, and re-layouts: 43.7 us -> none  [the longest x6 9.16 us: shards(): item[source_rank, within]]
    psum x1 -> x0, blocking collectives: 38.9 us -> none  [serve_step(): shrink = lax.psum(shrink_terms, 'tensor').astype(jnp.bfloat16)]
    dot_general x13 -> x0, matrix products: 30.4 us -> none  [the longest x2 17.8 us: serve_step(): jnp.dot(attended, output_weight, preferred_element_type=jnp.float32)]
    all_to_all x6 -> x1, starting transfers between devices: 24.4 us -> 7.06 us  [shards(): lax.all_to_all(send.reshape((replicas * tensor,) + send.shape[2:]), ('rep...]
    pallas_call x0 -> x3, Pallas kernels: none -> 17.1 us  [the longest x1 10.9 us: attend_call(): pl.pallas_call(attend_kernel, out_shape=jax.ShapeDtypeStruct((replicas, t...]
    select_n x14 -> x0, other arithmetic: 15.1 us -> none  [the longest x4 10.6 us: departing_requests(): return jnp.where(flags, values, jnp.zeros_like(values))]
    all_to_all x6 -> x1, waiting for transfers between devices: 0.02 us -> 9.34 us  [shards(): lax.all_to_all(send.reshape((replicas * tensor,) + send.shape[2:]), ('rep...]
  transfers between devices with their start and end apart: 8 -> 4, of which waited for: 1 -> 2; matrix products, arithmetic and copies ran while one was open for 38% -> 0% of each run, Pallas kernels for 0% -> 40%
where the time goes in v1:
time: 40.4 us; the launch traced here: 39.8 us
  Pallas kernels  17.1 us (42%)
  waiting for transfers between devices  10.9 us (27%)
  starting transfers between devices  8.15 us (20%)
  local copies, waits for them, and re-layouts  2.97 us (7%)
  between operations  0.68 us (2%)
    pallas_call x1, Pallas kernels, attend_call(): pl.pallas_call(attend_kernel, out_shape=jax.ShapeDtypeStruct((replicas, t...  10.9 us
    all_to_all x1, waiting for transfers between devices, shards(): lax.all_to_all(send.reshape((replicas * tensor,) + send.shape[2:]), ('rep...  9.34 us
    all_to_all x1, starting transfers between devices, shards(): lax.all_to_all(send.reshape((replicas * tensor,) + send.shape[2:]), ('rep...  7.06 us
    pallas_call x1, Pallas kernels, place_call(): pl.pallas_call(place_kernel, out_shape=(jax.ShapeDtypeStruct(cache, bf16)...  5.07 us
    unnamed x12, local copies, waits for them, and re-layouts  2.97 us
    ppermute x1, waiting for transfers between devices, shards(): other_residual = lax.ppermute(residual, 'replica', swap)  1.53 us
    pallas_call x1, Pallas kernels, shards(): pl.pallas_call(finish_kernel, out_shape=jax.ShapeDtypeStruct((steps, rows...  1.16 us
  transfers between devices with their start and end apart: 4, of which 2 were waited for; matrix products, arithmetic and copies ran while one was open for 0% of the time, Pallas kernels for 40%

profile of v1, /device:TPU:0, one launch (start us, length us, event | category | flops | bytes accessed | tf_op | source)
XLA Modules:
  0.0 39.8 jit_solution(10589966496861185567)
XLA Ops:
  0.6 0.5 %collective-permute-start = (bf16[128,64,256]{2,1,0:T(8,128)(2,1)}, bf16[128,64,256]{2,1,0:T(8,128)(2,1)}, u32[]{:S(2)}, u32[]{:S(2)}) collective-permute-start(bf16[128,64,256]{2,1,0:T(8,128)(2,1)} %bitcast.9), channel_id=1, source_target_pairs={{0,8},{8,0},{1,9},{9,1},{2,10},{10,2},{3,11},{11,3},{4,12},{12,4},... | collective-permute-start | bytes 12582920 | tf_op jit(solution)/shard_map/ppermute | solution.py:412
  1.1 0.0 copy-start
  1.2 0.0 copy-start.4
  1.2 10.9 %attend.1 = bf16[2,8,16,1152]{3,2,1,0:T(8,128)(2,1)} custom-call(s32[32]{0:T(128)} %order_ref.3, s32[32]{0:T(128)} %lengths_ref.3, s32[8,32]{1,0:T(8,128)} %bitcast.14, s32[32]{0:T(128)} %adapter_ref.3, bf16[2,16,1024]{2,1,0:T(8,128)(2,1)} %queries_hbm.1, bf16[2,16,256]{2,1,0:T(8,128)(2,1)} %bitcast.13, bf16[4,64,1024]{2,1,0:T(8,128)(2,1)} %down_hbm.1, ...), custom_call_target="tpu_custom_call" | custom-call | tf_op jit(solution)/shard_map/attend/pallas_call | solution.py:229
  12.0 7.1 %all-to-all-start = ((bf16[16,16,1152]{2,1,0:T(8,128)(2,1)}), bf16[16,16,1152]{2,1,0:T(8,128)(2,1)S(1)}, u32[]{:S(2)}, u32[]{:S(2)}) async-start(bf16[16,16,1152]{2,1,0:T(8,128)(2,1)} %bitcast.12), calls=%async_computation | async-start | bytes 1179648 | tf_op jit(solution)/shard_map/all_to_all | solution.py:428
  19.1 0.0 copy-done
  19.1 0.5 %collective-permute-start.2 = (bf16[4,64,1024]{2,1,0:T(8,128)(2,1)S(1)}, bf16[4,64,1024]{2,1,0:T(8,128)(2,1)S(1)}, u32[]{:S(2)}, u32[]{:S(2)}) collective-permute-start(bf16[4,64,1024]{2,1,0:T(8,128)(2,1)S(1)} %copy-done), channel_id=1, source_target_pairs={{0,8},{8,0},{1,9},{9,1},{2,10},{10,2},{3,11},{11,3},{4,12},{12,4},... | collective-permute-start | bytes 1572872 | tf_op jit(solution)/shard_map/ppermute | solution.py:414
  19.6 0.0 copy-done.4
  19.6 0.1 collective-permute-start.1
  19.7 1.5 %collective-permute-done.1.other_residual_ref = bf16[2,16,1024]{2,1,0:T(8,128)(2,1)S(1)} collective-permute-done((bf16[2,16,1024]{2,1,0:T(8,128)(2,1)S(1)}, bf16[2,16,1024]{2,1,0:T(8,128)(2,1)S(1)}, u32[]{:S(2)}, u32[]{:S(2)}) %collective-permute-start.1) | collective-permute-done | bytes 65568 | tf_op jit(solution)/shard_map/ppermute | solution.py:413
  21.2 0.0 copy-start.5
  21.2 0.0 collective-permute-done.other_ref
  21.2 0.6 %copy-done.5 = bf16[2,16,1024]{2,1,0:T(8,128)(2,1)} copy-done((bf16[2,16,1024]{2,1,0:T(8,128)(2,1)}, bf16[2,16,1024]{2,1,0:T(8,128)(2,1)S(1)}, u32[]{:S(2)}) %copy-start.5) | copy-done | bytes 65560
  21.9 5.1 %place.1 = (bf16[16,8,64,256]{3,2,1,0:T(8,128)(2,1)}, f32[32,1024]{1,0:T(8,128)}, bf16[32,256]{1,0:T(8,128)(2,1)}, f32[32,8]{1,0:T(8,128)}) custom-call(s32[32]{0:T(128)} %order_ref.3, s32[32]{0:T(128)} %lengths_ref.3, s32[8,32]{1,0:T(8,128)} %bitcast.15, s32[32]{0:T(128)} %adapter_ref.3, bf16[128,64,256]{2,1,0:T(8,128)(2,1)} %bitcast.11, ...), custom_call_target="tpu_custom_call" | custom-call | tf_op jit(solution)/shard_map/place/pallas_call | solution.py:356
  26.9 0.0 collective-permute-done.2.other_up_ref
  26.9 9.3 %all-to-all-done = bf16[16,16,1152]{2,1,0:T(8,128)(2,1)S(1)} async-done(((bf16[16,16,1152]{2,1,0:T(8,128)(2,1)}), bf16[16,16,1152]{2,1,0:T(8,128)(2,1)S(1)}, u32[]{:S(2)}, u32[]{:S(2)}) %all-to-all-start) | async-done | bytes 589856 | tf_op jit(solution)/shard_map/all_to_all | solution.py:428
  36.3 0.0 copy-start.1
  36.3 0.9 %copy-done.1 = f32[32,1024]{1,0:T(8,128)S(1)} copy-done((f32[32,1024]{1,0:T(8,128)S(1)}, f32[32,1024]{1,0:T(8,128)}, u32[]{:S(2)}) %copy-start.1) | copy-done | bytes 131096
  37.2 0.0 copy-start.2
  37.2 0.7 %copy-done.2 = bf16[32,256]{1,0:T(8,128)(2,1)S(1)} copy-done((bf16[32,256]{1,0:T(8,128)(2,1)S(1)}, bf16[32,256]{1,0:T(8,128)(2,1)}, u32[]{:S(2)}) %copy-start.2) | copy-done | bytes 16408
  37.9 0.0 copy-start.3
  37.9 0.7 %copy-done.3 = f32[32,8]{1,0:T(8,128)S(1)} copy-done((f32[32,8]{1,0:T(8,128)S(1)}, f32[32,8]{1,0:T(8,128)}, u32[]{:S(2)}) %copy-start.3) | copy-done | bytes 1048
  38.6 1.2 %finish.1 = bf16[2,16,1024]{2,1,0:T(8,128)(2,1)} custom-call(bf16[256,1152]{1,0:T(8,128)(2,1)S(1)} %bitcast.8, f32[32,1024]{1,0:T(8,128)S(1)} %copy-done.1, bf16[32,256]{1,0:T(8,128)(2,1)S(1)} %copy-done.2, f32[32,8]{1,0:T(8,128)S(1)} %copy-done.3, bf16[4,64,1024]{2,1,0:T(8,128)(2,1)S(1)} %copy-done, bf16[4,64,1024]{2,1,0:T(8,128)(2,1)S(1)} %collective-permute-done.2.other_up_ref), custom_call_target="tpu_custom_call" | custom-call | tf_op jit(solution)/shard_map/finish/pallas_call | solution.py:448
Async XLA Ops:
  0.6 20.6 %collective-permute-start = (bf16[128,64,256]{2,1,0:T(8,128)(2,1)}, bf16[128,64,256]{2,1,0:T(8,128)(2,1)}, u32[]{:S(2)}, u32[]{:S(2)}) collective-permute-start(bf16[128,64,256]{2,1,0:T(8,128)(2,1)} %bitcast.9), channel_id=1, source_target_pairs={{0,8},{8,0},{1,9},{9,1},{2,10},{10,2},{3,11},{11,3},{4,12},{12,4},... | collective-permute-start | bytes 12582920 | tf_op jit(solution)/shard_map/ppermute | solution.py:412
  1.1 18.0 %copy-start = (bf16[4,64,1024]{2,1,0:T(8,128)(2,1)S(1)}, bf16[4,64,1024]{2,1,0:T(8,128)(2,1)}, u32[]{:S(2)}) copy-start(bf16[4,64,1024]{2,1,0:T(8,128)(2,1)} %up_ref.1) | copy-start | bytes 1572868
  1.2 18.5 %copy-start.4 = (bf16[2,16,1024]{2,1,0:T(8,128)(2,1)S(1)}, bf16[2,16,1024]{2,1,0:T(8,128)(2,1)}, u32[]{:S(2)}) copy-start(bf16[2,16,1024]{2,1,0:T(8,128)(2,1)} %residual_ref.1) | copy-start | bytes 196612
  12.0 24.2 %all-to-all-start = ((bf16[16,16,1152]{2,1,0:T(8,128)(2,1)}), bf16[16,16,1152]{2,1,0:T(8,128)(2,1)S(1)}, u32[]{:S(2)}, u32[]{:S(2)}) async-start(bf16[16,16,1152]{2,1,0:T(8,128)(2,1)} %bitcast.12), calls=%async_computation | async-start | bytes 1179648 | tf_op jit(solution)/shard_map/all_to_all | solution.py:428
  19.1 7.8 %collective-permute-start.2 = (bf16[4,64,1024]{2,1,0:T(8,128)(2,1)S(1)}, bf16[4,64,1024]{2,1,0:T(8,128)(2,1)S(1)}, u32[]{:S(2)}, u32[]{:S(2)}) collective-permute-start(bf16[4,64,1024]{2,1,0:T(8,128)(2,1)S(1)} %copy-done), channel_id=1, source_target_pairs={{0,8},{8,0},{1,9},{9,1},{2,10},{10,2},{3,11},{11,3},{4,12},{12,4},... | collective-permute-start | bytes 1572872 | tf_op jit(solution)/shard_map/ppermute | solution.py:414
  19.6 1.6 %collective-permute-start.1 = (bf16[2,16,1024]{2,1,0:T(8,128)(2,1)S(1)}, bf16[2,16,1024]{2,1,0:T(8,128)(2,1)S(1)}, u32[]{:S(2)}, u32[]{:S(2)}) collective-permute-start(bf16[2,16,1024]{2,1,0:T(8,128)(2,1)S(1)} %copy-done.4), channel_id=1, source_target_pairs={{0,8},{8,0},{1,9},{9,1},{2,10},{10,2},{3,11},{11,3},{4,12},{12,4},... | collective-permute-start | bytes 196616 | tf_op jit(solution)/shard_map/ppermute | solution.py:413
  21.2 0.6 %copy-start.5 = (bf16[2,16,1024]{2,1,0:T(8,128)(2,1)}, bf16[2,16,1024]{2,1,0:T(8,128)(2,1)S(1)}, u32[]{:S(2)}) copy-start(bf16[2,16,1024]{2,1,0:T(8,128)(2,1)S(1)} %collective-permute-done.1.other_residual_ref) | copy-start | bytes 196612
  36.3 0.9 %copy-start.1 = (f32[32,1024]{1,0:T(8,128)S(1)}, f32[32,1024]{1,0:T(8,128)}, u32[]{:S(2)}) copy-start(f32[32,1024]{1,0:T(8,128)} %get-tuple-element.6.base_ref) | copy-start | bytes 393220
  37.2 0.7 %copy-start.2 = (bf16[32,256]{1,0:T(8,128)(2,1)S(1)}, bf16[32,256]{1,0:T(8,128)(2,1)}, u32[]{:S(2)}) copy-start(bf16[32,256]{1,0:T(8,128)(2,1)} %get-tuple-element.7.mix_ref) | copy-start | bytes 49156
  37.9 0.7 %copy-start.3 = (f32[32,8]{1,0:T(8,128)S(1)}, f32[32,8]{1,0:T(8,128)}, u32[]{:S(2)}) copy-start(f32[32,8]{1,0:T(8,128)} %get-tuple-element.8.slot_ref) | copy-start | bytes 3076

commit v2 on v1

v2 whole, which is shorter than its diff:
```python
import functools

import jax
import jax.numpy as jnp
from jax import lax
from jax.experimental import pallas as pl
from jax.experimental.pallas import tpu as pltpu
from jax.sharding import PartitionSpec as P

adapter_scale = 2.0
bf16 = jnp.bfloat16
f32 = jnp.float32
LANES = 128
QUAD = 4
VMEM_BYTES = 56 * 1024 * 1024
SMALL_BYTES = 8 * 1024 * 1024
MIDDLE_BYTES = 52 * 1024 * 1024


def iota(shape, dim):
    return lax.broadcasted_iota(jnp.int32, shape, dim)


def div(value, size):
    return value >> (size.bit_length() - 1) if size & (size - 1) == 0 else value // size


def mod(value, size):
    return value & (size - 1) if size & (size - 1) == 0 else value % size


def dot(a, b, contract=((1,), (0,))):
    return lax.dot_general(a, b, (contract, ((), ())), preferred_element_type=f32)


def one_hot(mask):
    return jnp.where(mask, 1.0, 0.0).astype(bf16)


def rank_rows(order_ref, found_ref, target_ref, holder, place, row_count, base):
    def step(j, count):
        request = order_ref[place * row_count + j]
        hit = div(request, row_count) == holder

        @pl.when(hit)
        def _():
            found_ref[base + count] = request - holder * row_count
            target_ref[base + count] = j

        return count + hit.astype(jnp.int32)

    lax.fori_loop(0, row_count, step, jnp.int32(0))


def weight_columns(weight_ref, weight_v, sems, partners):
    out_width = weight_v.shape[2]
    spans = weight_v.shape[0] // len(partners)
    here = lax.axis_index("tensor")
    copies = []
    for n, partner in enumerate(partners):
        for span in range(spans):
            start = pl.multiple_of((here ^ (span * QUAD + partner)) * out_width, out_width)
            slot = n * spans + span
            copies.append(
                pltpu.make_async_copy(
                    weight_ref.at[:, pl.ds(start, out_width)], weight_v.at[slot], sems.at[slot]
                )
            )
    return copies


def project(mixed, shrink, weight_copies, weight_v, message_refs):
    out_width = weight_v.shape[2]
    spans = weight_v.shape[0] // len(message_refs)
    for n, message_ref in enumerate(message_refs):
        message_ref[:, spans * out_width :] = shrink
        for span in range(spans):
            slot = n * spans + span
            weight_copies[slot].wait()
            part = dot(mixed, weight_v[slot]).astype(bf16)
            message_ref[:, span * out_width : (span + 1) * out_width] = part


def attend_kernel(
    order_ref,
    lengths_ref,
    table_ref,
    adapter_ref,
    queries_hbm,
    fresh_hbm,
    down_hbm,
    pool_ref,
    weight_ref,
    *rest,
    partners,
):
    message_refs, rest = rest[: len(partners)], rest[len(partners) :]
    (
        mixed_ref,
        shrink_ref,
        placed_ref,
        leaving_ref,
        queries_ref,
        fresh_ref,
        down_ref,
        pool_v,
        weight_v,
        scores_v,
        probs_v,
        attended_v,
        zero_v,
        found,
        target,
        small_sem,
        pool_sem,
        weight_sem,
        cache_sem,
    ) = rest
    steps, rows, features = queries_ref.shape
    blocks, block_size, width = pool_v.shape
    head = width // 2
    heads = features // head
    sh = steps * heads
    table_blocks = table_ref.shape[0]
    positions = table_blocks * block_size
    places = lengths_ref.shape[0] // rows
    half = rows // places
    slots, rank = down_ref.shape[:2]
    me = lax.axis_index("replica")
    first = me * rows

    small_copies = [
        pltpu.make_async_copy(source, target, small_sem.at[n])
        for n, (source, target) in enumerate(
            ((queries_hbm, queries_ref), (fresh_hbm, fresh_ref), (down_hbm, down_ref))
        )
    ]
    pool_copy = pltpu.make_async_copy(pool_ref, pool_v, pool_sem)
    weight_copies = weight_columns(weight_ref, weight_v, weight_sem, partners)
    small_copies[0].start()
    small_copies[1].start()
    pool_copy.start()
    small_copies[2].start()
    for copy in weight_copies[:2]:
        copy.start()

    for place in range(places):
        rank_rows(order_ref, found, target, me, me if place == 0 else 1 - me, rows, place * half)

    small_copies[0].wait()
    small_copies[1].wait()
    stacked = jnp.concatenate(
        [
            queries_ref[s, :, h * head : (h + 1) * head]
            for s in range(steps)
            for h in range(heads)
        ],
        axis=0,
    )
    total = rows * sh
    out_row, in_row = iota((total, total), 0), iota((total, total), 1)
    turn = one_hot((div(out_row, sh) == mod(in_row, rows)) & (mod(out_row, sh) == div(in_row, rows)))
    turned = dot(turn, stacked)
    query_rows = turned.astype(bf16)
    spread = one_hot(div(iota((total, rows), 0), sh) == iota((total, rows), 1))
    scale = head ** (-0.5)
    fresh_rows = [dot(spread, fresh_ref[s]) for s in range(steps)]
    step_of = div(mod(iota((total, 1), 0), sh), heads)
    fresh_scores = []
    for s in range(steps):
        value = jnp.sum(turned * fresh_rows[s][:, :head], axis=1, keepdims=True) * scale
        fresh_scores.append(jnp.where(step_of >= s, value, f32(-1e30)))

    pool_copy.wait()
    for copy in weight_copies[2:]:
        copy.start()

    def block_rows(row, lo):
        return jnp.concatenate(
            [pool_v[table_ref[b, first + row], :, lo : lo + head] for b in range(table_blocks)],
            axis=0,
        )

    zero_v[...] = jnp.zeros_like(zero_v)
    position = iota(zero_v.shape, 0)
    for row in range(rows):
        length = lengths_ref[first + row]
        full = div(length, block_size)

        @pl.when(full < table_blocks)
        def _(row=row, length=length, full=full):
            block = table_ref[full, first + row]
            kept = jnp.where(
                position < length - full * block_size, pool_v[block].astype(f32), 0.0
            )
            pool_v[block] = kept.astype(bf16)

    column = iota((sh, positions), 1)
    for row in range(rows):
        part = dot(query_rows[row * sh : (row + 1) * sh], block_rows(row, 0), ((1,), (1,)))
        part = jnp.where(column < lengths_ref[first + row], part * scale, f32(-1e30))
        scores_v[row * sh : (row + 1) * sh, :] = part

    scores = scores_v[...]
    top = jnp.max(scores, axis=1, keepdims=True)
    for value in fresh_scores:
        top = jnp.maximum(top, value)
    weights = jnp.exp(scores - top)
    fresh_weights = [jnp.exp(value - top) for value in fresh_scores]
    totals = jnp.sum(weights, axis=1, keepdims=True)
    for value in fresh_weights:
        totals = totals + value
    probs_v[...] = weights / totals

    for row in range(rows):
        span = slice(row * sh, (row + 1) * sh)
        attended_v[span, :] = dot(probs_v[span, :].astype(bf16), block_rows(row, head))
    attended = attended_v[...]
    for value, row in zip(fresh_weights, fresh_rows):
        share = (value / totals).astype(bf16).astype(f32)
        attended = attended + share * row[:, head:]
    attended = attended.astype(bf16)

    row_index = iota((places * steps * half, 1), 0)
    source = jnp.zeros_like(row_index)
    adapter = jnp.zeros_like(row_index)
    for place in range(places):
        for slot in range(half):
            local = found[place * half + slot]
            here = (div(row_index, steps * half) == place) & (mod(row_index, half) == slot)
            source = jnp.where(here, local, source)
            adapter = jnp.where(here, adapter_ref[first + local], adapter)
    step_index = div(mod(row_index, steps * half), half)
    columns = iota((places * steps * half, total), 1)
    pieces = []
    for h in range(heads):
        wanted = source * sh + step_index * heads + h
        pieces.append(dot(one_hot(columns == wanted), attended))
    mixed = jnp.concatenate(pieces, axis=1).astype(bf16)

    small_copies[2].wait()
    wide = dot(mixed, down_ref[...].reshape(slots * rank, features), ((1,), (1,)))
    shrink = jnp.zeros((places * steps * half, rank), f32)
    for slot in range(slots):
        shrink = shrink + jnp.where(
            adapter == slot, wide[:, slot * rank : (slot + 1) * rank], 0.0
        )
    shrink = jnp.concatenate(
        [shrink, jnp.zeros((places * steps * half, LANES - rank), f32)], axis=1
    ).astype(bf16)

    mixed_ref[...] = mixed
    shrink_ref[...] = shrink

    def write_cache(index, carry):
        local = found[index]
        length = lengths_ref[first + local]

        def write(row_ref, sem):
            for b in range(table_blocks):

                @pl.when(b * block_size < length)
                def _():
                    source = pool_v.at[table_ref[b, first + local]]
                    pltpu.make_async_copy(source, row_ref.at[b], sem).start()

                @pl.when(b * block_size >= length)
                def _():
                    pltpu.make_async_copy(zero_v, row_ref.at[b], sem).start()

        @pl.when(index < half)
        def _():
            write(placed_ref.at[target[index]], cache_sem.at[0])

        @pl.when(index >= half)
        def _():
            write(leaving_ref.at[index - half], cache_sem.at[1])

        return carry

    lax.fori_loop(0, rows, write_cache, 0)
    project(mixed, shrink, weight_copies, weight_v, message_refs)
    staying = placed_ref.at[pl.ds(0, half)]
    pltpu.make_async_copy(staying, staying, cache_sem.at[0]).wait()
    pltpu.make_async_copy(leaving_ref, leaving_ref, cache_sem.at[1]).wait()


def own_kernel(
    order_ref,
    adapter_ref,
    mixed_ref,
    shrink_ref,
    weight_ref,
    residual_ref,
    message_ref,
    stream_ref,
    mix_ref,
    slot_ref,
    weight_v,
    weight_sem,
):
    weight_copies = weight_columns(weight_ref, weight_v, weight_sem, (0,))
    for copy in weight_copies:
        copy.start()

    steps, rows, features = residual_ref.shape
    group = mix_ref.shape[0] // 2
    half = group // steps
    blocks = mix_ref.shape[1] // (2 * group)
    slots = slot_ref.shape[1] // 2
    me = lax.axis_index("replica")
    out_row = iota((steps * rows, 1), 0)
    step_of, place_of = div(out_row, rows), mod(out_row, rows)
    landed_row = jnp.zeros_like(out_row)
    slot = jnp.zeros_like(out_row)
    counts = [jnp.int32(0), jnp.int32(0)]
    for j in range(rows):
        request = order_ref[me * rows + j]
        away = jnp.where(div(request, rows) == me, 0, 1)
        count = jnp.where(away == 0, counts[0], counts[1])
        counts = [counts[0] + 1 - away, counts[1] + away]
        here = place_of == j
        landed_row = jnp.where(here, away * (blocks * group) + count, landed_row)
        slot = jnp.where(here, away * slots + adapter_ref[request], slot)
    landed_row = landed_row + step_of * half
    column = iota(mix_ref.shape, 1)
    kept = column - mod(column, blocks * group) + mod(column, group)
    mix_ref[...] = one_hot(kept == landed_row)
    slot_ref[...] = one_hot(iota(slot_ref.shape, 1) == slot).astype(f32)
    source = jnp.zeros_like(out_row)
    for side in range(2):
        place = me if side == 0 else 1 - me
        count = jnp.int32(0)
        for j in range(rows):
            request = order_ref[place * rows + j]
            hit = div(request, rows) == me
            index = jnp.where(hit, count, -1)
            here = (div(out_row, group) == side) & (mod(out_row, half) == index)
            source = jnp.where(here, mod(request, rows), source)
            count = count + hit.astype(jnp.int32)
    source = source + div(mod(out_row, group), half) * rows
    stream = dot(
        one_hot(iota((steps * rows, steps * rows), 1) == source),
        residual_ref[...].reshape(steps * rows, features),
    )
    stream_ref[:, :features] = stream.astype(bf16)
    stream_ref[:, features:] = jnp.zeros((steps * rows, LANES), bf16)

    project(mixed_ref[...], shrink_ref[...], weight_copies, weight_v, [message_ref])


def attend_call(order, lengths, table, adapters, queries, fresh, down, pool, weight, partners):
    steps, rows, features = queries.shape
    tensor = lax.axis_size("tensor")
    blocks, block_size, width = pool.shape
    positions = table.shape[0] * block_size
    score_rows = rows * steps * features // (width // 2)
    out_width = weight.shape[1] // tensor
    spans = tensor // QUAD
    message = (steps * rows, spans * out_width + LANES)
    cache = (table.shape[0], block_size, width)
    smem = pl.BlockSpec(memory_space=pltpu.SMEM)
    vmem = pl.BlockSpec(memory_space=pltpu.VMEM)
    hbm = pl.BlockSpec(memory_space=pl.ANY)
    return pl.pallas_call(
        functools.partial(attend_kernel, partners=partners),
        out_shape=[jax.ShapeDtypeStruct(message, bf16)] * len(partners)
        + [
            jax.ShapeDtypeStruct((steps * rows, features), bf16),
            jax.ShapeDtypeStruct((steps * rows, LANES), bf16),
            jax.ShapeDtypeStruct((rows,) + cache, bf16),
            jax.ShapeDtypeStruct((rows // lax.axis_size("replica"),) + cache, bf16),
        ],
        in_specs=[smem] * 4 + [hbm] * 5,
        out_specs=[vmem] * (len(partners) + 2) + [hbm] * 2,
        scratch_shapes=[
            pltpu.VMEM(queries.shape, bf16),
            pltpu.VMEM(fresh.shape, bf16),
            pltpu.VMEM(down.shape, bf16),
            pltpu.VMEM((blocks, block_size, width), bf16),
            pltpu.VMEM((len(partners) * spans, weight.shape[0], out_width), bf16),
            pltpu.VMEM((score_rows, positions), f32),
            pltpu.VMEM((score_rows, positions), f32),
            pltpu.VMEM((score_rows, width // 2), f32),
            pltpu.VMEM((block_size, width), bf16),
            pltpu.SMEM((rows,), jnp.int32),
            pltpu.SMEM((rows,), jnp.int32),
            pltpu.SemaphoreType.DMA((3,)),
            pltpu.SemaphoreType.DMA,
            pltpu.SemaphoreType.DMA((len(partners) * spans,)),
            pltpu.SemaphoreType.DMA((2,)),
        ],
        compiler_params=pltpu.CompilerParams(vmem_limit_bytes=VMEM_BYTES),
        name="attend",
    )(order, lengths, table, adapters, queries, fresh, down, pool, weight)


def own_call(order, adapters, mixed, shrink, weight, residual, slots):
    steps, rows, features = residual.shape
    tensor = lax.axis_size("tensor")
    out_width = weight.shape[1] // tensor
    spans = tensor // QUAD
    message = (mixed.shape[0], spans * out_width + LANES)
    smem = pl.BlockSpec(memory_space=pltpu.SMEM)
    vmem = pl.BlockSpec(memory_space=pltpu.VMEM)
    hbm = pl.BlockSpec(memory_space=pl.ANY)
    return pl.pallas_call(
        own_kernel,
        out_shape=(
            jax.ShapeDtypeStruct(message, bf16),
            jax.ShapeDtypeStruct((steps * rows, features + LANES), bf16),
            jax.ShapeDtypeStruct((steps * rows, (spans + 1) * steps * rows), bf16),
            jax.ShapeDtypeStruct((steps * rows, 2 * slots), f32),
        ),
        in_specs=[smem] * 2 + [vmem] * 2 + [hbm, vmem],
        out_specs=(vmem,) * 4,
        scratch_shapes=[
            pltpu.VMEM((spans, weight.shape[0], out_width), bf16),
            pltpu.SemaphoreType.DMA((spans,)),
        ],
        compiler_params=pltpu.CompilerParams(vmem_limit_bytes=MIDDLE_BYTES),
        cost_estimate=pl.CostEstimate(
            flops=2 * mixed.shape[0] * weight.shape[0] * spans * out_width,
            bytes_accessed=4 * weight.shape[0] * spans * out_width,
            transcendentals=0,
        ),
        name="own",
    )(order, adapters, mixed, shrink, weight, residual)


def merge_kernel(*refs, spans):
    stream_ref, messages, outs = refs[0], refs[1 : -2 * spans], refs[-2 * spans :]
    total = messages[0][...].astype(f32)
    for ref in messages[1:]:
        total = total + ref[...].astype(f32)
    total = total.astype(bf16)
    group = total.shape[0] // 2
    out_width = (total.shape[1] - LANES) // spans
    for side in range(2):
        span = slice(side * group, (side + 1) * group)
        for n in range(spans):
            ref = outs[side * spans + n]
            ref[:group, :out_width] = total[span, n * out_width : (n + 1) * out_width]
            ref[:group, out_width:] = total[span, spans * out_width :]
        outs[side * spans][group:] = stream_ref[span, :]


def merge_call(stream, messages, spans):
    rows, columns = messages[0].shape
    vmem = pl.BlockSpec(memory_space=pltpu.VMEM)
    width = (columns - LANES) // spans + LANES
    pieces = [
        jax.ShapeDtypeStruct((rows if n == 0 else rows // 2, width), bf16) for n in range(spans)
    ]
    pieces = pl.pallas_call(
        functools.partial(merge_kernel, spans=spans),
        out_shape=pieces * 2,
        in_specs=[vmem] * (1 + len(messages)),
        out_specs=[vmem] * (2 * spans),
        compiler_params=pltpu.CompilerParams(vmem_limit_bytes=SMALL_BYTES),
        name="merge",
    )(stream, *messages)
    return pieces[:spans], pieces[spans:]


def arrive_kernel(order_ref, arrived_ref, placed_in_ref, placed_ref, sem):
    rows = placed_ref.shape[0]
    me = lax.axis_index("replica")

    def step(j, count):
        hit = div(order_ref[me * rows + j], rows) != me

        @pl.when(hit)
        def _():
            pltpu.make_async_copy(arrived_ref.at[count], placed_ref.at[j], sem).start()

        return count + hit.astype(jnp.int32)

    lax.fori_loop(0, rows, step, jnp.int32(0))
    pltpu.make_async_copy(arrived_ref, arrived_ref, sem).wait()


def arrive_call(order, arrived, placed):
    hbm = pl.BlockSpec(memory_space=pl.ANY)
    return pl.pallas_call(
        arrive_kernel,
        out_shape=jax.ShapeDtypeStruct(placed.shape, bf16),
        in_specs=[
            pl.BlockSpec(memory_space=pltpu.SMEM),
            pl.BlockSpec(memory_space=pltpu.VMEM),
            hbm,
        ],
        out_specs=hbm,
        scratch_shapes=[pltpu.SemaphoreType.DMA],
        input_output_aliases={2: 0},
        compiler_params=pltpu.CompilerParams(vmem_limit_bytes=SMALL_BYTES),
        cost_estimate=pl.CostEstimate(
            flops=0, bytes_accessed=4 * arrived.size, transcendentals=0
        ),
        name="arrive",
    )(order, arrived, placed)


def finish_kernel(mix_ref, slot_ref, up_ref, other_up_ref, *rest):
    landed_refs, out_ref = rest[:-1], rest[-1]
    slots, rank, features = up_ref.shape
    sums = dot(mix_ref[...], jnp.concatenate([ref[...] for ref in landed_refs], axis=0))
    shrink = sums[:, features : features + rank].astype(bf16).astype(f32)
    result = sums[:, :features]
    for side, up in enumerate((up_ref, other_up_ref)):
        wide = jnp.concatenate(
            [shrink * slot_ref[:, side * slots + n : side * slots + n + 1] for n in range(slots)],
            axis=1,
        ).astype(bf16)
        result = result + adapter_scale * dot(wide, up[...].reshape(slots * rank, features))
    out_ref[...] = result.astype(bf16).reshape(out_ref.shape)


def shards(
    queries,
    latest_key_value,
    residual,
    paged_cache_pool,
    adapter_down_weight,
    adapter_up_weight,
    output_weight,
    lengths,
    previous_block_table,
    request_order_after,
    request_adapter_index,
):
    steps, rows, features = queries.shape
    replicas = lax.axis_size("replica")
    tensor = lax.axis_size("tensor")
    blocks, _, block_size, width = paged_cache_pool.shape
    table_blocks = previous_block_table.shape[1]
    pool = paged_cache_pool.reshape(blocks, block_size, width)
    fresh = latest_key_value.reshape(steps, rows, width)
    swap = [(0, 1), (1, 0)]
    other_up = lax.ppermute(adapter_up_weight, "replica", swap)

    table = previous_block_table.T
    *messages, mixed, shrink, placed, leaving = attend_call(
        request_order_after,
        lengths,
        table,
        request_adapter_index,
        queries,
        fresh,
        adapter_down_weight,
        pool,
        output_weight,
        (3, 2, 1),
    )
    spans = tensor // QUAD
    landed = []
    for partner, message in zip((3, 2, 1), messages):
        pairs = [(t, t ^ partner) for t in range(tensor)]
        landed.append(lax.ppermute(message, "tensor", pairs))
    own, stream, mix, slot = own_call(
        request_order_after,
        request_adapter_index,
        mixed,
        shrink,
        output_weight,
        residual,
        adapter_up_weight.shape[0],
    )
    arrived = lax.ppermute(leaving, "replica", swap)
    stays, leaves = merge_call(stream, [own] + landed, spans)

    def deliver(piece, span, away):
        pairs = [
            (r * tensor + t, (r ^ away) * tensor + (t ^ (span * QUAD)))
            for r in range(replicas)
            for t in range(tensor)
        ]
        return lax.ppermute(piece, ("replica", "tensor"), pairs)

    stays = [stays[0]] + [deliver(stays[n], n, 0) for n in range(1, spans)]
    leaves = [deliver(leaves[n], n, 1) for n in reversed(range(spans))][::-1]
    placed_cache = arrive_call(request_order_after, arrived, placed)
    placed_cache, mix = lax.optimization_barrier((placed_cache, mix))
    vmem = pl.BlockSpec(memory_space=pltpu.VMEM)
    layer_out = pl.pallas_call(
        finish_kernel,
        out_shape=jax.ShapeDtypeStruct((steps, rows, features), bf16),
        in_specs=[vmem] * (4 + 2 * spans),
        out_specs=vmem,
        compiler_params=pltpu.CompilerParams(vmem_limit_bytes=SMALL_BYTES),
        name="finish",
    )(mix, slot, adapter_up_weight, other_up, *stays, *leaves)
    return (layer_out, placed_cache.reshape(rows, table_blocks, 1, block_size, width))


def solution(mesh):
    in_specs = (
        P(None, ("groups", "replica"), "tensor"),
        P(None, ("groups", "replica"), "tensor", None),
        P(None, ("groups", "replica"), "tensor"),
        P(("groups", "replica"), "tensor", None, None),
        P(("groups", "replica"), None, "tensor"),
        P(("groups", "replica"), None, "tensor"),
        P("tensor", None),
        P("groups"),
        P("groups", None),
        P("groups"),
        P("groups"),
    )
    out_specs = (
        P(None, ("groups", "replica"), "tensor"),
        P(("groups", "replica"), None, "tensor", None, None),
    )
    return jax.shard_map(shards, mesh=mesh, in_specs=in_specs, out_specs=out_specs, check_vma=False)
```

time: 40.4 us -> 31.1 us (0.77)
  waiting for transfers between devices: 10.9 us -> 4.09 us
  local copies, waits for them, and re-layouts: 2.97 us -> 1.55 us
  Pallas kernels: 17.1 us -> 16.5 us
    all_to_all x1 -> x0, waiting for transfers between devices: 9.34 us -> none  [shards(): lax.all_to_all(send.reshape((replicas * tensor,) + send.shape[2:]), ('rep...]
    ppermute x2 -> x7, starting transfers between devices: 0.62 us -> 7.87 us  [the longest x3 4.52 us: shards(): landed.append(lax.ppermute(message, 'tensor', pairs))]
    all_to_all x1 -> x0, starting transfers between devices: 7.06 us -> none  [shards(): lax.all_to_all(send.reshape((replicas * tensor,) + send.shape[2:]), ('rep...]
    ppermute x2 -> x7, waiting for transfers between devices: 1.53 us -> 4.08 us  [the longest x3 2.33 us: deliver(): return lax.ppermute(piece, ('replica', 'tensor'), pairs)]
    unnamed x12, local copies, waits for them, and re-layouts: 2.97 us -> 1.55 us
    pallas_call x2 -> x4, Pallas kernels: 16 us -> 15.4 us  [the longest x1 10 us: attend_call(): pl.pallas_call(functools.partial(attend_kernel, partners=partners), out_s...]
  transfers between devices with their start and end apart: 4 -> 8, of which waited for: 2 -> 3; matrix products, arithmetic and copies ran while one was open for 0% -> 0% of each run, Pallas kernels for 40% -> 17%
where the time goes in v2:
time: 31.1 us; the launch traced here: 30.8 us
  Pallas kernels  16.5 us (53%)
  starting transfers between devices  7.95 us (26%)
  waiting for transfers between devices  4.09 us (13%)
  local copies, waits for them, and re-layouts  1.55 us (5%)
  between operations  0.73 us (2%)
    pallas_call x1, Pallas kernels, attend_call(): pl.pallas_call(functools.partial(attend_kernel, partners=partners), out_s...  10 us
    ppermute x3, starting transfers between devices, shards(): landed.append(lax.ppermute(message, 'tensor', pairs))  4.52 us
    pallas_call x1, Pallas kernels, own_call(): pl.pallas_call(own_kernel, out_shape=(jax.ShapeDtypeStruct(message, bf16)...  3.43 us
    ppermute x3, starting transfers between devices, deliver(): return lax.ppermute(piece, ('replica', 'tensor'), pairs)  2.83 us
    ppermute x3, waiting for transfers between devices, deliver(): return lax.ppermute(piece, ('replica', 'tensor'), pairs)  2.33 us
    pallas_call x1, Pallas kernels, arrive_call(): pl.pallas_call(arrive_kernel, out_shape=jax.ShapeDtypeStruct(placed.shape...  1.87 us
    ppermute x3, waiting for transfers between devices, shards(): landed.append(lax.ppermute(message, 'tensor', pairs))  1.76 us
    unnamed x12, local copies, waits for them, and re-layouts  1.55 us
  transfers between devices with their start and end apart: 8, of which 3 were waited for; matrix products, arithmetic and copies ran while one was open for 0% of the time, Pallas kernels for 17%

profile of v2, /device:TPU:0, one launch (start us, length us, event | category | flops | bytes accessed | tf_op | source)
XLA Modules:
  0.0 30.8 jit_solution(9723496851637856137)
XLA Ops:
  0.6 0.0 copy-start
  0.6 0.0 copy-start.1
  0.7 0.0 copy-start.4
  0.7 0.0 copy-start.5
  0.7 10.0 %attend.1 = (bf16[32,2176]{1,0:T(8,128)(2,1)}, bf16[32,2176]{1,0:T(8,128)(2,1)}, bf16[32,2176]{1,0:T(8,128)(2,1)}, bf16[32,1024]{1,0:T(8,128)(2,1)}, bf16[32,128...) custom-call(s32[32]{0:T(128)} %order_ref.5, s32[32]{0:T(128)} %lengths_ref.1, ...), custom_call_target="tpu_custom_call" | custom-call | tf_op jit(solution)/shard_map/attend/pallas_call | solution.py:365
  10.7 0.5 %collective-permute-start = (bf16[8,8,64,256]{3,2,1,0:T(8,128)(2,1)}, bf16[8,8,64,256]{3,2,1,0:T(8,128)(2,1)S(1)}, u32[]{:S(2)}, u32[]{:S(2)}) collective-permute-start(bf16[8,8,64,256]{3,2,1,0:T(8,128)(2,1)} %get-tuple-element.19), channel_id=1, source_target_pairs={{0,8},{8,0},{1,9},{9,1},{2,10},{10,2},{3,11},{11,3},{4,12},{12,4},... | collective-permute-start | bytes 6291464 | tf_op jit(solution)/shard_map/ppermute | solution.py:569
  11.2 0.0 copy-done
  11.2 0.1 collective-permute-start.1
  11.3 4.0 %collective-permute-start.2 = (bf16[32,2176]{1,0:T(8,128)(2,1)}, bf16[32,2176]{1,0:T(8,128)(2,1)S(1)}, u32[]{:S(2)}, u32[]{:S(2)}) collective-permute-start(bf16[32,2176]{1,0:T(8,128)(2,1)} %get-tuple-element.28), channel_id=1, source_target_pairs={{0,3},{1,2},{2,1},{3,0},{4,7},{5,6},{6,5},{7,4},{8,11},{9,10},{10,... | collective-permute-start | bytes 417800 | tf_op jit(solution)/shard_map/ppermute | solution.py:559
  15.3 0.4 %collective-permute-start.3 = (bf16[32,2176]{1,0:T(8,128)(2,1)}, bf16[32,2176]{1,0:T(8,128)(2,1)S(1)}, u32[]{:S(2)}, u32[]{:S(2)}) collective-permute-start(bf16[32,2176]{1,0:T(8,128)(2,1)} %get-tuple-element.29), channel_id=1, source_target_pairs={{0,2},{1,3},{2,0},{3,1},{4,6},{5,7},{6,4},{7,5},{8,10},{9,11},{10,... | collective-permute-start | bytes 417800 | tf_op jit(solution)/shard_map/ppermute | solution.py:559
  15.7 0.1 collective-permute-start.4
  15.8 0.0 copy-done.1
  15.8 0.0 copy-done.4
  15.8 0.0 copy-done.5
  15.8 0.0 copy-start.2
  15.8 0.8 %copy-done.2 = bf16[32,1024]{1,0:T(8,128)(2,1)S(1)} copy-done((bf16[32,1024]{1,0:T(8,128)(2,1)S(1)}, bf16[32,1024]{1,0:T(8,128)(2,1)}, u32[]{:S(2)}) %copy-start.2) | copy-done | bytes 65560
  16.7 0.7 %copy-done.3 = bf16[32,128]{1,0:T(8,128)(2,1)S(1)} copy-done((bf16[32,128]{1,0:T(8,128)(2,1)S(1)}, bf16[32,128]{1,0:T(8,128)(2,1)}, u32[]{:S(2)}) %copy-start.3) | copy-done | bytes 8216
  17.4 3.4 %own.1 = (bf16[32,2176]{1,0:T(8,128)(2,1)S(1)}, bf16[32,1152]{1,0:T(8,128)(2,1)S(1)}, bf16[32,96]{1,0:T(8,128)(2,1)S(1)}, f32[32,8]{1,0:T(8,128)S(1)}) custom-call(s32[32]{0:T(128)S(1)} %copy-done.4, s32[32]{0:T(128)S(1)} %copy-done.5, bf16[32,1024]{1,0:T(8,128)(2,1)S(1)} %copy-done.2, bf16[32,128]{1,0:T(8,128)(2,1)S(1)} %copy-done.3, ...), custom_call_target="tpu_custom_call" | custom-call | flops 134217728 | bytes 8388608 | tf_op jit(solution)/shard_map/own/pallas_call | solution.py:407
  20.8 0.0 collective-permute-done.2.refs_2_
  20.8 1.8 %collective-permute-done.3.refs_3_ = bf16[32,2176]{1,0:T(8,128)(2,1)S(1)} collective-permute-done((bf16[32,2176]{1,0:T(8,128)(2,1)}, bf16[32,2176]{1,0:T(8,128)(2,1)S(1)}, u32[]{:S(2)}, u32[]{:S(2)}) %collective-permute-start.3) | collective-permute-done | bytes 139296 | tf_op jit(solution)/shard_map/ppermute | solution.py:559
  22.6 0.0 collective-permute-done.4.refs_4_
  22.6 0.1 merge.1
  22.7 0.1 collective-permute-start.6
  22.7 2.6 %collective-permute-start.5 = (bf16[16,1152]{1,0:T(8,128)(2,1)S(1)}, bf16[16,1152]{1,0:T(8,128)(2,1)S(1)}, u32[]{:S(2)}, u32[]{:S(2)}) collective-permute-start(bf16[16,1152]{1,0:T(8,128)(2,1)S(1)} %get-tuple-element.32), channel_id=1, source_target_pairs={{0,4},{1,5},{2,6},{3,7},{4,0},{5,1},{6,2},{7,3},{8,12},{9,13},{10,... | collective-permute-start | bytes 110600 | tf_op jit(solution)/shard_map/ppermute | solution.py:578
  25.4 0.1 collective-permute-start.7
  25.5 0.0 collective-permute-done.arrived_ref
  25.5 1.9 %arrive.1 = bf16[16,8,64,256]{3,2,1,0:T(8,128)(2,1)} custom-call(s32[32]{0:T(128)S(1)} %copy-done.4, bf16[8,8,64,256]{3,2,1,0:T(8,128)(2,1)S(1)} %collective-permute-done.arrived_ref, bf16[16,8,64,256]{3,2,1,0:T(8,128)(2,1)} %get-tuple-element.20.placed_in_ref), custom_call_target="tpu_custom_call", output_to_operand_aliasing={{}: (2, {})} | custom-call | bytes 4194304 | tf_op jit(solution)/shard_map/arrive/pallas_call | solution.py:485
  27.4 0.3 collective-permute-done.5.rest_1_
  27.7 2.0 %collective-permute-done.7.rest_3_ = bf16[16,1152]{1,0:T(8,128)(2,1)S(1)} collective-permute-done((bf16[16,1152]{1,0:T(8,128)(2,1)S(1)}, bf16[16,1152]{1,0:T(8,128)(2,1)S(1)}, u32[]{:S(2)}, u32[]{:S(2)}) %collective-permute-start.7) | collective-permute-done | bytes 36896 | tf_op jit(solution)/shard_map/ppermute | solution.py:578
  29.7 0.0 collective-permute-done.6.rest_2_
  29.7 0.0 collective-permute-done.1.other_up_ref
  29.7 1.1 %finish.1 = bf16[2,16,1024]{2,1,0:T(8,128)(2,1)} custom-call(bf16[32,96]{1,0:T(8,128)(2,1)S(1)} %get-tuple-element.24.mix_ref, f32[32,8]{1,0:T(8,128)S(1)} %get-tuple-element.25.slot_ref, bf16[4,64,1024]{2,1,0:T(8,128)(2,1)S(1)} %copy-done, bf16[4,64,1024]{2,1,0:T(8,128)(2,1)S(1)} %collective-permute-done.1.other_up_ref, ...), custom_call_target="tpu_custom_call" | custom-call | tf_op jit(solution)/shard_map/finish/pallas_call | solution.py:585
  (1 shorter events, 0.0 us)
Async XLA Ops:
  0.6 10.6 %copy-start = (bf16[4,64,1024]{2,1,0:T(8,128)(2,1)S(1)}, bf16[4,64,1024]{2,1,0:T(8,128)(2,1)}, u32[]{:S(2)}) copy-start(bf16[4,64,1024]{2,1,0:T(8,128)(2,1)} %up_ref.1) | copy-start | bytes 1572868
  0.6 15.2 %copy-start.1 = (bf16[2,16,1024]{2,1,0:T(8,128)(2,1)S(1)}, bf16[2,16,1024]{2,1,0:T(8,128)(2,1)}, u32[]{:S(2)}) copy-start(bf16[2,16,1024]{2,1,0:T(8,128)(2,1)} %residual_ref.1) | copy-start | bytes 196612
  0.7 15.2 %copy-start.4 = (s32[32]{0:T(128)S(1)}, s32[32]{0:T(128)}, u32[]{:S(2)}) copy-start(s32[32]{0:T(128)} %order_ref.5) | copy-start | bytes 388
  0.7 15.2 %copy-start.5 = (s32[32]{0:T(128)S(1)}, s32[32]{0:T(128)}, u32[]{:S(2)}) copy-start(s32[32]{0:T(128)} %adapter_ref.3) | copy-start | bytes 388
  10.7 14.8 %collective-permute-start = (bf16[8,8,64,256]{3,2,1,0:T(8,128)(2,1)}, bf16[8,8,64,256]{3,2,1,0:T(8,128)(2,1)S(1)}, u32[]{:S(2)}, u32[]{:S(2)}) collective-permute-start(bf16[8,8,64,256]{3,2,1,0:T(8,128)(2,1)} %get-tuple-element.19), channel_id=1, source_target_pairs={{0,8},{8,0},{1,9},{9,1},{2,10},{10,2},{3,11},{11,3},{4,12},{12,4},... | collective-permute-start | bytes 6291464 | tf_op jit(solution)/shard_map/ppermute | solution.py:569
  11.2 18.5 %collective-permute-start.1 = (bf16[4,64,1024]{2,1,0:T(8,128)(2,1)S(1)}, bf16[4,64,1024]{2,1,0:T(8,128)(2,1)S(1)}, u32[]{:S(2)}, u32[]{:S(2)}) collective-permute-start(bf16[4,64,1024]{2,1,0:T(8,128)(2,1)S(1)} %copy-done), channel_id=1, source_target_pairs={{0,8},{8,0},{1,9},{9,1},{2,10},{10,2},{3,11},{11,3},{4,12},{12,4},... | collective-permute-start | bytes 1572872 | tf_op jit(solution)/shard_map/ppermute | solution.py:540
  11.3 9.5 %collective-permute-start.2 = (bf16[32,2176]{1,0:T(8,128)(2,1)}, bf16[32,2176]{1,0:T(8,128)(2,1)S(1)}, u32[]{:S(2)}, u32[]{:S(2)}) collective-permute-start(bf16[32,2176]{1,0:T(8,128)(2,1)} %get-tuple-element.28), channel_id=1, source_target_pairs={{0,3},{1,2},{2,1},{3,0},{4,7},{5,6},{6,5},{7,4},{8,11},{9,10},{10,... | collective-permute-start | bytes 417800 | tf_op jit(solution)/shard_map/ppermute | solution.py:559
  15.3 7.3 %collective-permute-start.3 = (bf16[32,2176]{1,0:T(8,128)(2,1)}, bf16[32,2176]{1,0:T(8,128)(2,1)S(1)}, u32[]{:S(2)}, u32[]{:S(2)}) collective-permute-start(bf16[32,2176]{1,0:T(8,128)(2,1)} %get-tuple-element.29), channel_id=1, source_target_pairs={{0,2},{1,3},{2,0},{3,1},{4,6},{5,7},{6,4},{7,5},{8,10},{9,11},{10,... | collective-permute-start | bytes 417800 | tf_op jit(solution)/shard_map/ppermute | solution.py:559
  15.7 6.9 %collective-permute-start.4 = (bf16[32,2176]{1,0:T(8,128)(2,1)}, bf16[32,2176]{1,0:T(8,128)(2,1)S(1)}, u32[]{:S(2)}, u32[]{:S(2)}) collective-permute-start(bf16[32,2176]{1,0:T(8,128)(2,1)} %get-tuple-element.30), channel_id=1, source_target_pairs={{0,1},{1,0},{2,3},{3,2},{4,5},{5,4},{6,7},{7,6},{8,9},{9,8},{10,11... | collective-permute-start | bytes 417800 | tf_op jit(solution)/shard_map/ppermute | solution.py:559
  15.8 0.8 %copy-start.2 = (bf16[32,1024]{1,0:T(8,128)(2,1)S(1)}, bf16[32,1024]{1,0:T(8,128)(2,1)}, u32[]{:S(2)}) copy-start(bf16[32,1024]{1,0:T(8,128)(2,1)} %get-tuple-element.21.mixed_ref) | copy-start | bytes 196612
  16.7 0.7 %copy-start.3 = (bf16[32,128]{1,0:T(8,128)(2,1)S(1)}, bf16[32,128]{1,0:T(8,128)(2,1)}, u32[]{:S(2)}) copy-start(bf16[32,128]{1,0:T(8,128)(2,1)} %get-tuple-element.22.shrink_ref) | copy-start | bytes 24580
  22.7 7.1 %collective-permute-start.6 = (bf16[32,1152]{1,0:T(8,128)(2,1)S(1)}, bf16[32,1152]{1,0:T(8,128)(2,1)S(1)}, u32[]{:S(2)}, u32[]{:S(2)}) collective-permute-start(bf16[32,1152]{1,0:T(8,128)(2,1)S(1)} %get-tuple-element.33), channel_id=1, source_target_pairs={{0,8},{1,9},{2,10},{3,11},{4,12},{5,13},{6,14},{7,15},{8,0},{9,1},... | collective-permute-start | bytes 221192 | tf_op jit(solution)/shard_map/ppermute | solution.py:578
  22.7 4.9 %collective-permute-start.5 = (bf16[16,1152]{1,0:T(8,128)(2,1)S(1)}, bf16[16,1152]{1,0:T(8,128)(2,1)S(1)}, u32[]{:S(2)}, u32[]{:S(2)}) collective-permute-start(bf16[16,1152]{1,0:T(8,128)(2,1)S(1)} %get-tuple-element.32), channel_id=1, source_target_pairs={{0,4},{1,5},{2,6},{3,7},{4,0},{5,1},{6,2},{7,3},{8,12},{9,13},{10,... | collective-permute-start | bytes 110600 | tf_op jit(solution)/shard_map/ppermute | solution.py:578
  25.4 4.3 %collective-permute-start.7 = (bf16[16,1152]{1,0:T(8,128)(2,1)S(1)}, bf16[16,1152]{1,0:T(8,128)(2,1)S(1)}, u32[]{:S(2)}, u32[]{:S(2)}) collective-permute-start(bf16[16,1152]{1,0:T(8,128)(2,1)S(1)} %get-tuple-element.34), channel_id=1, source_target_pairs={{0,12},{1,13},{2,14},{3,15},{4,8},{5,9},{6,10},{7,11},{8,4},{9,5},... | collective-permute-start | bytes 110600 | tf_op jit(solution)/shard_map/ppermute | solution.py:578

commit v3 on v2

--- a/solution.py
+++ b/solution.py
@@ -12,9 +12,11 @@
 f32 = jnp.float32
 LANES = 128
 QUAD = 4
+PARTNERS = ((3, 3), (2, 1), (1, 2))
+ATTEND_FLOPS = 40_000_000_000
+MERGE_FLOPS = 50_000_000_000
 VMEM_BYTES = 56 * 1024 * 1024
 SMALL_BYTES = 8 * 1024 * 1024
-MIDDLE_BYTES = 52 * 1024 * 1024
 
 
 def iota(shape, dim):
@@ -52,33 +54,15 @@
     lax.fori_loop(0, row_count, step, jnp.int32(0))
 
 
-def weight_columns(weight_ref, weight_v, sems, partners):
-    out_width = weight_v.shape[2]
-    spans = weight_v.shape[0] // len(partners)
+def project(mixed_ref, shrink_ref, weight_ref, message_ref, partner):
+    out_width = weight_ref.shape[1] // lax.axis_size("tensor")
+    spans = message_ref.shape[1] // out_width
     here = lax.axis_index("tensor")
-    copies = []
-    for n, partner in enumerate(partners):
-        for span in range(spans):
-            start = pl.multiple_of((here ^ (span * QUAD + partner)) * out_width, out_width)
-            slot = n * spans + span
-            copies.append(
-                pltpu.make_async_copy(
-                    weight_ref.at[:, pl.ds(start, out_width)], weight_v.at[slot], sems.at[slot]
-                )
-            )
-    return copies
-
-
-def project(mixed, shrink, weight_copies, weight_v, message_refs):
-    out_width = weight_v.shape[2]
-    spans = weight_v.shape[0] // len(message_refs)
-    for n, message_ref in enumerate(message_refs):
-        message_ref[:, spans * out_width :] = shrink
-        for span in range(spans):
-            slot = n * spans + span
-            weight_copies[slot].wait()
-            part = dot(mixed, weight_v[slot]).astype(bf16)
-            message_ref[:, span * out_width : (span + 1) * out_width] = part
+    message_ref[:, spans * out_width :] = shrink_ref[...]
+    for span in range(spans):
+        start = pl.multiple_of((here ^ (span * QUAD + partner)) * out_width, out_width)
+        part = dot(mixed_ref[...], weight_ref[:, pl.ds(start, out_width)])
+        message_ref[:, span * out_width : (span + 1) * out_width] = part.astype(bf16)
 
 
 def attend_kernel(
@@ -89,33 +73,27 @@
     queries_hbm,
     fresh_hbm,
     down_hbm,
+    residual_hbm,
     pool_ref,
-    weight_ref,
-    *rest,
-    partners,
+    mixed_ref,
+    shrink_ref,
+    pool_v,
+    leaving_ref,
+    stream_ref,
+    mix_ref,
+    slot_ref,
+    queries_ref,
+    fresh_ref,
+    down_ref,
+    residual_ref,
+    scores_v,
+    probs_v,
+    attended_v,
+    found,
+    target,
+    small_sem,
+    pool_sem,
 ):
-    message_refs, rest = rest[: len(partners)], rest[len(partners) :]
-    (
-        mixed_ref,
-        shrink_ref,
-        placed_ref,
-        leaving_ref,
-        queries_ref,
-        fresh_ref,
-        down_ref,
-        pool_v,
-        weight_v,
-        scores_v,
-        probs_v,
-        attended_v,
-        zero_v,
-        found,
-        target,
-        small_sem,
-        pool_sem,
-        weight_sem,
-        cache_sem,
-    ) = rest
     steps, rows, features = queries_ref.shape
     blocks, block_size, width = pool_v.shape
     head = width // 2
@@ -132,17 +110,20 @@
     small_copies = [
         pltpu.make_async_copy(source, target, small_sem.at[n])
         for n, (source, target) in enumerate(
-            ((queries_hbm, queries_ref), (fresh_hbm, fresh_ref), (down_hbm, down_ref))
+            (
+                (queries_hbm, queries_ref),
+                (fresh_hbm, fresh_ref),
+                (down_hbm, down_ref),
+                (residual_hbm, residual_ref),
+            )
         )
     ]
     pool_copy = pltpu.make_async_copy(pool_ref, pool_v, pool_sem)
-    weight_copies = weight_columns(weight_ref, weight_v, weight_sem, partners)
     small_copies[0].start()
     small_copies[1].start()
     pool_copy.start()
     small_copies[2].start()
-    for copy in weight_copies[:2]:
-        copy.start()
+    small_copies[3].start()
 
     for place in range(places):
         rank_rows(order_ref, found, target, me, me if place == 0 else 1 - me, rows, place * half)
@@ -172,8 +153,6 @@
         fresh_scores.append(jnp.where(step_of >= s, value, f32(-1e30)))
 
     pool_copy.wait()
-    for copy in weight_copies[2:]:
-        copy.start()
 
     def block_rows(row, lo):
         return jnp.concatenate(
@@ -181,8 +160,7 @@
             axis=0,
         )
 
-    zero_v[...] = jnp.zeros_like(zero_v)
-    position = iota(zero_v.shape, 0)
+    position = iota((block_size, width), 0)
     for row in range(rows):
         length = lengths_ref[first + row]
         full = div(length, block_size)
@@ -252,180 +230,165 @@
     mixed_ref[...] = mixed
     shrink_ref[...] = shrink
 
-    def write_cache(index, carry):
-        local = found[index]
-        length = lengths_ref[first + local]
-
-        def write(row_ref, sem):
-            for b in range(table_blocks):
-
-                @pl.when(b * block_size < length)
-                def _():
-                    source = pool_v.at[table_ref[b, first + local]]
-                    pltpu.make_async_copy(source, row_ref.at[b], sem).start()
-
-                @pl.when(b * block_size >= length)
-                def _():
-                    pltpu.make_async_copy(zero_v, row_ref.at[b], sem).start()
-
-        @pl.when(index < half)
-        def _():
-            write(placed_ref.at[target[index]], cache_sem.at[0])
-
-        @pl.when(index >= half)
-        def _():
-            write(leaving_ref.at[index - half], cache_sem.at[1])
+    def copy_leaving(index, carry):
+        request = first + found[half + index]
+        length = lengths_ref[request]
+        for b in range(table_blocks):
+
+            @pl.when(b * block_size < length)
+            def _():
+                leaving_ref[index, b] = pool_v[table_ref[b, request]]
+
+            @pl.when(b * block_size >= length)
+            def _():
+                leaving_ref[index, b] = jnp.zeros((block_size, width), bf16)
 
         return carry
 
-    lax.fori_loop(0, rows, write_cache, 0)
-    project(mixed, shrink, weight_copies, weight_v, message_refs)
-    staying = placed_ref.at[pl.ds(0, half)]
-    pltpu.make_async_copy(staying, staying, cache_sem.at[0]).wait()
-    pltpu.make_async_copy(leaving_ref, leaving_ref, cache_sem.at[1]).wait()
-
-
-def own_kernel(
-    order_ref,
-    adapter_ref,
-    mixed_ref,
-    shrink_ref,
-    weight_ref,
-    residual_ref,
-    message_ref,
-    stream_ref,
-    mix_ref,
-    slot_ref,
-    weight_v,
-    weight_sem,
-):
-    weight_copies = weight_columns(weight_ref, weight_v, weight_sem, (0,))
-    for copy in weight_copies:
-        copy.start()
-
-    steps, rows, features = residual_ref.shape
-    group = mix_ref.shape[0] // 2
-    half = group // steps
-    blocks = mix_ref.shape[1] // (2 * group)
-    slots = slot_ref.shape[1] // 2
-    me = lax.axis_index("replica")
+    lax.fori_loop(0, half, copy_leaving, 0)
+
+    small_copies[3].wait()
+    wanted = step_index * rows + source
+    stream = dot(
+        one_hot(iota((steps * rows, steps * rows), 1) == wanted),
+        residual_ref[...].reshape(steps * rows, features),
+    )
+    stream_ref[:, :features] = stream.astype(bf16)
+    stream_ref[:, features:] = jnp.zeros((steps * rows, LANES), bf16)
+
+    group = steps * half
+    landed_blocks = mix_ref.shape[1] // (places * group)
     out_row = iota((steps * rows, 1), 0)
     step_of, place_of = div(out_row, rows), mod(out_row, rows)
     landed_row = jnp.zeros_like(out_row)
-    slot = jnp.zeros_like(out_row)
+    slot_of = jnp.zeros_like(out_row)
     counts = [jnp.int32(0), jnp.int32(0)]
     for j in range(rows):
-        request = order_ref[me * rows + j]
+        request = order_ref[first + j]
         away = jnp.where(div(request, rows) == me, 0, 1)
         count = jnp.where(away == 0, counts[0], counts[1])
         counts = [counts[0] + 1 - away, counts[1] + away]
         here = place_of == j
-        landed_row = jnp.where(here, away * (blocks * group) + count, landed_row)
-        slot = jnp.where(here, away * slots + adapter_ref[request], slot)
+        landed_row = jnp.where(here, away * (landed_blocks * group) + count, landed_row)
+        slot_of = jnp.where(here, away * slots + adapter_ref[request], slot_of)
     landed_row = landed_row + step_of * half
     column = iota(mix_ref.shape, 1)
-    kept = column - mod(column, blocks * group) + mod(column, group)
+    kept = column - mod(column, landed_blocks * group) + mod(column, group)
     mix_ref[...] = one_hot(kept == landed_row)
-    slot_ref[...] = one_hot(iota(slot_ref.shape, 1) == slot).astype(f32)
-    source = jnp.zeros_like(out_row)
-    for side in range(2):
-        place = me if side == 0 else 1 - me
-        count = jnp.int32(0)
-        for j in range(rows):
-            request = order_ref[place * rows + j]
-            hit = div(request, rows) == me
-            index = jnp.where(hit, count, -1)
-            here = (div(out_row, group) == side) & (mod(out_row, half) == index)
-            source = jnp.where(here, mod(request, rows), source)
-            count = count + hit.astype(jnp.int32)
-    source = source + div(mod(out_row, group), half) * rows
-    stream = dot(
-        one_hot(iota((steps * rows, steps * rows), 1) == source),
-        residual_ref[...].reshape(steps * rows, features),
-    )
-    stream_ref[:, :features] = stream.astype(bf16)
-    stream_ref[:, features:] = jnp.zeros((steps * rows, LANES), bf16)
-
-    project(mixed_ref[...], shrink_ref[...], weight_copies, weight_v, [message_ref])
-
-
-def attend_call(order, lengths, table, adapters, queries, fresh, down, pool, weight, partners):
+    slot_ref[...] = one_hot(iota(slot_ref.shape, 1) == slot_of).astype(f32)
+
+
+def message_kernel(mixed_ref, shrink_ref, weight_ref, message_ref, *, partners):
+    partner = jnp.where(lax.axis_index("replica") == 0, partners[0], partners[1])
+    project(mixed_ref, shrink_ref, weight_ref, message_ref, partner)
+
+
+def stay_kernel(order_ref, lengths_ref, table_ref, pool_v, placed_ref, zero_v, sem):
+    rows, table_blocks, block_size, _ = placed_ref.shape
+    me = lax.axis_index("replica")
+    zero_v[...] = jnp.zeros_like(zero_v)
+
+    def step(j, carry):
+        request = order_ref[me * rows + j]
+        length = lengths_ref[request]
+
+        @pl.when(div(request, rows) == me)
+        def _():
+            for b in range(table_blocks):
+                target = placed_ref.at[j, b]
+
+                @pl.when(b * block_size < length)
+                def _():
+                    source = pool_v.at[table_ref[b, request]]
+                    pltpu.make_async_copy(source, target, sem).start()
+
+                @pl.when(b * block_size >= length)
+                def _():
+                    pltpu.make_async_copy(zero_v, target, sem).start()
+
+        return carry
+
+    lax.fori_loop(0, rows, step, 0)
+    staying = placed_ref.at[pl.ds(0, rows // 2)]
+    pltpu.make_async_copy(staying, staying, sem).wait()
+
+
+def in_hbm(value):
+    return pltpu.with_memory_space_constraint(value, pltpu.HBM)
+
+
+def attend_call(order, lengths, table, adapters, queries, fresh, down, residual, pool):
     steps, rows, features = queries.shape
-    tensor = lax.axis_size("tensor")
     blocks, block_size, width = pool.shape
-    positions = table.shape[0] * block_size
+    table_blocks = table.shape[0]
+    positions = table_blocks * block_size
     score_rows = rows * steps * features // (width // 2)
-    out_width = weight.shape[1] // tensor
-    spans = tensor // QUAD
-    message = (steps * rows, spans * out_width + LANES)
-    cache = (table.shape[0], block_size, width)
+    spans = lax.axis_size("tensor") // QUAD
     smem = pl.BlockSpec(memory_space=pltpu.SMEM)
     vmem = pl.BlockSpec(memory_space=pltpu.VMEM)
     hbm = pl.BlockSpec(memory_space=pl.ANY)
     return pl.pallas_call(
-        functools.partial(attend_kernel, partners=partners),
-        out_shape=[jax.ShapeDtypeStruct(message, bf16)] * len(partners)
-        + [
-            jax.ShapeDtypeStruct((steps * rows, features), bf16),
-            jax.ShapeDtypeStruct((steps * rows, LANES), bf16),
-            jax.ShapeDtypeStruct((rows,) + cache, bf16),
-            jax.ShapeDtypeStruct((rows // lax.axis_size("replica"),) + cache, bf16),
-        ],
+        attend_kernel,
+        out_shape=(
+            pltpu.VMEM((steps * rows, features), bf16),
+            pltpu.VMEM((steps * rows, LANES), bf16),
+            pltpu.VMEM(pool.shape, bf16),
+            pltpu.VMEM((rows // 2, table_blocks, block_size, width), bf16),
+            pltpu.VMEM((steps * rows, features + LANES), bf16),
+            pltpu.VMEM((steps * rows, (spans + 1) * steps * rows), bf16),
+            pltpu.VMEM((steps * rows, 2 * down.shape[0]), f32),
+        ),
         in_specs=[smem] * 4 + [hbm] * 5,
-        out_specs=[vmem] * (len(partners) + 2) + [hbm] * 2,
+        out_specs=(vmem,) * 7,
         scratch_shapes=[
             pltpu.VMEM(queries.shape, bf16),
             pltpu.VMEM(fresh.shape, bf16),
             pltpu.VMEM(down.shape, bf16),
-            pltpu.VMEM((blocks, block_size, width), bf16),
-            pltpu.VMEM((len(partners) * spans, weight.shape[0], out_width), bf16),
+            pltpu.VMEM(residual.shape, bf16),
             pltpu.VMEM((score_rows, positions), f32),
             pltpu.VMEM((score_rows, positions), f32),
             pltpu.VMEM((score_rows, width // 2), f32),
-            pltpu.VMEM((block_size, width), bf16),
             pltpu.SMEM((rows,), jnp.int32),
             pltpu.SMEM((rows,), jnp.int32),
-            pltpu.SemaphoreType.DMA((3,)),
+            pltpu.SemaphoreType.DMA((4,)),
             pltpu.SemaphoreType.DMA,
-            pltpu.SemaphoreType.DMA((len(partners) * spans,)),
-            pltpu.SemaphoreType.DMA((2,)),
         ],
-        compiler_params=pltpu.CompilerParams(vmem_limit_bytes=VMEM_BYTES),
+        compiler_params=pltpu.CompilerParams(vmem_limit_bytes=2 * SMALL_BYTES),
+        cost_estimate=pl.CostEstimate(
+            flops=ATTEND_FLOPS, bytes_accessed=4 * pool.size, transcendentals=0
+        ),
         name="attend",
-    )(order, lengths, table, adapters, queries, fresh, down, pool, weight)
-
-
-def own_call(order, adapters, mixed, shrink, weight, residual, slots):
-    steps, rows, features = residual.shape
+    )(*(in_hbm(x) for x in (order, lengths, table, adapters, queries, fresh, down, residual, pool)))
+
+
+def message_call(mixed, shrink, weight, partners):
     tensor = lax.axis_size("tensor")
-    out_width = weight.shape[1] // tensor
     spans = tensor // QUAD
-    message = (mixed.shape[0], spans * out_width + LANES)
+    columns = spans * weight.shape[1] // tensor
+    vmem = pl.BlockSpec(memory_space=pltpu.VMEM)
+    return pl.pallas_call(
+        functools.partial(message_kernel, partners=partners),
+        out_shape=pltpu.VMEM((mixed.shape[0], columns + LANES), bf16),
+        in_specs=[vmem] * 3,
+        out_specs=vmem,
+        compiler_params=pltpu.CompilerParams(vmem_limit_bytes=SMALL_BYTES),
+        name="message",
+    )(mixed, shrink, weight)
+
+
+def stay_call(order, lengths, table, pool, rows):
     smem = pl.BlockSpec(memory_space=pltpu.SMEM)
     vmem = pl.BlockSpec(memory_space=pltpu.VMEM)
-    hbm = pl.BlockSpec(memory_space=pl.ANY)
     return pl.pallas_call(
-        own_kernel,
-        out_shape=(
-            jax.ShapeDtypeStruct(message, bf16),
-            jax.ShapeDtypeStruct((steps * rows, features + LANES), bf16),
-            jax.ShapeDtypeStruct((steps * rows, (spans + 1) * steps * rows), bf16),
-            jax.ShapeDtypeStruct((steps * rows, 2 * slots), f32),
-        ),
-        in_specs=[smem] * 2 + [vmem] * 2 + [hbm, vmem],
-        out_specs=(vmem,) * 4,
-        scratch_shapes=[
-            pltpu.VMEM((spans, weight.shape[0], out_width), bf16),
-            pltpu.SemaphoreType.DMA((spans,)),
-        ],
-        compiler_params=pltpu.CompilerParams(vmem_limit_bytes=MIDDLE_BYTES),
-        cost_estimate=pl.CostEstimate(
-            flops=2 * mixed.shape[0] * weight.shape[0] * spans * out_width,
-            bytes_accessed=4 * weight.shape[0] * spans * out_width,
-            transcendentals=0,
-        ),
-        name="own",
-    )(order, adapters, mixed, shrink, weight, residual)
+        stay_kernel,
+        out_shape=jax.ShapeDtypeStruct((rows, table.shape[0]) + pool.shape[1:], bf16),
+        in_specs=[smem] * 3 + [vmem],
+        out_specs=pl.BlockSpec(memory_space=pl.ANY),
+        scratch_shapes=[pltpu.VMEM(pool.shape[1:], bf16), pltpu.SemaphoreType.DMA],
+        compiler_params=pltpu.CompilerParams(vmem_limit_bytes=SMALL_BYTES),
+        cost_estimate=pl.CostEstimate(flops=0, bytes_accessed=2 * pool.size, transcendentals=0),
+        name="stay",
+    )(order, lengths, table, pool)
 
 
 def merge_kernel(*refs, spans):
@@ -458,6 +421,7 @@
         in_specs=[vmem] * (1 + len(messages)),
         out_specs=[vmem] * (2 * spans),
         compiler_params=pltpu.CompilerParams(vmem_limit_bytes=SMALL_BYTES),
+        cost_estimate=pl.CostEstimate(flops=MERGE_FLOPS, bytes_accessed=0, transcendentals=0),
         name="merge",
     )(stream, *messages)
     return pieces[:spans], pieces[spans:]
@@ -540,32 +504,22 @@
     other_up = lax.ppermute(adapter_up_weight, "replica", swap)
 
     table = previous_block_table.T
-    *messages, mixed, shrink, placed, leaving = attend_call(
-        request_order_after,
-        lengths,
-        table,
-        request_adapter_index,
-        queries,
-        fresh,
-        adapter_down_weight,
-        pool,
-        output_weight,
-        (3, 2, 1),
+    integers = (request_order_after, lengths, table, request_adapter_index)
+    mixed, shrink, pool, leaving, stream, mix, slot = attend_call(
+        *integers, queries, fresh, adapter_down_weight, residual, pool
     )
     spans = tensor // QUAD
     landed = []
-    for partner, message in zip((3, 2, 1), messages):
-        pairs = [(t, t ^ partner) for t in range(tensor)]
-        landed.append(lax.ppermute(message, "tensor", pairs))
-    own, stream, mix, slot = own_call(
-        request_order_after,
-        request_adapter_index,
-        mixed,
-        shrink,
-        output_weight,
-        residual,
-        adapter_up_weight.shape[0],
-    )
+    for partners in PARTNERS:
+        message = message_call(mixed, shrink, output_weight, partners)
+        pairs = [
+            (r * tensor + t, r * tensor + (t ^ partners[r]))
+            for r in range(replicas)
+            for t in range(tensor)
+        ]
+        landed.append(lax.ppermute(message, ("replica", "tensor"), pairs))
+    own = message_call(mixed, shrink, output_weight, (0, 0))
+    placed = stay_call(*integers[:3], pool, rows)
     arrived = lax.ppermute(leaving, "replica", swap)
     stays, leaves = merge_call(stream, [own] + landed, spans)
 

time: 31.1 us -> 28.4 us (0.913)
  Pallas kernels: 16.5 us -> 15.2 us
  local copies, waits for them, and re-layouts: 1.55 us -> 0.37 us
    ppermute x3, waiting for transfers between devices: 2.33 us -> 0.38 us  [deliver(): return lax.ppermute(piece, ('replica', 'tensor'), pairs)]
    ppermute x3, waiting for transfers between devices: 1.76 us -> 3.6 us  [shards(): landed.append(lax.ppermute(message, ('replica', 'tensor'), pairs))]
    pallas_call x2 -> x6, Pallas kernels: 13.4 us -> 12.1 us  [the longest x1 6.93 us: attend_call(): pl.pallas_call(attend_kernel, out_shape=(pltpu.VMEM((steps * rows, featur...]
    unnamed x12 -> x16, local copies, waits for them, and re-layouts: 1.55 us -> 0.37 us
    ppermute x1, starting transfers between devices: 0.52 us -> 0.01 us  [shards(): arrived = lax.ppermute(leaving, 'replica', swap)]
    ppermute x1, starting transfers between devices: 0.09 us -> 0.51 us  [shards(): other_up = lax.ppermute(adapter_up_weight, 'replica', swap)]
  transfers between devices with their start and end apart: 8 -> 8, of which waited for: 3 -> 4; matrix products, arithmetic and copies ran while one was open for 0% -> 0% of each run, Pallas kernels for 17% -> 22%
where the time goes in v3:
time: 28.4 us; the launch traced here: 28.3 us
  Pallas kernels  15.2 us (54%)
  starting transfers between devices  7.95 us (28%)
  waiting for transfers between devices  3.98 us (14%)
  between operations  0.75 us (3%)
  local copies, waits for them, and re-layouts  0.37 us (1%)
    pallas_call x1, Pallas kernels, attend_call(): pl.pallas_call(attend_kernel, out_shape=(pltpu.VMEM((steps * rows, featur...  6.93 us
    ppermute x3, starting transfers between devices, shards(): landed.append(lax.ppermute(message, ('replica', 'tensor'), pairs))  4.61 us
    ppermute x3, waiting for transfers between devices, shards(): landed.append(lax.ppermute(message, ('replica', 'tensor'), pairs))  3.6 us
    pallas_call x4, Pallas kernels, message_call(): pl.pallas_call(functools.partial(message_kernel, partners=partners), out_...  3.28 us
    ppermute x3, starting transfers between devices, deliver(): return lax.ppermute(piece, ('replica', 'tensor'), pairs)  2.83 us
    pallas_call x1, Pallas kernels, stay_call(): pl.pallas_call(stay_kernel, out_shape=jax.ShapeDtypeStruct((rows, table.s...  1.94 us
    pallas_call x1, Pallas kernels, arrive_call(): pl.pallas_call(arrive_kernel, out_shape=jax.ShapeDtypeStruct(placed.shape...  1.87 us
    pallas_call x1, Pallas kernels, shards(): pl.pallas_call(finish_kernel, out_shape=jax.ShapeDtypeStruct((steps, rows...  1.13 us
  transfers between devices with their start and end apart: 8, of which 4 were waited for; matrix products, arithmetic and copies ran while one was open for 0% of the time, Pallas kernels for 22%

profile of v3, /device:TPU:0, one launch (start us, length us, event | category | flops | bytes accessed | tf_op | source)
XLA Modules:
  0.0 28.3 jit_solution(3531281637490418879)
XLA Ops:
  0.6 0.0 slice-start
  0.6 0.0 slice-start.1
  0.7 0.0 slice-start.2
  0.7 0.0 slice-start.3
  0.7 6.9 %attend.1 = (bf16[32,1024]{1,0:T(8,128)(2,1)S(1)}, bf16[32,128]{1,0:T(8,128)(2,1)S(1)}, bf16[128,64,256]{2,1,0:T(8,128)(2,1)S(1)}, bf16[8,8,64,256]{3,2,1,0:T(8,...) custom-call(s32[32]{0:T(128)} %order_ref.5, s32[32]{0:T(128)} %lengths_ref.3, ...), custom_call_target="tpu_custom_call" | custom-call | flops 40000000000 | bytes 8388608 | tf_op jit(solution)/shard_map/attend/pallas_call | solution.py:330
  7.6 0.0 slice-done
  7.6 0.0 slice-done.1
  7.6 0.3 %slice-done.3 = s8[4194304]{0:T(1024)(128)(4,1)S(1)} async-done(((s8[16777216]{0:T(1024)(128)(4,1)}), s8[4194304]{0:T(1024)(128)(4,1)S(1)}, s32[]{:S(2)}) %slice-start.3) | async-done | bytes 4194328
  8.0 0.8 %message.5 = bf16[32,2176]{1,0:T(8,128)(2,1)S(1)} custom-call(bf16[32,1024]{1,0:T(8,128)(2,1)S(1)} %get-tuple-element.21.mixed_ref, bf16[32,128]{1,0:T(8,128)(2,1)S(1)} %get-tuple-element.22.shrink_ref, bf16[1024,8192]{1,0:T(8,128)(2,1)S(1)} %bitcast.7), custom_call_target="tpu_custom_call" | custom-call | tf_op jit(solution)/shard_map/message/pallas_call | solution.py:369
  8.8 4.0 %collective-permute-start.2 = (bf16[32,2176]{1,0:T(8,128)(2,1)S(1)}, bf16[32,2176]{1,0:T(8,128)(2,1)S(1)}, u32[]{:S(2)}, u32[]{:S(2)}) collective-permute-start(bf16[32,2176]{1,0:T(8,128)(2,1)S(1)} %message.5), channel_id=1, source_target_pairs={{0,3},{1,2},{2,1},{3,0},{4,7},{5,6},{6,5},{7,4},{8,11},{9,10},{10,... | collective-permute-start | bytes 417800 | tf_op jit(solution)/shard_map/ppermute | solution.py:520
  12.8 0.8 %message.6 = bf16[32,2176]{1,0:T(8,128)(2,1)S(1)} custom-call(bf16[32,1024]{1,0:T(8,128)(2,1)S(1)} %get-tuple-element.21.mixed_ref, bf16[32,128]{1,0:T(8,128)(2,1)S(1)} %get-tuple-element.22.shrink_ref, bf16[1024,8192]{1,0:T(8,128)(2,1)S(1)} %bitcast.7), custom_call_target="tpu_custom_call" | custom-call | tf_op jit(solution)/shard_map/message/pallas_call | solution.py:369
  13.6 0.5 %collective-permute-start.3 = (bf16[32,2176]{1,0:T(8,128)(2,1)S(1)}, bf16[32,2176]{1,0:T(8,128)(2,1)S(1)}, u32[]{:S(2)}, u32[]{:S(2)}) collective-permute-start(bf16[32,2176]{1,0:T(8,128)(2,1)S(1)} %message.6), channel_id=1, source_target_pairs={{0,2},{1,3},{2,0},{3,1},{4,6},{5,7},{6,4},{7,5},{8,9},{9,8},{10,11... | collective-permute-start | bytes 417800 | tf_op jit(solution)/shard_map/ppermute | solution.py:520
  14.1 0.8 %message.7 = bf16[32,2176]{1,0:T(8,128)(2,1)S(1)} custom-call(bf16[32,1024]{1,0:T(8,128)(2,1)S(1)} %get-tuple-element.21.mixed_ref, bf16[32,128]{1,0:T(8,128)(2,1)S(1)} %get-tuple-element.22.shrink_ref, bf16[1024,8192]{1,0:T(8,128)(2,1)S(1)} %bitcast.7), custom_call_target="tpu_custom_call" | custom-call | tf_op jit(solution)/shard_map/message/pallas_call | solution.py:369
  14.9 0.1 collective-permute-start.4
  15.1 0.0 collective-permute-start
  15.1 0.5 %collective-permute-start.1 = (bf16[4,64,1024]{2,1,0:T(8,128)(2,1)S(1)}, bf16[4,64,1024]{2,1,0:T(8,128)(2,1)S(1)}, u32[]{:S(2)}, u32[]{:S(2)}) collective-permute-start(bf16[4,64,1024]{2,1,0:T(8,128)(2,1)S(1)} %copy-done), channel_id=1, source_target_pairs={{0,8},{8,0},{1,9},{9,1},{2,10},{10,2},{3,11},{11,3},{4,12},{12,4},... | collective-permute-start | bytes 1572872 | tf_op jit(solution)/shard_map/ppermute | solution.py:504
  15.6 0.8 %message.4.refs_1_ = bf16[32,2176]{1,0:T(8,128)(2,1)S(1)} custom-call(bf16[32,1024]{1,0:T(8,128)(2,1)S(1)} %get-tuple-element.21.mixed_ref, bf16[32,128]{1,0:T(8,128)(2,1)S(1)} %get-tuple-element.22.shrink_ref, bf16[1024,8192]{1,0:T(8,128)(2,1)S(1)} %bitcast.7), custom_call_target="tpu_custom_call" | custom-call | tf_op jit(solution)/shard_map/message/pallas_call | solution.py:369
  16.4 0.5 %collective-permute-done.2.refs_2_ = bf16[32,2176]{1,0:T(8,128)(2,1)S(1)} collective-permute-done((bf16[32,2176]{1,0:T(8,128)(2,1)S(1)}, bf16[32,2176]{1,0:T(8,128)(2,1)S(1)}, u32[]{:S(2)}, u32[]{:S(2)}) %collective-permute-start.2) | collective-permute-done | bytes 139296 | tf_op jit(solution)/shard_map/ppermute | solution.py:520
  16.8 3.0 %collective-permute-done.3.refs_3_ = bf16[32,2176]{1,0:T(8,128)(2,1)S(1)} collective-permute-done((bf16[32,2176]{1,0:T(8,128)(2,1)S(1)}, bf16[32,2176]{1,0:T(8,128)(2,1)S(1)}, u32[]{:S(2)}, u32[]{:S(2)}) %collective-permute-start.3) | collective-permute-done | bytes 139296 | tf_op jit(solution)/shard_map/ppermute | solution.py:520
  19.8 0.1 collective-permute-done.4.refs_4_
  20.0 0.1 merge.1
  20.1 0.1 collective-permute-start.6
  20.2 2.7 %collective-permute-start.5 = (bf16[16,1152]{1,0:T(8,128)(2,1)S(1)}, bf16[16,1152]{1,0:T(8,128)(2,1)S(1)}, u32[]{:S(2)}, u32[]{:S(2)}) collective-permute-start(bf16[16,1152]{1,0:T(8,128)(2,1)S(1)} %get-tuple-element.24), channel_id=1, source_target_pairs={{0,4},{1,5},{2,6},{3,7},{4,0},{5,1},{6,2},{7,3},{8,12},{9,13},{10,... | collective-permute-start | bytes 110600 | tf_op jit(solution)/shard_map/ppermute | solution.py:532
  22.8 0.1 collective-permute-start.7
  22.9 1.9 %stay.1.placed_in_ref = bf16[16,8,64,256]{3,2,1,0:T(8,128)(2,1)} custom-call(s32[32]{0:T(128)S(1)} %copy-done.2, s32[32]{0:T(128)S(1)} %copy-done.3, s32[8,32]{1,0:T(8,128)S(1)} %bitcast.9, bf16[128,64,256]{2,1,0:T(8,128)(2,1)S(1)} %get-tuple-element.16.pool_v), custom_call_target="tpu_custom_call" | custom-call | bytes 4194304 | tf_op jit(solution)/shard_map/stay/pallas_call | solution.py:382
  24.9 0.0 collective-permute-done.arrived_ref
  24.9 1.9 %arrive.1 = bf16[16,8,64,256]{3,2,1,0:T(8,128)(2,1)} custom-call(s32[32]{0:T(128)S(1)} %copy-done.2, bf16[8,8,64,256]{3,2,1,0:T(8,128)(2,1)S(1)} %collective-permute-done.arrived_ref, bf16[16,8,64,256]{3,2,1,0:T(8,128)(2,1)} %stay.1.placed_in_ref), custom_call_target="tpu_custom_call", output_to_operand_aliasing={{}: (2, {})} | custom-call | bytes 4194304 | tf_op jit(solution)/shard_map/arrive/pallas_call | solution.py:449
  26.8 0.0 collective-permute-done.5.rest_1_
  26.8 0.4 %collective-permute-done.7.rest_3_ = bf16[16,1152]{1,0:T(8,128)(2,1)S(1)} collective-permute-done((bf16[16,1152]{1,0:T(8,128)(2,1)S(1)}, bf16[16,1152]{1,0:T(8,128)(2,1)S(1)}, u32[]{:S(2)}, u32[]{:S(2)}) %collective-permute-start.7) | collective-permute-done | bytes 36896 | tf_op jit(solution)/shard_map/ppermute | solution.py:532
  27.1 0.0 collective-permute-done.6.rest_2_
  27.1 0.0 collective-permute-done.1.other_up_ref
  27.1 1.1 %finish.1 = bf16[2,16,1024]{2,1,0:T(8,128)(2,1)} custom-call(bf16[32,96]{1,0:T(8,128)(2,1)S(1)} %get-tuple-element.18.mix_ref, f32[32,8]{1,0:T(8,128)S(1)} %get-tuple-element.19.slot_ref, bf16[4,64,1024]{2,1,0:T(8,128)(2,1)S(1)} %copy-done, bf16[4,64,1024]{2,1,0:T(8,128)(2,1)S(1)} %collective-permute-done.1.other_up_ref, ...), custom_call_target="tpu_custom_call" | custom-call | tf_op jit(solution)/shard_map/finish/pallas_call | solution.py:539
  (10 shorter events, 0.0 us)
Async XLA Ops:
  0.6 7.0 %slice-start = ((s8[16777216]{0:T(1024)(128)(4,1)}), s8[4194304]{0:T(1024)(128)(4,1)S(1)}, s32[]{:S(2)}) async-start(s8[16777216]{0:T(1024)(128)(4,1)} %bitcast.6), calls=%async_computation | async-start | bytes 8388608
  0.6 7.0 %slice-start.1 = ((s8[16777216]{0:T(1024)(128)(4,1)}), s8[4194304]{0:T(1024)(128)(4,1)S(1)}, s32[]{:S(2)}) async-start(s8[16777216]{0:T(1024)(128)(4,1)} %bitcast.6), calls=%async_computation.1 | async-start | bytes 8388608
  0.7 7.0 %slice-start.2 = ((s8[16777216]{0:T(1024)(128)(4,1)}), s8[4194304]{0:T(1024)(128)(4,1)S(1)}, s32[]{:S(2)}) async-start(s8[16777216]{0:T(1024)(128)(4,1)} %bitcast.6), calls=%async_computation.2 | async-start | bytes 8388608
  0.7 7.3 %slice-start.3 = ((s8[16777216]{0:T(1024)(128)(4,1)}), s8[4194304]{0:T(1024)(128)(4,1)S(1)}, s32[]{:S(2)}) async-start(s8[16777216]{0:T(1024)(128)(4,1)} %bitcast.6), calls=%async_computation.3 | async-start | bytes 8388608
  8.8 8.0 %collective-permute-start.2 = (bf16[32,2176]{1,0:T(8,128)(2,1)S(1)}, bf16[32,2176]{1,0:T(8,128)(2,1)S(1)}, u32[]{:S(2)}, u32[]{:S(2)}) collective-permute-start(bf16[32,2176]{1,0:T(8,128)(2,1)S(1)} %message.5), channel_id=1, source_target_pairs={{0,3},{1,2},{2,1},{3,0},{4,7},{5,6},{6,5},{7,4},{8,11},{9,10},{10,... | collective-permute-start | bytes 417800 | tf_op jit(solution)/shard_map/ppermute | solution.py:520
  13.6 1.4 %copy-start = (bf16[4,64,1024]{2,1,0:T(8,128)(2,1)S(1)}, bf16[4,64,1024]{2,1,0:T(8,128)(2,1)}, u32[]{:S(2)}) copy-start(bf16[4,64,1024]{2,1,0:T(8,128)(2,1)} %up_ref.1) | copy-start | bytes 1572868
  13.6 6.2 %collective-permute-start.3 = (bf16[32,2176]{1,0:T(8,128)(2,1)S(1)}, bf16[32,2176]{1,0:T(8,128)(2,1)S(1)}, u32[]{:S(2)}, u32[]{:S(2)}) collective-permute-start(bf16[32,2176]{1,0:T(8,128)(2,1)S(1)} %message.6), channel_id=1, source_target_pairs={{0,2},{1,3},{2,0},{3,1},{4,6},{5,7},{6,4},{7,5},{8,9},{9,8},{10,11... | collective-permute-start | bytes 417800 | tf_op jit(solution)/shard_map/ppermute | solution.py:520
  14.9 5.1 %collective-permute-start.4 = (bf16[32,2176]{1,0:T(8,128)(2,1)S(1)}, bf16[32,2176]{1,0:T(8,128)(2,1)S(1)}, u32[]{:S(2)}, u32[]{:S(2)}) collective-permute-start(bf16[32,2176]{1,0:T(8,128)(2,1)S(1)} %message.7), channel_id=1, source_target_pairs={{0,1},{1,0},{2,3},{3,2},{4,5},{5,4},{6,7},{7,6},{8,10},{9,11},{10,... | collective-permute-start | bytes 417800 | tf_op jit(solution)/shard_map/ppermute | solution.py:520
  15.1 9.8 %collective-permute-start = (bf16[8,8,64,256]{3,2,1,0:T(8,128)(2,1)S(1)}, bf16[8,8,64,256]{3,2,1,0:T(8,128)(2,1)S(1)}, u32[]{:S(2)}, u32[]{:S(2)}) collective-permute-start(bf16[8,8,64,256]{3,2,1,0:T(8,128)(2,1)S(1)} %get-tuple-element.15), channel_id=1, source_target_pairs={{0,8},{8,0},{1,9},{9,1},{2,10},{10,2},{3,11},{11,3},{4,12},{12,4},... | collective-permute-start | bytes 6291464 | tf_op jit(solution)/shard_map/ppermute | solution.py:523
  15.1 12.1 %collective-permute-start.1 = (bf16[4,64,1024]{2,1,0:T(8,128)(2,1)S(1)}, bf16[4,64,1024]{2,1,0:T(8,128)(2,1)S(1)}, u32[]{:S(2)}, u32[]{:S(2)}) collective-permute-start(bf16[4,64,1024]{2,1,0:T(8,128)(2,1)S(1)} %copy-done), channel_id=1, source_target_pairs={{0,8},{8,0},{1,9},{9,1},{2,10},{10,2},{3,11},{11,3},{4,12},{12,4},... | collective-permute-start | bytes 1572872 | tf_op jit(solution)/shard_map/ppermute | solution.py:504
  20.0 2.9 %copy-start.1 = (s32[32,8]{0,1:T(8,128)S(1)}, s32[32,8]{0,1:T(8,128)}, u32[]{:S(2)}) copy-start(s32[32,8]{0,1:T(8,128)} %param.19) | copy-start | bytes 3076
  20.0 2.9 %copy-start.2 = (s32[32]{0:T(128)S(1)}, s32[32]{0:T(128)}, u32[]{:S(2)}) copy-start(s32[32]{0:T(128)} %order_ref.5) | copy-start | bytes 388
  20.0 2.9 %copy-start.3 = (s32[32]{0:T(128)S(1)}, s32[32]{0:T(128)}, u32[]{:S(2)}) copy-start(s32[32]{0:T(128)} %lengths_ref.3) | copy-start | bytes 388
  20.1 7.1 %collective-permute-start.6 = (bf16[32,1152]{1,0:T(8,128)(2,1)S(1)}, bf16[32,1152]{1,0:T(8,128)(2,1)S(1)}, u32[]{:S(2)}, u32[]{:S(2)}) collective-permute-start(bf16[32,1152]{1,0:T(8,128)(2,1)S(1)} %get-tuple-element.25), channel_id=1, source_target_pairs={{0,8},{1,9},{2,10},{3,11},{4,12},{5,13},{6,14},{7,15},{8,0},{9,1},... | collective-permute-start | bytes 221192 | tf_op jit(solution)/shard_map/ppermute | solution.py:532
  20.2 6.6 %collective-permute-start.5 = (bf16[16,1152]{1,0:T(8,128)(2,1)S(1)}, bf16[16,1152]{1,0:T(8,128)(2,1)S(1)}, u32[]{:S(2)}, u32[]{:S(2)}) collective-permute-start(bf16[16,1152]{1,0:T(8,128)(2,1)S(1)} %get-tuple-element.24), channel_id=1, source_target_pairs={{0,4},{1,5},{2,6},{3,7},{4,0},{5,1},{6,2},{7,3},{8,12},{9,13},{10,... | collective-permute-start | bytes 110600 | tf_op jit(solution)/shard_map/ppermute | solution.py:532
  22.8 4.3 %collective-permute-start.7 = (bf16[16,1152]{1,0:T(8,128)(2,1)S(1)}, bf16[16,1152]{1,0:T(8,128)(2,1)S(1)}, u32[]{:S(2)}, u32[]{:S(2)}) collective-permute-start(bf16[16,1152]{1,0:T(8,128)(2,1)S(1)} %get-tuple-element.26), channel_id=1, source_target_pairs={{0,12},{1,13},{2,14},{3,15},{4,8},{5,9},{6,10},{7,11},{8,4},{9,5},... | collective-permute-start | bytes 110600 | tf_op jit(solution)/shard_map/ppermute | solution.py:532

commit v4 on v3

--- a/solution.py
+++ b/solution.py
@@ -12,8 +12,9 @@
 f32 = jnp.float32
 LANES = 128
 QUAD = 4
-PARTNERS = ((3, 3), (2, 1), (1, 2))
+PARTNERS = ((3, 3), (2, 2), (1, 1))
 ATTEND_FLOPS = 40_000_000_000
+PREPARE_FLOPS = 2_000_000_000
 MERGE_FLOPS = 50_000_000_000
 VMEM_BYTES = 56 * 1024 * 1024
 SMALL_BYTES = 8 * 1024 * 1024
@@ -52,17 +53,6 @@
         return count + hit.astype(jnp.int32)
 
     lax.fori_loop(0, row_count, step, jnp.int32(0))
-
-
-def project(mixed_ref, shrink_ref, weight_ref, message_ref, partner):
-    out_width = weight_ref.shape[1] // lax.axis_size("tensor")
-    spans = message_ref.shape[1] // out_width
-    here = lax.axis_index("tensor")
-    message_ref[:, spans * out_width :] = shrink_ref[...]
-    for span in range(spans):
-        start = pl.multiple_of((here ^ (span * QUAD + partner)) * out_width, out_width)
-        part = dot(mixed_ref[...], weight_ref[:, pl.ds(start, out_width)])
-        message_ref[:, span * out_width : (span + 1) * out_width] = part.astype(bf16)
 
 
 def attend_kernel(
@@ -75,13 +65,9 @@
     down_hbm,
     residual_hbm,
     pool_ref,
-    mixed_ref,
-    shrink_ref,
+    stay_ref,
+    leave_ref,
     pool_v,
-    leaving_ref,
-    stream_ref,
-    mix_ref,
-    slot_ref,
     queries_ref,
     fresh_ref,
     down_ref,
@@ -227,72 +213,107 @@
         [shrink, jnp.zeros((places * steps * half, LANES - rank), f32)], axis=1
     ).astype(bf16)
 
-    mixed_ref[...] = mixed
-    shrink_ref[...] = shrink
-
-    def copy_leaving(index, carry):
-        request = first + found[half + index]
-        length = lengths_ref[request]
-        for b in range(table_blocks):
-
-            @pl.when(b * block_size < length)
-            def _():
-                leaving_ref[index, b] = pool_v[table_ref[b, request]]
-
-            @pl.when(b * block_size >= length)
-            def _():
-                leaving_ref[index, b] = jnp.zeros((block_size, width), bf16)
-
-        return carry
-
-    lax.fori_loop(0, half, copy_leaving, 0)
-
     small_copies[3].wait()
     wanted = step_index * rows + source
     stream = dot(
         one_hot(iota((steps * rows, steps * rows), 1) == wanted),
         residual_ref[...].reshape(steps * rows, features),
-    )
-    stream_ref[:, :features] = stream.astype(bf16)
-    stream_ref[:, features:] = jnp.zeros((steps * rows, LANES), bf16)
-
+    ).astype(bf16)
     group = steps * half
-    landed_blocks = mix_ref.shape[1] // (places * group)
-    out_row = iota((steps * rows, 1), 0)
-    step_of, place_of = div(out_row, rows), mod(out_row, rows)
-    landed_row = jnp.zeros_like(out_row)
-    slot_of = jnp.zeros_like(out_row)
+    for place, ref in enumerate((stay_ref, leave_ref)):
+        span = slice(place * group, (place + 1) * group)
+        ref[:, :features] = mixed[span]
+        ref[:, features : features + LANES] = shrink[span]
+        ref[:, features + LANES :] = stream[span]
+
+
+def prepare_kernel(
+    order_ref,
+    lengths_ref,
+    table_ref,
+    adapter_ref,
+    pool_v,
+    leaving_ref,
+    turn_ref,
+    slot_ref,
+):
+    half, table_blocks, block_size, width = leaving_ref.shape
+    rows = 2 * half
+    group = turn_ref.shape[0] // 2
+    me = lax.axis_index("replica")
+
+    def copy_leaving(j, count):
+        request = order_ref[(1 - me) * rows + j]
+        hit = div(request, rows) == me
+
+        @pl.when(hit)
+        def _():
+            length = lengths_ref[request]
+            for b in range(table_blocks):
+
+                @pl.when(b * block_size < length)
+                def _():
+                    leaving_ref[count, b] = pool_v[table_ref[b, request]]
+
+                @pl.when(b * block_size >= length)
+                def _():
+                    leaving_ref[count, b] = jnp.zeros((block_size, width), bf16)
+
+        return count + hit.astype(jnp.int32)
+
+    lax.fori_loop(0, rows, copy_leaving, jnp.int32(0))
+
+    row = iota((2 * group, 1), 0)
+    step_of, place_of = div(row, rows), mod(row, rows)
+    side_of, rank_of = div(row, group), mod(row, half)
+    wanted = jnp.zeros_like(row)
+    adapter = jnp.zeros_like(row)
     counts = [jnp.int32(0), jnp.int32(0)]
     for j in range(rows):
-        request = order_ref[first + j]
+        request = order_ref[me * rows + j]
         away = jnp.where(div(request, rows) == me, 0, 1)
         count = jnp.where(away == 0, counts[0], counts[1])
         counts = [counts[0] + 1 - away, counts[1] + away]
-        here = place_of == j
-        landed_row = jnp.where(here, away * (landed_blocks * group) + count, landed_row)
-        slot_of = jnp.where(here, away * slots + adapter_ref[request], slot_of)
-    landed_row = landed_row + step_of * half
-    column = iota(mix_ref.shape, 1)
-    kept = column - mod(column, landed_blocks * group) + mod(column, group)
-    mix_ref[...] = one_hot(kept == landed_row)
-    slot_ref[...] = one_hot(iota(slot_ref.shape, 1) == slot_of).astype(f32)
-
-
-def message_kernel(mixed_ref, shrink_ref, weight_ref, message_ref, *, partners):
+        wanted = jnp.where(place_of == j, away * group + count, wanted)
+        here = (side_of == away) & (rank_of == count)
+        adapter = jnp.where(here, adapter_ref[request], adapter)
+    wanted = wanted + step_of * half
+    turn_ref[...] = one_hot(iota(turn_ref.shape, 1) == wanted)
+    slot_ref[...] = one_hot(iota(slot_ref.shape, 1) == adapter).astype(f32)
+
+
+def message_kernel(stay_ref, arrived_ref, weight_ref, message_ref, *, partners):
+    out_width = weight_ref.shape[1] // lax.axis_size("tensor")
+    features = weight_ref.shape[0]
+    spans = message_ref.shape[1] // out_width
+    here = lax.axis_index("tensor")
     partner = jnp.where(lax.axis_index("replica") == 0, partners[0], partners[1])
-    project(mixed_ref, shrink_ref, weight_ref, message_ref, partner)
-
-
-def stay_kernel(order_ref, lengths_ref, table_ref, pool_v, placed_ref, zero_v, sem):
+    mixed = jnp.concatenate([stay_ref[:, :features], arrived_ref[:, :features]], axis=0)
+    group = stay_ref.shape[0]
+    for side, ref in enumerate((stay_ref, arrived_ref)):
+        shrink = ref[:, features : features + LANES].astype(message_ref.dtype)
+        message_ref[side * group : (side + 1) * group, spans * out_width :] = shrink
+    for span in range(spans):
+        start = pl.multiple_of((here ^ (span * QUAD + partner)) * out_width, out_width)
+        part = dot(mixed, weight_ref[:, pl.ds(start, out_width)])
+        message_ref[:, span * out_width : (span + 1) * out_width] = part.astype(message_ref.dtype)
+
+
+def place_kernel(order_ref, lengths_ref, table_ref, pool_v, arrived_ref, placed_ref, zero_v, sem):
     rows, table_blocks, block_size, _ = placed_ref.shape
     me = lax.axis_index("replica")
     zero_v[...] = jnp.zeros_like(zero_v)
 
-    def step(j, carry):
+    def step(j, count):
         request = order_ref[me * rows + j]
         length = lengths_ref[request]
-
-        @pl.when(div(request, rows) == me)
+        stayed = div(request, rows) == me
+
+        @pl.when(jnp.logical_not(stayed))
+        def _():
+            pltpu.make_async_copy(arrived_ref.at[count], placed_ref.at[j], sem).start()
+
+        @pl.when(stayed)
         def _():
             for b in range(table_blocks):
                 target = placed_ref.at[j, b]
@@ -306,11 +327,10 @@
                 def _():
                     pltpu.make_async_copy(zero_v, target, sem).start()
 
-        return carry
-
-    lax.fori_loop(0, rows, step, 0)
-    staying = placed_ref.at[pl.ds(0, rows // 2)]
-    pltpu.make_async_copy(staying, staying, sem).wait()
+        return count + 1 - stayed.astype(jnp.int32)
+
+    lax.fori_loop(0, rows, step, jnp.int32(0))
+    pltpu.make_async_copy(placed_ref, placed_ref, sem).wait()
 
 
 def in_hbm(value):
@@ -323,23 +343,18 @@
     table_blocks = table.shape[0]
     positions = table_blocks * block_size
     score_rows = rows * steps * features // (width // 2)
-    spans = lax.axis_size("tensor") // QUAD
     smem = pl.BlockSpec(memory_space=pltpu.SMEM)
     vmem = pl.BlockSpec(memory_space=pltpu.VMEM)
     hbm = pl.BlockSpec(memory_space=pl.ANY)
     return pl.pallas_call(
         attend_kernel,
         out_shape=(
-            pltpu.VMEM((steps * rows, features), bf16),
-            pltpu.VMEM((steps * rows, LANES), bf16),
+            pltpu.VMEM((steps * rows // 2, 2 * features + LANES), bf16),
+            pltpu.VMEM((steps * rows // 2, 2 * features + LANES), bf16),
             pltpu.VMEM(pool.shape, bf16),
-            pltpu.VMEM((rows // 2, table_blocks, block_size, width), bf16),
-            pltpu.VMEM((steps * rows, features + LANES), bf16),
-            pltpu.VMEM((steps * rows, (spans + 1) * steps * rows), bf16),
-            pltpu.VMEM((steps * rows, 2 * down.shape[0]), f32),
         ),
         in_specs=[smem] * 4 + [hbm] * 5,
-        out_specs=(vmem,) * 7,
+        out_specs=(vmem,) * 3,
         scratch_shapes=[
             pltpu.VMEM(queries.shape, bf16),
             pltpu.VMEM(fresh.shape, bf16),
@@ -361,123 +376,101 @@
     )(*(in_hbm(x) for x in (order, lengths, table, adapters, queries, fresh, down, residual, pool)))
 
 
-def message_call(mixed, shrink, weight, partners):
+def prepare_call(order, lengths, table, adapters, pool, steps, rows, slots):
+    smem = pl.BlockSpec(memory_space=pltpu.SMEM)
+    vmem = pl.BlockSpec(memory_space=pltpu.VMEM)
+    return pl.pallas_call(
+        prepare_kernel,
+        out_shape=(
+            pltpu.VMEM((rows // 2, table.shape[0]) + pool.shape[1:], bf16),
+            pltpu.VMEM((steps * rows, steps * rows), bf16),
+            pltpu.VMEM((steps * rows, slots), f32),
+        ),
+        in_specs=[smem] * 4 + [vmem],
+        out_specs=(vmem,) * 3,
+        compiler_params=pltpu.CompilerParams(vmem_limit_bytes=SMALL_BYTES),
+        cost_estimate=pl.CostEstimate(flops=PREPARE_FLOPS, bytes_accessed=0, transcendentals=0),
+        name="prepare",
+    )(order, lengths, table, adapters, pool)
+
+
+def message_call(stay, arrived, weight, partners, dtype):
     tensor = lax.axis_size("tensor")
     spans = tensor // QUAD
     columns = spans * weight.shape[1] // tensor
     vmem = pl.BlockSpec(memory_space=pltpu.VMEM)
     return pl.pallas_call(
         functools.partial(message_kernel, partners=partners),
-        out_shape=pltpu.VMEM((mixed.shape[0], columns + LANES), bf16),
+        out_shape=pltpu.VMEM((2 * stay.shape[0], columns + LANES), dtype),
         in_specs=[vmem] * 3,
         out_specs=vmem,
         compiler_params=pltpu.CompilerParams(vmem_limit_bytes=SMALL_BYTES),
         name="message",
-    )(mixed, shrink, weight)
-
-
-def stay_call(order, lengths, table, pool, rows):
+    )(stay, arrived, weight)
+
+
+def place_call(order, lengths, table, pool, arrived, rows):
     smem = pl.BlockSpec(memory_space=pltpu.SMEM)
     vmem = pl.BlockSpec(memory_space=pltpu.VMEM)
     return pl.pallas_call(
-        stay_kernel,
+        place_kernel,
         out_shape=jax.ShapeDtypeStruct((rows, table.shape[0]) + pool.shape[1:], bf16),
-        in_specs=[smem] * 3 + [vmem],
+        in_specs=[smem] * 3 + [vmem] * 2,
         out_specs=pl.BlockSpec(memory_space=pl.ANY),
         scratch_shapes=[pltpu.VMEM(pool.shape[1:], bf16), pltpu.SemaphoreType.DMA],
         compiler_params=pltpu.CompilerParams(vmem_limit_bytes=SMALL_BYTES),
         cost_estimate=pl.CostEstimate(flops=0, bytes_accessed=2 * pool.size, transcendentals=0),
-        name="stay",
-    )(order, lengths, table, pool)
+        name="place",
+    )(order, lengths, table, pool, arrived)
 
 
 def merge_kernel(*refs, spans):
-    stream_ref, messages, outs = refs[0], refs[1 : -2 * spans], refs[-2 * spans :]
-    total = messages[0][...].astype(f32)
+    messages, outs = refs[:-spans], refs[-spans:]
+    total = messages[0][...]
     for ref in messages[1:]:
         total = total + ref[...].astype(f32)
-    total = total.astype(bf16)
-    group = total.shape[0] // 2
     out_width = (total.shape[1] - LANES) // spans
-    for side in range(2):
-        span = slice(side * group, (side + 1) * group)
-        for n in range(spans):
-            ref = outs[side * spans + n]
-            ref[:group, :out_width] = total[span, n * out_width : (n + 1) * out_width]
-            ref[:group, out_width:] = total[span, spans * out_width :]
-        outs[side * spans][group:] = stream_ref[span, :]
-
-
-def merge_call(stream, messages, spans):
+    for n, ref in enumerate(outs):
+        ref[:, :out_width] = total[:, n * out_width : (n + 1) * out_width].astype(ref.dtype)
+        ref[:, out_width:] = total[:, spans * out_width :].astype(ref.dtype)
+
+
+def merge_call(messages, spans):
     rows, columns = messages[0].shape
     vmem = pl.BlockSpec(memory_space=pltpu.VMEM)
     width = (columns - LANES) // spans + LANES
-    pieces = [
-        jax.ShapeDtypeStruct((rows if n == 0 else rows // 2, width), bf16) for n in range(spans)
-    ]
-    pieces = pl.pallas_call(
+    return pl.pallas_call(
         functools.partial(merge_kernel, spans=spans),
-        out_shape=pieces * 2,
-        in_specs=[vmem] * (1 + len(messages)),
-        out_specs=[vmem] * (2 * spans),
+        out_shape=[pltpu.VMEM((rows, width), f32 if n == 0 else bf16) for n in range(spans)],
+        in_specs=[vmem] * len(messages),
+        out_specs=[vmem] * spans,
         compiler_params=pltpu.CompilerParams(vmem_limit_bytes=SMALL_BYTES),
         cost_estimate=pl.CostEstimate(flops=MERGE_FLOPS, bytes_accessed=0, transcendentals=0),
         name="merge",
-    )(stream, *messages)
-    return pieces[:spans], pieces[spans:]
-
-
-def arrive_kernel(order_ref, arrived_ref, placed_in_ref, placed_ref, sem):
-    rows = placed_ref.shape[0]
-    me = lax.axis_index("replica")
-
-    def step(j, count):
-        hit = div(order_ref[me * rows + j], rows) != me
-
-        @pl.when(hit)
-        def _():
-            pltpu.make_async_copy(arrived_ref.at[count], placed_ref.at[j], sem).start()
-
-        return count + hit.astype(jnp.int32)
-
-    lax.fori_loop(0, rows, step, jnp.int32(0))
-    pltpu.make_async_copy(arrived_ref, arrived_ref, sem).wait()
-
-
-def arrive_call(order, arrived, placed):
-    hbm = pl.BlockSpec(memory_space=pl.ANY)
-    return pl.pallas_call(
-        arrive_kernel,
-        out_shape=jax.ShapeDtypeStruct(placed.shape, bf16),
-        in_specs=[
-            pl.BlockSpec(memory_space=pltpu.SMEM),
-            pl.BlockSpec(memory_space=pltpu.VMEM),
-            hbm,
-        ],
-        out_specs=hbm,
-        scratch_shapes=[pltpu.SemaphoreType.DMA],
-        input_output_aliases={2: 0},
-        compiler_params=pltpu.CompilerParams(vmem_limit_bytes=SMALL_BYTES),
-        cost_estimate=pl.CostEstimate(
-            flops=0, bytes_accessed=4 * arrived.size, transcendentals=0
-        ),
-        name="arrive",
-    )(order, arrived, placed)
-
-
-def finish_kernel(mix_ref, slot_ref, up_ref, other_up_ref, *rest):
-    landed_refs, out_ref = rest[:-1], rest[-1]
+    )(*messages)
+
+
+def finish_kernel(
+    turn_ref, slot_ref, up_ref, other_up_ref, stay_ref, arrived_ref, home_ref, *rest
+):
+    across_refs, out_ref = rest[:-1], rest[-1]
     slots, rank, features = up_ref.shape
-    sums = dot(mix_ref[...], jnp.concatenate([ref[...] for ref in landed_refs], axis=0))
-    shrink = sums[:, features : features + rank].astype(bf16).astype(f32)
-    result = sums[:, :features]
-    for side, up in enumerate((up_ref, other_up_ref)):
-        wide = jnp.concatenate(
-            [shrink * slot_ref[:, side * slots + n : side * slots + n + 1] for n in range(slots)],
-            axis=1,
-        ).astype(bf16)
-        result = result + adapter_scale * dot(wide, up[...].reshape(slots * rank, features))
-    out_ref[...] = result.astype(bf16).reshape(out_ref.shape)
+    group = stay_ref.shape[0]
+    total = home_ref[...]
+    for ref in across_refs:
+        total = total + ref[...].astype(f32)
+    shrink = total[:, features : features + rank].astype(bf16).astype(f32)
+    wide = jnp.concatenate(
+        [shrink * slot_ref[:, n : n + 1] for n in range(slots)], axis=1
+    ).astype(bf16)
+    finished = []
+    for side, (up, stream) in enumerate(((up_ref, stay_ref), (other_up_ref, arrived_ref))):
+        span = slice(side * group, (side + 1) * group)
+        raised = dot(wide[span], up[...].reshape(slots * rank, features))
+        residual = stream[:, features + LANES :].astype(f32)
+        finished.append(residual + total[span, :features] + adapter_scale * raised)
+    finished = jnp.concatenate(finished, axis=0).astype(bf16)
+    out_ref[...] = dot(turn_ref[...], finished).astype(bf16).reshape(out_ref.shape)
 
 
 def shards(
@@ -505,45 +498,38 @@
 
     table = previous_block_table.T
     integers = (request_order_after, lengths, table, request_adapter_index)
-    mixed, shrink, pool, leaving, stream, mix, slot = attend_call(
+    stay, leave, pool = attend_call(
         *integers, queries, fresh, adapter_down_weight, residual, pool
     )
+    came = lax.ppermute(leave, "replica", swap)
+    leaving, turn, slot = prepare_call(*integers, pool, steps, rows, adapter_up_weight.shape[0])
     spans = tensor // QUAD
-    landed = []
-    for partners in PARTNERS:
-        message = message_call(mixed, shrink, output_weight, partners)
+
+    def trade(message, partners):
         pairs = [
             (r * tensor + t, r * tensor + (t ^ partners[r]))
             for r in range(replicas)
             for t in range(tensor)
         ]
-        landed.append(lax.ppermute(message, ("replica", "tensor"), pairs))
-    own = message_call(mixed, shrink, output_weight, (0, 0))
-    placed = stay_call(*integers[:3], pool, rows)
+        return lax.ppermute(message, ("replica", "tensor"), pairs)
+
+    message = functools.partial(message_call, stay, came, output_weight)
+    landed = [trade(message(partners, bf16), partners) for partners in PARTNERS]
+    own = message((0, 0), f32)
     arrived = lax.ppermute(leaving, "replica", swap)
-    stays, leaves = merge_call(stream, [own] + landed, spans)
-
-    def deliver(piece, span, away):
-        pairs = [
-            (r * tensor + t, (r ^ away) * tensor + (t ^ (span * QUAD)))
-            for r in range(replicas)
-            for t in range(tensor)
-        ]
-        return lax.ppermute(piece, ("replica", "tensor"), pairs)
-
-    stays = [stays[0]] + [deliver(stays[n], n, 0) for n in range(1, spans)]
-    leaves = [deliver(leaves[n], n, 1) for n in reversed(range(spans))][::-1]
-    placed_cache = arrive_call(request_order_after, arrived, placed)
-    placed_cache, mix = lax.optimization_barrier((placed_cache, mix))
+    home, *across = merge_call([own] + landed, spans)
+    across = [trade(piece, (n * QUAD, n * QUAD)) for n, piece in enumerate(across, 1)]
+    placed_cache = place_call(*integers[:3], pool, arrived, rows)
+    placed_cache, turn = lax.optimization_barrier((placed_cache, turn))
     vmem = pl.BlockSpec(memory_space=pltpu.VMEM)
     layer_out = pl.pallas_call(
         finish_kernel,
         out_shape=jax.ShapeDtypeStruct((steps, rows, features), bf16),
-        in_specs=[vmem] * (4 + 2 * spans),
+        in_specs=[vmem] * (7 + len(across)),
         out_specs=vmem,
         compiler_params=pltpu.CompilerParams(vmem_limit_bytes=SMALL_BYTES),
         name="finish",
-    )(mix, slot, adapter_up_weight, other_up, *stays, *leaves)
+    )(turn, slot, adapter_up_weight, other_up, stay, came, home, *across)
     return (layer_out, placed_cache.reshape(rows, table_blocks, 1, block_size, width))
 
 

time: 28.4 us -> 27 us (0.951)
  waiting for transfers between devices: 3.98 us -> 2.69 us
  starting transfers between devices: 7.95 us -> 8.48 us
  Pallas kernels: 15.2 us -> 14.8 us
  local copies, waits for them, and re-layouts: 0.37 us -> 0.05 us
    ppermute x6 -> x5, waiting for transfers between devices: 3.98 us -> 2.69 us  [the longest x4 1.78 us: trade(): return lax.ppermute(message, ('replica', 'tensor'), pairs)]
    ppermute x6 -> x5, starting transfers between devices: 7.44 us -> 7.92 us  [the longest x4 7.39 us: trade(): return lax.ppermute(message, ('replica', 'tensor'), pairs)]
    pallas_call x4, Pallas kernels: 10.8 us -> 10.5 us  [the longest x1 5.91 us: attend_call(): pl.pallas_call(attend_kernel, out_shape=(pltpu.VMEM((steps * rows // 2, 2...]
    unnamed x16 -> x18, local copies, waits for them, and re-layouts: 0.37 us -> 0.05 us
  transfers between devices with their start and end apart: 8 -> 7, of which waited for: 4 -> 3; matrix products, arithmetic and copies ran while one was open for 0% -> 0% of each run, Pallas kernels for 22% -> 26%
where the time goes in v4:
time: 27 us; the launch traced here: 26.8 us
  Pallas kernels  14.8 us (55%)
  starting transfers between devices  8.48 us (31%)
  waiting for transfers between devices  2.69 us (10%)
  between operations  0.77 us (3%)
    ppermute x4, starting transfers between devices, trade(): return lax.ppermute(message, ('replica', 'tensor'), pairs)  7.39 us
    pallas_call x1, Pallas kernels, attend_call(): pl.pallas_call(attend_kernel, out_shape=(pltpu.VMEM((steps * rows // 2, 2...  5.91 us
    pallas_call x4, Pallas kernels, message_call(): pl.pallas_call(functools.partial(message_kernel, partners=partners), out_...  3.26 us
    pallas_call x1, Pallas kernels, place_call(): pl.pallas_call(place_kernel, out_shape=jax.ShapeDtypeStruct((rows, table....  2.6 us
    pallas_call x1, Pallas kernels, prepare_call(): pl.pallas_call(prepare_kernel, out_shape=(pltpu.VMEM((rows // 2, table.sh...  1.87 us
    ppermute x4, waiting for transfers between devices, trade(): return lax.ppermute(message, ('replica', 'tensor'), pairs)  1.78 us
    pallas_call x1, Pallas kernels, shards(): pl.pallas_call(finish_kernel, out_shape=jax.ShapeDtypeStruct((steps, rows...  1.12 us
    ppermute x1, waiting for transfers between devices, shards(): came = lax.ppermute(leave, 'replica', swap)  0.91 us
  transfers between devices with their start and end apart: 7, of which 3 were waited for; matrix products, arithmetic and copies ran while one was open for 0% of the time, Pallas kernels for 26%

profile of v4, /device:TPU:0, one launch (start us, length us, event | category | flops | bytes accessed | tf_op | source)
XLA Modules:
  0.0 26.8 jit_solution(16078987298215261153)
XLA Ops:
  0.6 0.0 slice-start
  0.6 0.0 slice-start.1
  0.7 0.0 slice-start.2
  0.7 0.0 slice-start.3
  0.7 5.9 %attend.1 = (bf16[16,2176]{1,0:T(8,128)(2,1)S(1)}, bf16[16,2176]{1,0:T(8,128)(2,1)S(1)}, bf16[128,64,256]{2,1,0:T(8,128)(2,1)S(1)}) custom-call(s32[32]{0:T(128)} %order_ref.5, s32[32]{0:T(128)} %lengths_ref.5, s32[8,32]{1,0:T(8,128)} %bitcast.8, s32[32]{0:T(128)} %adapter_ref.3, bf16[2,16,1024]{2,1,0:T(8,128)(2,1)} %queries_hbm.1, ...), custom_call_target="tpu_custom_call" | custom-call | flops 40000000000 | bytes 8388608 | tf_op jit(solution)/shard_map/attend/pallas_call | solution.py:349
  6.6 0.5 %collective-permute-start.2 = (bf16[16,2176]{1,0:T(8,128)(2,1)S(1)}, bf16[16,2176]{1,0:T(8,128)(2,1)S(1)}, u32[]{:S(2)}, u32[]{:S(2)}) collective-permute-start(bf16[16,2176]{1,0:T(8,128)(2,1)S(1)} %get-tuple-element.18), channel_id=1, source_target_pairs={{0,8},{8,0},{1,9},{9,1},{2,10},{10,2},{3,11},{11,3},{4,12},{12,4},... | collective-permute-start | bytes 208904 | tf_op jit(solution)/shard_map/ppermute | solution.py:504
  7.1 0.9 %collective-permute-done.2.arrived_ref = bf16[16,2176]{1,0:T(8,128)(2,1)S(1)} collective-permute-done((bf16[16,2176]{1,0:T(8,128)(2,1)S(1)}, bf16[16,2176]{1,0:T(8,128)(2,1)S(1)}, u32[]{:S(2)}, u32[]{:S(2)}) %collective-permute-start.2) | collective-permute-done | bytes 69664 | tf_op jit(solution)/shard_map/ppermute | solution.py:504
  8.0 0.0 slice-done
  8.1 0.8 %message.5 = bf16[32,2176]{1,0:T(8,128)(2,1)S(1)} custom-call(bf16[16,2176]{1,0:T(8,128)(2,1)S(1)} %get-tuple-element.17.stay_ref, bf16[16,2176]{1,0:T(8,128)(2,1)S(1)} %collective-permute-done.2.arrived_ref, bf16[1024,8192]{1,0:T(8,128)(2,1)S(1)} %bitcast.7), custom_call_target="tpu_custom_call" | custom-call | tf_op jit(solution)/shard_map/message/pallas_call | solution.py:402
  8.9 3.9 %collective-permute-start.3 = (bf16[32,2176]{1,0:T(8,128)(2,1)S(1)}, bf16[32,2176]{1,0:T(8,128)(2,1)S(1)}, u32[]{:S(2)}, u32[]{:S(2)}) collective-permute-start(bf16[32,2176]{1,0:T(8,128)(2,1)S(1)} %message.5), channel_id=1, source_target_pairs={{0,3},{1,2},{2,1},{3,0},{4,7},{5,6},{6,5},{7,4},{8,11},{9,10},{10,... | collective-permute-start | bytes 417800 | tf_op jit(solution)/shard_map/ppermute | solution.py:514
  12.8 0.8 %message.6 = bf16[32,2176]{1,0:T(8,128)(2,1)S(1)} custom-call(bf16[16,2176]{1,0:T(8,128)(2,1)S(1)} %get-tuple-element.17.stay_ref, bf16[16,2176]{1,0:T(8,128)(2,1)S(1)} %collective-permute-done.2.arrived_ref, bf16[1024,8192]{1,0:T(8,128)(2,1)S(1)} %bitcast.7), custom_call_target="tpu_custom_call" | custom-call | tf_op jit(solution)/shard_map/message/pallas_call | solution.py:402
  13.6 0.0 copy-start.2
  13.6 0.0 copy-start.3
  13.6 0.0 copy-start.4
  13.6 0.5 %collective-permute-start.4 = (bf16[32,2176]{1,0:T(8,128)(2,1)S(1)}, bf16[32,2176]{1,0:T(8,128)(2,1)S(1)}, u32[]{:S(2)}, u32[]{:S(2)}) collective-permute-start(bf16[32,2176]{1,0:T(8,128)(2,1)S(1)} %message.6), channel_id=1, source_target_pairs={{0,2},{1,3},{2,0},{3,1},{4,6},{5,7},{6,4},{7,5},{8,10},{9,11},{10,... | collective-permute-start | bytes 417800 | tf_op jit(solution)/shard_map/ppermute | solution.py:514
  14.2 0.8 %message.7 = bf16[32,2176]{1,0:T(8,128)(2,1)S(1)} custom-call(bf16[16,2176]{1,0:T(8,128)(2,1)S(1)} %get-tuple-element.17.stay_ref, bf16[16,2176]{1,0:T(8,128)(2,1)S(1)} %collective-permute-done.2.arrived_ref, bf16[1024,8192]{1,0:T(8,128)(2,1)S(1)} %bitcast.7), custom_call_target="tpu_custom_call" | custom-call | tf_op jit(solution)/shard_map/message/pallas_call | solution.py:402
  15.0 0.1 collective-permute-start.5
  15.1 0.0 copy-done.3
  15.1 1.9 %prepare.1 = (bf16[8,8,64,256]{3,2,1,0:T(8,128)(2,1)S(1)}, bf16[32,32]{1,0:T(8,128)(2,1)S(1)}, f32[32,4]{1,0:T(8,128)S(1)}) custom-call(s32[32]{0:T(128)S(1)} %copy-done.2, s32[32]{0:T(128)S(1)} %copy-done.3, s32[8,32]{1,0:T(8,128)S(1)} %bitcast.9, s32[32]{0:T(128)S(1)} %copy-done.4, bf16[128,64,256]{2,1,0:T(8,128)(2,1)S(1)} %get-tuple-element.12.pool_v), custom_call_target="tpu_custom_call" | custom-call | flops 2000000000 | tf_op jit(solution)/shard_map/prepare/pallas_call | solution.py:382
  17.0 0.1 collective-permute-start
  17.1 0.5 %collective-permute-start.1 = (bf16[4,64,1024]{2,1,0:T(8,128)(2,1)S(1)}, bf16[4,64,1024]{2,1,0:T(8,128)(2,1)S(1)}, u32[]{:S(2)}, u32[]{:S(2)}) collective-permute-start(bf16[4,64,1024]{2,1,0:T(8,128)(2,1)S(1)} %copy-done), channel_id=1, source_target_pairs={{0,8},{8,0},{1,9},{9,1},{2,10},{10,2},{3,11},{11,3},{4,12},{12,4},... | collective-permute-start | bytes 1572872 | tf_op jit(solution)/shard_map/ppermute | solution.py:497
  17.6 0.8 %message.4.refs_0_ = f32[32,2176]{1,0:T(8,128)S(1)} custom-call(bf16[16,2176]{1,0:T(8,128)(2,1)S(1)} %get-tuple-element.17.stay_ref, bf16[16,2176]{1,0:T(8,128)(2,1)S(1)} %collective-permute-done.2.arrived_ref, bf16[1024,8192]{1,0:T(8,128)(2,1)S(1)} %bitcast.7), custom_call_target="tpu_custom_call" | custom-call | tf_op jit(solution)/shard_map/message/pallas_call | solution.py:402
  18.4 0.0 collective-permute-done.3.refs_1_
  18.4 1.5 %collective-permute-done.4.refs_2_ = bf16[32,2176]{1,0:T(8,128)(2,1)S(1)} collective-permute-done((bf16[32,2176]{1,0:T(8,128)(2,1)S(1)}, bf16[32,2176]{1,0:T(8,128)(2,1)S(1)}, u32[]{:S(2)}, u32[]{:S(2)}) %collective-permute-start.4) | collective-permute-done | bytes 139296 | tf_op jit(solution)/shard_map/ppermute | solution.py:514
  19.9 0.3 %collective-permute-done.5.refs_3_ = bf16[32,2176]{1,0:T(8,128)(2,1)S(1)} collective-permute-done((bf16[32,2176]{1,0:T(8,128)(2,1)S(1)}, bf16[32,2176]{1,0:T(8,128)(2,1)S(1)}, u32[]{:S(2)}, u32[]{:S(2)}) %collective-permute-start.5) | collective-permute-done | bytes 139296 | tf_op jit(solution)/shard_map/ppermute | solution.py:514
  20.2 0.1 merge.1
  20.3 2.8 %collective-permute-start.6 = (bf16[32,1152]{1,0:T(8,128)(2,1)S(1)}, bf16[32,1152]{1,0:T(8,128)(2,1)S(1)}, u32[]{:S(2)}, u32[]{:S(2)}) collective-permute-start(bf16[32,1152]{1,0:T(8,128)(2,1)S(1)} %get-tuple-element.20), channel_id=1, source_target_pairs={{0,4},{1,5},{2,6},{3,7},{4,0},{5,1},{6,2},{7,3},{8,12},{9,13},{10,... | collective-permute-start | bytes 221192 | tf_op jit(solution)/shard_map/ppermute | solution.py:514
  23.1 0.0 collective-permute-done.arrived_ref
  23.1 2.6 %place.1 = bf16[16,8,64,256]{3,2,1,0:T(8,128)(2,1)} custom-call(s32[32]{0:T(128)S(1)} %copy-done.2, s32[32]{0:T(128)S(1)} %copy-done.3, s32[8,32]{1,0:T(8,128)S(1)} %bitcast.10, bf16[128,64,256]{2,1,0:T(8,128)(2,1)S(1)} %get-tuple-element.12.pool_v, bf16[8,8,64,256]{3,2,1,0:T(8,128)(2,1)S(1)} %collective-permute-done.arrived_ref), custom_call_target="tpu_custom_call" | custom-call | bytes 4194304 | tf_op jit(solution)/shard_map/place/pallas_call | solution.py:415
  25.7 0.0 collective-permute-done.6.rest_0_
  25.7 0.0 collective-permute-done.1.other_up_ref
  25.7 1.1 %finish.1 = bf16[2,16,1024]{2,1,0:T(8,128)(2,1)} custom-call(bf16[32,32]{1,0:T(8,128)(2,1)S(1)} %get-tuple-element.15.turn_ref, f32[32,4]{1,0:T(8,128)S(1)} %get-tuple-element.16.slot_ref, bf16[4,64,1024]{2,1,0:T(8,128)(2,1)S(1)} %copy-done, bf16[4,64,1024]{2,1,0:T(8,128)(2,1)S(1)} %collective-permute-done.1.other_up_ref, ...), custom_call_target="tpu_custom_call" | custom-call | tf_op jit(solution)/shard_map/finish/pallas_call | solution.py:525
  (10 shorter events, 0.0 us)
Async XLA Ops:
  0.6 7.4 %slice-start = ((s8[16777216]{0:T(1024)(128)(4,1)}), s8[4194304]{0:T(1024)(128)(4,1)S(1)}, s32[]{:S(2)}) async-start(s8[16777216]{0:T(1024)(128)(4,1)} %bitcast.6), calls=%async_computation | async-start | bytes 8388608
  0.6 7.4 %slice-start.1 = ((s8[16777216]{0:T(1024)(128)(4,1)}), s8[4194304]{0:T(1024)(128)(4,1)S(1)}, s32[]{:S(2)}) async-start(s8[16777216]{0:T(1024)(128)(4,1)} %bitcast.6), calls=%async_computation.1 | async-start | bytes 8388608
  0.7 7.4 %slice-start.2 = ((s8[16777216]{0:T(1024)(128)(4,1)}), s8[4194304]{0:T(1024)(128)(4,1)S(1)}, s32[]{:S(2)}) async-start(s8[16777216]{0:T(1024)(128)(4,1)} %bitcast.6), calls=%async_computation.2 | async-start | bytes 8388608
  0.7 7.4 %slice-start.3 = ((s8[16777216]{0:T(1024)(128)(4,1)}), s8[4194304]{0:T(1024)(128)(4,1)S(1)}, s32[]{:S(2)}) async-start(s8[16777216]{0:T(1024)(128)(4,1)} %bitcast.6), calls=%async_computation.3 | async-start | bytes 8388608
  6.6 1.4 %collective-permute-start.2 = (bf16[16,2176]{1,0:T(8,128)(2,1)S(1)}, bf16[16,2176]{1,0:T(8,128)(2,1)S(1)}, u32[]{:S(2)}, u32[]{:S(2)}) collective-permute-start(bf16[16,2176]{1,0:T(8,128)(2,1)S(1)} %get-tuple-element.18), channel_id=1, source_target_pairs={{0,8},{8,0},{1,9},{9,1},{2,10},{10,2},{3,11},{11,3},{4,12},{12,4},... | collective-permute-start | bytes 208904 | tf_op jit(solution)/shard_map/ppermute | solution.py:504
  8.9 9.5 %collective-permute-start.3 = (bf16[32,2176]{1,0:T(8,128)(2,1)S(1)}, bf16[32,2176]{1,0:T(8,128)(2,1)S(1)}, u32[]{:S(2)}, u32[]{:S(2)}) collective-permute-start(bf16[32,2176]{1,0:T(8,128)(2,1)S(1)} %message.5), channel_id=1, source_target_pairs={{0,3},{1,2},{2,1},{3,0},{4,7},{5,6},{6,5},{7,4},{8,11},{9,10},{10,... | collective-permute-start | bytes 417800 | tf_op jit(solution)/shard_map/ppermute | solution.py:514
  13.6 1.5 %copy-start.1 = (s32[32,8]{0,1:T(8,128)S(1)}, s32[32,8]{0,1:T(8,128)}, u32[]{:S(2)}) copy-start(s32[32,8]{0,1:T(8,128)} %param.19) | copy-start | bytes 3076
  13.6 1.5 %copy-start.2 = (s32[32]{0:T(128)S(1)}, s32[32]{0:T(128)}, u32[]{:S(2)}) copy-start(s32[32]{0:T(128)} %order_ref.5) | copy-start | bytes 388
  13.6 1.5 %copy-start.3 = (s32[32]{0:T(128)S(1)}, s32[32]{0:T(128)}, u32[]{:S(2)}) copy-start(s32[32]{0:T(128)} %lengths_ref.5) | copy-start | bytes 388
  13.6 1.5 %copy-start.4 = (s32[32]{0:T(128)S(1)}, s32[32]{0:T(128)}, u32[]{:S(2)}) copy-start(s32[32]{0:T(128)} %adapter_ref.3) | copy-start | bytes 388
  13.6 6.3 %collective-permute-start.4 = (bf16[32,2176]{1,0:T(8,128)(2,1)S(1)}, bf16[32,2176]{1,0:T(8,128)(2,1)S(1)}, u32[]{:S(2)}, u32[]{:S(2)}) collective-permute-start(bf16[32,2176]{1,0:T(8,128)(2,1)S(1)} %message.6), channel_id=1, source_target_pairs={{0,2},{1,3},{2,0},{3,1},{4,6},{5,7},{6,4},{7,5},{8,10},{9,11},{10,... | collective-permute-start | bytes 417800 | tf_op jit(solution)/shard_map/ppermute | solution.py:514
  15.0 2.1 %copy-start = (bf16[4,64,1024]{2,1,0:T(8,128)(2,1)S(1)}, bf16[4,64,1024]{2,1,0:T(8,128)(2,1)}, u32[]{:S(2)}) copy-start(bf16[4,64,1024]{2,1,0:T(8,128)(2,1)} %up_ref.1) | copy-start | bytes 1572868
  15.0 5.2 %collective-permute-start.5 = (bf16[32,2176]{1,0:T(8,128)(2,1)S(1)}, bf16[32,2176]{1,0:T(8,128)(2,1)S(1)}, u32[]{:S(2)}, u32[]{:S(2)}) collective-permute-start(bf16[32,2176]{1,0:T(8,128)(2,1)S(1)} %message.7), channel_id=1, source_target_pairs={{0,1},{1,0},{2,3},{3,2},{4,5},{5,4},{6,7},{7,6},{8,9},{9,8},{10,11... | collective-permute-start | bytes 417800 | tf_op jit(solution)/shard_map/ppermute | solution.py:514
  17.0 6.1 %collective-permute-start = (bf16[8,8,64,256]{3,2,1,0:T(8,128)(2,1)S(1)}, bf16[8,8,64,256]{3,2,1,0:T(8,128)(2,1)S(1)}, u32[]{:S(2)}, u32[]{:S(2)}) collective-permute-start(bf16[8,8,64,256]{3,2,1,0:T(8,128)(2,1)S(1)} %get-tuple-element.13), channel_id=1, source_target_pairs={{0,8},{8,0},{1,9},{9,1},{2,10},{10,2},{3,11},{11,3},{4,12},{12,4},... | collective-permute-start | bytes 6291464 | tf_op jit(solution)/shard_map/ppermute | solution.py:519
  17.1 8.6 %collective-permute-start.1 = (bf16[4,64,1024]{2,1,0:T(8,128)(2,1)S(1)}, bf16[4,64,1024]{2,1,0:T(8,128)(2,1)S(1)}, u32[]{:S(2)}, u32[]{:S(2)}) collective-permute-start(bf16[4,64,1024]{2,1,0:T(8,128)(2,1)S(1)} %copy-done), channel_id=1, source_target_pairs={{0,8},{8,0},{1,9},{9,1},{2,10},{10,2},{3,11},{11,3},{4,12},{12,4},... | collective-permute-start | bytes 1572872 | tf_op jit(solution)/shard_map/ppermute | solution.py:497
  20.3 5.4 %collective-permute-start.6 = (bf16[32,1152]{1,0:T(8,128)(2,1)S(1)}, bf16[32,1152]{1,0:T(8,128)(2,1)S(1)}, u32[]{:S(2)}, u32[]{:S(2)}) collective-permute-start(bf16[32,1152]{1,0:T(8,128)(2,1)S(1)} %get-tuple-element.20), channel_id=1, source_target_pairs={{0,4},{1,5},{2,6},{3,7},{4,0},{5,1},{6,2},{7,3},{8,12},{9,13},{10,... | collective-permute-start | bytes 221192 | tf_op jit(solution)/shard_map/ppermute | solution.py:514

commit v5 on v4

--- a/solution.py
+++ b/solution.py
@@ -13,8 +13,9 @@
 LANES = 128
 QUAD = 4
 PARTNERS = ((3, 3), (2, 2), (1, 1))
+LATE = 0
+HOME = (0,)
 ATTEND_FLOPS = 40_000_000_000
-PREPARE_FLOPS = 2_000_000_000
 MERGE_FLOPS = 50_000_000_000
 VMEM_BYTES = 56 * 1024 * 1024
 SMALL_BYTES = 8 * 1024 * 1024
@@ -67,6 +68,8 @@
     pool_ref,
     stay_ref,
     leave_ref,
+    turn_ref,
+    slot_ref,
     pool_v,
     queries_ref,
     fresh_ref,
@@ -138,6 +141,25 @@
         value = jnp.sum(turned * fresh_rows[s][:, :head], axis=1, keepdims=True) * scale
         fresh_scores.append(jnp.where(step_of >= s, value, f32(-1e30)))
 
+    group = steps * half
+    row = iota((2 * group, 1), 0)
+    step_of, place_of = div(row, rows), mod(row, rows)
+    side_of, rank_of = div(row, group), mod(row, half)
+    wanted = jnp.zeros_like(row)
+    new_adapter = jnp.zeros_like(row)
+    counts = [jnp.int32(0), jnp.int32(0)]
+    for j in range(rows):
+        request = order_ref[me * rows + j]
+        away = jnp.where(div(request, rows) == me, 0, 1)
+        count = jnp.where(away == 0, counts[0], counts[1])
+        counts = [counts[0] + 1 - away, counts[1] + away]
+        wanted = jnp.where(place_of == j, away * group + count, wanted)
+        here = (side_of == away) & (rank_of == count)
+        new_adapter = jnp.where(here, adapter_ref[request], new_adapter)
+    wanted = wanted + step_of * half
+    turn_ref[...] = one_hot(iota(turn_ref.shape, 1) == wanted)
+    slot_ref[...] = one_hot(iota(slot_ref.shape, 1) == new_adapter).astype(f32)
+
     pool_copy.wait()
 
     def block_rows(row, lo):
@@ -227,93 +249,34 @@
         ref[:, features + LANES :] = stream[span]
 
 
-def prepare_kernel(
-    order_ref,
-    lengths_ref,
-    table_ref,
-    adapter_ref,
-    pool_v,
-    leaving_ref,
-    turn_ref,
-    slot_ref,
-):
-    half, table_blocks, block_size, width = leaving_ref.shape
-    rows = 2 * half
-    group = turn_ref.shape[0] // 2
-    me = lax.axis_index("replica")
-
-    def copy_leaving(j, count):
-        request = order_ref[(1 - me) * rows + j]
-        hit = div(request, rows) == me
-
-        @pl.when(hit)
-        def _():
-            length = lengths_ref[request]
-            for b in range(table_blocks):
-
-                @pl.when(b * block_size < length)
-                def _():
-                    leaving_ref[count, b] = pool_v[table_ref[b, request]]
-
-                @pl.when(b * block_size >= length)
-                def _():
-                    leaving_ref[count, b] = jnp.zeros((block_size, width), bf16)
-
-        return count + hit.astype(jnp.int32)
-
-    lax.fori_loop(0, rows, copy_leaving, jnp.int32(0))
-
-    row = iota((2 * group, 1), 0)
-    step_of, place_of = div(row, rows), mod(row, rows)
-    side_of, rank_of = div(row, group), mod(row, half)
-    wanted = jnp.zeros_like(row)
-    adapter = jnp.zeros_like(row)
-    counts = [jnp.int32(0), jnp.int32(0)]
-    for j in range(rows):
-        request = order_ref[me * rows + j]
-        away = jnp.where(div(request, rows) == me, 0, 1)
-        count = jnp.where(away == 0, counts[0], counts[1])
-        counts = [counts[0] + 1 - away, counts[1] + away]
-        wanted = jnp.where(place_of == j, away * group + count, wanted)
-        here = (side_of == away) & (rank_of == count)
-        adapter = jnp.where(here, adapter_ref[request], adapter)
-    wanted = wanted + step_of * half
-    turn_ref[...] = one_hot(iota(turn_ref.shape, 1) == wanted)
-    slot_ref[...] = one_hot(iota(slot_ref.shape, 1) == adapter).astype(f32)
-
-
-def message_kernel(stay_ref, arrived_ref, weight_ref, message_ref, *, partners):
+def message_kernel(stay_ref, arrived_ref, weight_ref, message_ref, *, partners, spans):
     out_width = weight_ref.shape[1] // lax.axis_size("tensor")
     features = weight_ref.shape[0]
-    spans = message_ref.shape[1] // out_width
     here = lax.axis_index("tensor")
     partner = jnp.where(lax.axis_index("replica") == 0, partners[0], partners[1])
     mixed = jnp.concatenate([stay_ref[:, :features], arrived_ref[:, :features]], axis=0)
-    group = stay_ref.shape[0]
-    for side, ref in enumerate((stay_ref, arrived_ref)):
-        shrink = ref[:, features : features + LANES].astype(message_ref.dtype)
-        message_ref[side * group : (side + 1) * group, spans * out_width :] = shrink
-    for span in range(spans):
+    for n, span in enumerate(spans):
         start = pl.multiple_of((here ^ (span * QUAD + partner)) * out_width, out_width)
         part = dot(mixed, weight_ref[:, pl.ds(start, out_width)])
-        message_ref[:, span * out_width : (span + 1) * out_width] = part.astype(message_ref.dtype)
-
-
-def place_kernel(order_ref, lengths_ref, table_ref, pool_v, arrived_ref, placed_ref, zero_v, sem):
+        message_ref[:, n * out_width : (n + 1) * out_width] = part.astype(message_ref.dtype)
+    if message_ref.shape[1] > len(spans) * out_width:
+        group = stay_ref.shape[0]
+        for side, ref in enumerate((stay_ref, arrived_ref)):
+            shrink = ref[:, features : features + LANES].astype(message_ref.dtype)
+            message_ref[side * group : (side + 1) * group, len(spans) * out_width :] = shrink
+
+
+def place_kernel(order_ref, lengths_ref, table_ref, pool_v, *refs, stayed):
+    placed_ref, zero_v, sem = refs[-3:]
     rows, table_blocks, block_size, _ = placed_ref.shape
     me = lax.axis_index("replica")
     zero_v[...] = jnp.zeros_like(zero_v)
 
-    def step(j, count):
+    def step(j, carry):
         request = order_ref[me * rows + j]
         length = lengths_ref[request]
-        stayed = div(request, rows) == me
-
-        @pl.when(jnp.logical_not(stayed))
-        def _():
-            pltpu.make_async_copy(arrived_ref.at[count], placed_ref.at[j], sem).start()
-
-        @pl.when(stayed)
+
+        @pl.when((div(request, rows) == me) == stayed)
         def _():
             for b in range(table_blocks):
                 target = placed_ref.at[j, b]
@@ -327,10 +290,11 @@
                 def _():
                     pltpu.make_async_copy(zero_v, target, sem).start()
 
-        return count + 1 - stayed.astype(jnp.int32)
-
-    lax.fori_loop(0, rows, step, jnp.int32(0))
-    pltpu.make_async_copy(placed_ref, placed_ref, sem).wait()
+        return carry
+
+    lax.fori_loop(0, rows, step, 0)
+    part = placed_ref.at[pl.ds(0, rows // 2)]
+    pltpu.make_async_copy(part, part, sem).wait()
 
 
 def in_hbm(value):
@@ -351,10 +315,12 @@
         out_shape=(
             pltpu.VMEM((steps * rows // 2, 2 * features + LANES), bf16),
             pltpu.VMEM((steps * rows // 2, 2 * features + LANES), bf16),
+            pltpu.VMEM((steps * rows, steps * rows), bf16),
+            pltpu.VMEM((steps * rows, down.shape[0]), f32),
             pltpu.VMEM(pool.shape, bf16),
         ),
         in_specs=[smem] * 4 + [hbm] * 5,
-        out_specs=(vmem,) * 3,
+        out_specs=(vmem,) * 5,
         scratch_shapes=[
             pltpu.VMEM(queries.shape, bf16),
             pltpu.VMEM(fresh.shape, bf16),
@@ -376,32 +342,13 @@
     )(*(in_hbm(x) for x in (order, lengths, table, adapters, queries, fresh, down, residual, pool)))
 
 
-def prepare_call(order, lengths, table, adapters, pool, steps, rows, slots):
-    smem = pl.BlockSpec(memory_space=pltpu.SMEM)
+def message_call(stay, arrived, weight, partners, spans, dtype):
+    out_width = weight.shape[1] // lax.axis_size("tensor")
+    columns = len(spans) * out_width + (0 if spans == HOME else LANES)
     vmem = pl.BlockSpec(memory_space=pltpu.VMEM)
     return pl.pallas_call(
-        prepare_kernel,
-        out_shape=(
-            pltpu.VMEM((rows // 2, table.shape[0]) + pool.shape[1:], bf16),
-            pltpu.VMEM((steps * rows, steps * rows), bf16),
-            pltpu.VMEM((steps * rows, slots), f32),
-        ),
-        in_specs=[smem] * 4 + [vmem],
-        out_specs=(vmem,) * 3,
-        compiler_params=pltpu.CompilerParams(vmem_limit_bytes=SMALL_BYTES),
-        cost_estimate=pl.CostEstimate(flops=PREPARE_FLOPS, bytes_accessed=0, transcendentals=0),
-        name="prepare",
-    )(order, lengths, table, adapters, pool)
-
-
-def message_call(stay, arrived, weight, partners, dtype):
-    tensor = lax.axis_size("tensor")
-    spans = tensor // QUAD
-    columns = spans * weight.shape[1] // tensor
-    vmem = pl.BlockSpec(memory_space=pltpu.VMEM)
-    return pl.pallas_call(
-        functools.partial(message_kernel, partners=partners),
-        out_shape=pltpu.VMEM((2 * stay.shape[0], columns + LANES), dtype),
+        functools.partial(message_kernel, partners=partners, spans=spans),
+        out_shape=pltpu.VMEM((2 * stay.shape[0], columns), dtype),
         in_specs=[vmem] * 3,
         out_specs=vmem,
         compiler_params=pltpu.CompilerParams(vmem_limit_bytes=SMALL_BYTES),
@@ -409,39 +356,45 @@
     )(stay, arrived, weight)
 
 
-def place_call(order, lengths, table, pool, arrived, rows):
+def place_call(order, lengths, table, pool, rows, placed=None):
     smem = pl.BlockSpec(memory_space=pltpu.SMEM)
     vmem = pl.BlockSpec(memory_space=pltpu.VMEM)
+    hbm = pl.BlockSpec(memory_space=pl.ANY)
+    before = [] if placed is None else [placed]
     return pl.pallas_call(
-        place_kernel,
+        functools.partial(place_kernel, stayed=placed is None),
         out_shape=jax.ShapeDtypeStruct((rows, table.shape[0]) + pool.shape[1:], bf16),
-        in_specs=[smem] * 3 + [vmem] * 2,
-        out_specs=pl.BlockSpec(memory_space=pl.ANY),
+        in_specs=[smem] * 3 + [vmem] + [hbm] * len(before),
+        out_specs=hbm,
         scratch_shapes=[pltpu.VMEM(pool.shape[1:], bf16), pltpu.SemaphoreType.DMA],
+        input_output_aliases={4: 0} if before else {},
         compiler_params=pltpu.CompilerParams(vmem_limit_bytes=SMALL_BYTES),
         cost_estimate=pl.CostEstimate(flops=0, bytes_accessed=2 * pool.size, transcendentals=0),
         name="place",
-    )(order, lengths, table, pool, arrived)
-
-
-def merge_kernel(*refs, spans):
-    messages, outs = refs[:-spans], refs[-spans:]
-    total = messages[0][...]
+    )(order, lengths, table, pool, *before)
+
+
+def merge_kernel(*refs, spans, out_width):
+    messages, outs, shrink_ref = refs[:-spans], refs[-spans:-1], refs[-1]
+    columns = (spans - 1) * out_width + LANES
+    total = messages[0][:, out_width:]
     for ref in messages[1:]:
-        total = total + ref[...].astype(f32)
-    out_width = (total.shape[1] - LANES) // spans
+        total = total + ref[:, ref.shape[1] - columns :].astype(f32)
+    shrink = total[:, (spans - 1) * out_width :]
+    shrink_ref[...] = shrink
     for n, ref in enumerate(outs):
-        ref[:, :out_width] = total[:, n * out_width : (n + 1) * out_width].astype(ref.dtype)
-        ref[:, out_width:] = total[:, spans * out_width :].astype(ref.dtype)
+        ref[:, :out_width] = total[:, n * out_width : (n + 1) * out_width].astype(bf16)
+        ref[:, out_width:] = shrink.astype(bf16)
 
 
 def merge_call(messages, spans):
     rows, columns = messages[0].shape
     vmem = pl.BlockSpec(memory_space=pltpu.VMEM)
-    width = (columns - LANES) // spans + LANES
+    out_width = (columns - LANES) // spans
     return pl.pallas_call(
-        functools.partial(merge_kernel, spans=spans),
-        out_shape=[pltpu.VMEM((rows, width), f32 if n == 0 else bf16) for n in range(spans)],
+        functools.partial(merge_kernel, spans=spans, out_width=out_width),
+        out_shape=[pltpu.VMEM((rows, out_width + LANES), bf16)] * (spans - 1)
+        + [pltpu.VMEM((rows, LANES), f32)],
         in_specs=[vmem] * len(messages),
         out_specs=[vmem] * spans,
         compiler_params=pltpu.CompilerParams(vmem_limit_bytes=SMALL_BYTES),
@@ -451,15 +404,18 @@
 
 
 def finish_kernel(
-    turn_ref, slot_ref, up_ref, other_up_ref, stay_ref, arrived_ref, home_ref, *rest
+    turn_ref, slot_ref, up_ref, other_up_ref, stay_ref, arrived_ref, shrink_ref, *rest, home_count
 ):
-    across_refs, out_ref = rest[:-1], rest[-1]
+    home_refs, across_refs, out_ref = rest[:home_count], rest[home_count:-1], rest[-1]
     slots, rank, features = up_ref.shape
     group = stay_ref.shape[0]
-    total = home_ref[...]
+    total, shrink = home_refs[0][:, :features], shrink_ref[:, :rank]
+    for ref in home_refs[1:]:
+        total = total + ref[:, :features].astype(f32)
     for ref in across_refs:
-        total = total + ref[...].astype(f32)
-    shrink = total[:, features : features + rank].astype(bf16).astype(f32)
+        total = total + ref[:, :features].astype(f32)
+        shrink = shrink + ref[:, features : features + rank].astype(f32)
+    shrink = shrink.astype(bf16).astype(f32)
     wide = jnp.concatenate(
         [shrink * slot_ref[:, n : n + 1] for n in range(slots)], axis=1
     ).astype(bf16)
@@ -468,7 +424,7 @@
         span = slice(side * group, (side + 1) * group)
         raised = dot(wide[span], up[...].reshape(slots * rank, features))
         residual = stream[:, features + LANES :].astype(f32)
-        finished.append(residual + total[span, :features] + adapter_scale * raised)
+        finished.append(residual + total[span] + adapter_scale * raised)
     finished = jnp.concatenate(finished, axis=0).astype(bf16)
     out_ref[...] = dot(turn_ref[...], finished).astype(bf16).reshape(out_ref.shape)
 
@@ -498,13 +454,11 @@
 
     table = previous_block_table.T
     integers = (request_order_after, lengths, table, request_adapter_index)
-    stay, leave, pool = attend_call(
+    stay, leave, turn, slot, pool = attend_call(
         *integers, queries, fresh, adapter_down_weight, residual, pool
     )
     came = lax.ppermute(leave, "replica", swap)
-    leaving, turn, slot = prepare_call(*integers, pool, steps, rows, adapter_up_weight.shape[0])
     spans = tensor // QUAD
-
     def trade(message, partners):
         pairs = [
             (r * tensor + t, r * tensor + (t ^ partners[r]))
@@ -513,23 +467,37 @@
         ]
         return lax.ppermute(message, ("replica", "tensor"), pairs)
 
-    message = functools.partial(message_call, stay, came, output_weight)
-    landed = [trade(message(partners, bf16), partners) for partners in PARTNERS]
-    own = message((0, 0), f32)
-    arrived = lax.ppermute(leaving, "replica", swap)
-    home, *across = merge_call([own] + landed, spans)
+    def message(came, partners, chosen, dtype=bf16):
+        return message_call(stay, came, output_weight, partners, chosen, dtype)
+
+    every = tuple(range(spans))
+    early = len(PARTNERS) - LATE
+    sent = [
+        message(came, partners, every if n < early else every[1:])
+        for n, partners in enumerate(PARTNERS)
+    ]
+    collected = [trade(*item) for item in zip(sent, PARTNERS)]
+    own = message(came, (0, 0), every, f32)
+    came_later, *_ = lax.optimization_barrier((came, *sent))
+    home = [own] + collected[:early]
+    home += [trade(message(came_later, partners, HOME), partners) for partners in PARTNERS[early:]]
+    other_pool = lax.ppermute(pool, "replica", swap)
+    placed = place_call(*integers[:3], pool, rows)
+    placed, own = lax.optimization_barrier((placed, own))
+    home[0] = own
+    *across, shrink = merge_call([own] + collected, spans)
     across = [trade(piece, (n * QUAD, n * QUAD)) for n, piece in enumerate(across, 1)]
-    placed_cache = place_call(*integers[:3], pool, arrived, rows)
+    placed_cache = place_call(*integers[:3], other_pool, rows, placed)
     placed_cache, turn = lax.optimization_barrier((placed_cache, turn))
     vmem = pl.BlockSpec(memory_space=pltpu.VMEM)
     layer_out = pl.pallas_call(
-        finish_kernel,
+        functools.partial(finish_kernel, home_count=len(home)),
         out_shape=jax.ShapeDtypeStruct((steps, rows, features), bf16),
-        in_specs=[vmem] * (7 + len(across)),
+        in_specs=[vmem] * (7 + len(home) + len(across)),
         out_specs=vmem,
         compiler_params=pltpu.CompilerParams(vmem_limit_bytes=SMALL_BYTES),
         name="finish",
-    )(turn, slot, adapter_up_weight, other_up, stay, came, home, *across)
+    )(turn, slot, adapter_up_weight, other_up, stay, came, shrink, *home, *across)
     return (layer_out, placed_cache.reshape(rows, table_blocks, 1, block_size, width))
 
 

time: 27 us -> 26.8 us (level)
  Pallas kernels: 14.8 us -> 14.2 us
  waiting for transfers between devices: 2.69 us -> 3.24 us
    pallas_call x8, Pallas kernels: 8.93 us -> 8.34 us  [the longest x2 3.87 us: place_call(): pl.pallas_call(functools.partial(place_kernel, stayed=placed is None), ou...]
    ppermute x4, waiting for transfers between devices: 1.78 us -> 2.33 us  [trade(): return lax.ppermute(message, ('replica', 'tensor'), pairs)]
  transfers between devices with their start and end apart: 7 -> 7, of which waited for: 3 -> 4; matrix products, arithmetic and copies ran while one was open for 0% -> 0% of each run, Pallas kernels for 26% -> 24%
where the time goes in v5:
time: 26.8 us; the launch traced here: 26.7 us
  Pallas kernels  14.2 us (53%)
  starting transfers between devices  8.45 us (32%)
  waiting for transfers between devices  3.24 us (12%)
  between operations  0.74 us (3%)
    ppermute x4, starting transfers between devices, trade(): return lax.ppermute(message, ('replica', 'tensor'), pairs)  7.4 us
    pallas_call x1, Pallas kernels, attend_call(): pl.pallas_call(attend_kernel, out_shape=(pltpu.VMEM((steps * rows // 2, 2...  5.85 us
    pallas_call x2, Pallas kernels, place_call(): pl.pallas_call(functools.partial(place_kernel, stayed=placed is None), ou...  3.87 us
    pallas_call x4, Pallas kernels, message_call(): pl.pallas_call(functools.partial(message_kernel, partners=partners, spans...  3.3 us
    ppermute x4, waiting for transfers between devices, trade(): return lax.ppermute(message, ('replica', 'tensor'), pairs)  2.33 us
    pallas_call x1, Pallas kernels, shards(): pl.pallas_call(functools.partial(finish_kernel, home_count=len(home)), ou...  1.13 us
    ppermute x1, waiting for transfers between devices, shards(): came = lax.ppermute(leave, 'replica', swap)  0.91 us
    ppermute x1, starting transfers between devices, shards(): came = lax.ppermute(leave, 'replica', swap)  0.54 us
  transfers between devices with their start and end apart: 7, of which 4 were waited for; matrix products, arithmetic and copies ran while one was open for 0% of the time, Pallas kernels for 24%

profile of v5, /device:TPU:0, one launch (start us, length us, event | category | flops | bytes accessed | tf_op | source)
XLA Modules:
  0.0 26.7 jit_solution(12742121273897262075)
XLA Ops:
  0.6 0.0 slice-start
  0.6 0.0 slice-start.1
  0.7 0.0 slice-start.2
  0.7 0.0 slice-start.3
  0.7 5.8 %attend.1 = (bf16[16,2176]{1,0:T(8,128)(2,1)S(1)}, bf16[16,2176]{1,0:T(8,128)(2,1)S(1)}, bf16[32,32]{1,0:T(8,128)(2,1)S(1)}, f32[32,4]{1,0:T(8,128)S(1)}, bf16[128,64,256]{2,1,0:T(8,128)(2,1)S(1)}) custom-call(s32[32]{0:T(128)} %order_ref.5, s32[32]{0:T(128)} %lengths_ref.5, s32[8,32]{1,0:T(8,128)} %bitcast.8, s32[32]{0:T(128)} %adapter_ref.1, ...), custom_call_target="tpu_custom_call" | custom-call | flops 40000000000 | bytes 8388608 | tf_op jit(solution)/shard_map/attend/pallas_call | solution.py:313
  6.5 0.5 %collective-permute-start.1 = (bf16[16,2176]{1,0:T(8,128)(2,1)S(1)}, bf16[16,2176]{1,0:T(8,128)(2,1)S(1)}, u32[]{:S(2)}, u32[]{:S(2)}) collective-permute-start(bf16[16,2176]{1,0:T(8,128)(2,1)S(1)} %get-tuple-element.15), channel_id=1, source_target_pairs={{0,8},{8,0},{1,9},{9,1},{2,10},{10,2},{3,11},{11,3},{4,12},{12,4},... | collective-permute-start | bytes 208904 | tf_op jit(solution)/shard_map/ppermute | solution.py:460
  7.1 0.9 %collective-permute-done.1.arrived_ref = bf16[16,2176]{1,0:T(8,128)(2,1)S(1)} collective-permute-done((bf16[16,2176]{1,0:T(8,128)(2,1)S(1)}, bf16[16,2176]{1,0:T(8,128)(2,1)S(1)}, u32[]{:S(2)}, u32[]{:S(2)}) %collective-permute-start.1) | collective-permute-done | bytes 69664 | tf_op jit(solution)/shard_map/ppermute | solution.py:460
  8.0 0.0 slice-done
  8.0 0.0 slice-done.1
  8.0 0.8 %message.5 = bf16[32,2176]{1,0:T(8,128)(2,1)S(1)} custom-call(bf16[16,2176]{1,0:T(8,128)(2,1)S(1)} %get-tuple-element.14.stay_ref, bf16[16,2176]{1,0:T(8,128)(2,1)S(1)} %collective-permute-done.1.arrived_ref, bf16[1024,8192]{1,0:T(8,128)(2,1)S(1)} %bitcast.7), custom_call_target="tpu_custom_call" | custom-call | tf_op jit(solution)/shard_map/message/pallas_call | solution.py:349
  8.8 4.0 %collective-permute-start.3 = (bf16[32,2176]{1,0:T(8,128)(2,1)S(1)}, bf16[32,2176]{1,0:T(8,128)(2,1)S(1)}, u32[]{:S(2)}, u32[]{:S(2)}) collective-permute-start(bf16[32,2176]{1,0:T(8,128)(2,1)S(1)} %message.5), channel_id=1, source_target_pairs={{0,3},{1,2},{2,1},{3,0},{4,7},{5,6},{6,5},{7,4},{8,11},{9,10},{10,... | collective-permute-start | bytes 417800 | tf_op jit(solution)/shard_map/ppermute | solution.py:468
  12.8 0.8 %message.6 = bf16[32,2176]{1,0:T(8,128)(2,1)S(1)} custom-call(bf16[16,2176]{1,0:T(8,128)(2,1)S(1)} %get-tuple-element.14.stay_ref, bf16[16,2176]{1,0:T(8,128)(2,1)S(1)} %collective-permute-done.1.arrived_ref, bf16[1024,8192]{1,0:T(8,128)(2,1)S(1)} %bitcast.7), custom_call_target="tpu_custom_call" | custom-call | tf_op jit(solution)/shard_map/message/pallas_call | solution.py:349
  13.6 0.0 copy-start.1
  13.6 0.0 copy-start.2
  13.7 0.0 copy-start.3
  13.7 0.5 %collective-permute-start.4 = (bf16[32,2176]{1,0:T(8,128)(2,1)S(1)}, bf16[32,2176]{1,0:T(8,128)(2,1)S(1)}, u32[]{:S(2)}, u32[]{:S(2)}) collective-permute-start(bf16[32,2176]{1,0:T(8,128)(2,1)S(1)} %message.6), channel_id=1, source_target_pairs={{0,2},{1,3},{2,0},{3,1},{4,6},{5,7},{6,4},{7,5},{8,10},{9,11},{10,... | collective-permute-start | bytes 417800 | tf_op jit(solution)/shard_map/ppermute | solution.py:468
  14.2 0.8 %message.7 = bf16[32,2176]{1,0:T(8,128)(2,1)S(1)} custom-call(bf16[16,2176]{1,0:T(8,128)(2,1)S(1)} %get-tuple-element.14.stay_ref, bf16[16,2176]{1,0:T(8,128)(2,1)S(1)} %collective-permute-done.1.arrived_ref, bf16[1024,8192]{1,0:T(8,128)(2,1)S(1)} %bitcast.7), custom_call_target="tpu_custom_call" | custom-call | tf_op jit(solution)/shard_map/message/pallas_call | solution.py:349
  15.0 0.1 collective-permute-start.5
  15.1 0.0 collective-permute-start
  15.1 0.5 %collective-permute-start.2 = (bf16[4,64,1024]{2,1,0:T(8,128)(2,1)S(1)}, bf16[4,64,1024]{2,1,0:T(8,128)(2,1)S(1)}, u32[]{:S(2)}, u32[]{:S(2)}) collective-permute-start(bf16[4,64,1024]{2,1,0:T(8,128)(2,1)S(1)} %copy-done), channel_id=1, source_target_pairs={{0,8},{8,0},{1,9},{9,1},{2,10},{10,2},{3,11},{11,3},{4,12},{12,4},... | collective-permute-start | bytes 1572872 | tf_op jit(solution)/shard_map/ppermute | solution.py:453
  15.7 0.0 copy-done.2
  15.7 2.0 %place.2.refs_0_ = bf16[16,8,64,256]{3,2,1,0:T(8,128)(2,1)} custom-call(s32[32]{0:T(128)S(1)} %copy-done.2, s32[32]{0:T(128)S(1)} %copy-done.3, s32[8,32]{1,0:T(8,128)S(1)} %bitcast.9, bf16[128,64,256]{2,1,0:T(8,128)(2,1)S(1)} %get-tuple-element.13.pool_v), custom_call_target="tpu_custom_call" | custom-call | bytes 4194304 | tf_op jit(solution)/shard_map/place/pallas_call | solution.py:364
  17.6 0.8 %message.4.refs_0_.rest_0_ = f32[32,2176]{1,0:T(8,128)S(1)} custom-call(bf16[16,2176]{1,0:T(8,128)(2,1)S(1)} %get-tuple-element.14.stay_ref, bf16[16,2176]{1,0:T(8,128)(2,1)S(1)} %collective-permute-done.1.arrived_ref, bf16[1024,8192]{1,0:T(8,128)(2,1)S(1)} %bitcast.7), custom_call_target="tpu_custom_call" | custom-call | tf_op jit(solution)/shard_map/message/pallas_call | solution.py:349
  18.4 0.0 collective-permute-done.3.refs_1_.rest_1_
  18.4 1.4 %collective-permute-done.4.refs_2_.rest_2_ = bf16[32,2176]{1,0:T(8,128)(2,1)S(1)} collective-permute-done((bf16[32,2176]{1,0:T(8,128)(2,1)S(1)}, bf16[32,2176]{1,0:T(8,128)(2,1)S(1)}, u32[]{:S(2)}, u32[]{:S(2)}) %collective-permute-start.4) | collective-permute-done | bytes 139296 | tf_op jit(solution)/shard_map/ppermute | solution.py:468
  19.8 0.3 %collective-permute-done.5.refs_3_.rest_3_ = bf16[32,2176]{1,0:T(8,128)(2,1)S(1)} collective-permute-done((bf16[32,2176]{1,0:T(8,128)(2,1)S(1)}, bf16[32,2176]{1,0:T(8,128)(2,1)S(1)}, u32[]{:S(2)}, u32[]{:S(2)}) %collective-permute-start.5) | collective-permute-done | bytes 139296 | tf_op jit(solution)/shard_map/ppermute | solution.py:468
  20.2 2.8 %collective-permute-start.6 = (bf16[32,1152]{1,0:T(8,128)(2,1)S(1)}, bf16[32,1152]{1,0:T(8,128)(2,1)S(1)}, u32[]{:S(2)}, u32[]{:S(2)}) collective-permute-start(bf16[32,1152]{1,0:T(8,128)(2,1)S(1)} %get-tuple-element.22), channel_id=1, source_target_pairs={{0,4},{1,5},{2,6},{3,7},{4,0},{5,1},{6,2},{7,3},{8,12},{9,13},{10,... | collective-permute-start | bytes 221192 | tf_op jit(solution)/shard_map/ppermute | solution.py:468
  23.0 0.0 collective-permute-done.pool_v
  23.0 1.9 %place.3 = bf16[16,8,64,256]{3,2,1,0:T(8,128)(2,1)} custom-call(s32[32]{0:T(128)S(1)} %copy-done.2, s32[32]{0:T(128)S(1)} %copy-done.3, s32[8,32]{1,0:T(8,128)S(1)} %bitcast.10, bf16[128,64,256]{2,1,0:T(8,128)(2,1)S(1)} %collective-permute-done.pool_v, bf16[16,8,64,256]{3,2,1,0:T(8,128)(2,1)} %place.2.refs_0_), custom_call_target="tpu_custom_call", output_to_operand_aliasing={{}: (4, {})} | custom-call | bytes 4194304 | tf_op jit(solution)/shard_map/place/pallas_call | solution.py:364
  24.9 0.6 %collective-permute-done.6.rest_4_ = bf16[32,1152]{1,0:T(8,128)(2,1)S(1)} collective-permute-done((bf16[32,1152]{1,0:T(8,128)(2,1)S(1)}, bf16[32,1152]{1,0:T(8,128)(2,1)S(1)}, u32[]{:S(2)}, u32[]{:S(2)}) %collective-permute-start.6) | collective-permute-done | bytes 73760 | tf_op jit(solution)/shard_map/ppermute | solution.py:468
  25.5 0.0 collective-permute-done.2.other_up_ref
  25.5 1.1 %finish.1 = bf16[2,16,1024]{2,1,0:T(8,128)(2,1)} custom-call(bf16[32,32]{1,0:T(8,128)(2,1)S(1)} %get-tuple-element.18.turn_ref, f32[32,4]{1,0:T(8,128)S(1)} %get-tuple-element.19.slot_ref, bf16[4,64,1024]{2,1,0:T(8,128)(2,1)S(1)} %copy-done, bf16[4,64,1024]{2,1,0:T(8,128)(2,1)S(1)} %collective-permute-done.2.other_up_ref, ...), custom_call_target="tpu_custom_call" | custom-call | tf_op jit(solution)/shard_map/finish/pallas_call | solution.py:493
  (8 shorter events, 0.1 us)
Async XLA Ops:
  0.6 7.4 %slice-start = ((s8[16777216]{0:T(1024)(128)(4,1)}), s8[4194304]{0:T(1024)(128)(4,1)S(1)}, s32[]{:S(2)}) async-start(s8[16777216]{0:T(1024)(128)(4,1)} %bitcast.6), calls=%async_computation | async-start | bytes 8388608
  0.6 7.3 %slice-start.1 = ((s8[16777216]{0:T(1024)(128)(4,1)}), s8[4194304]{0:T(1024)(128)(4,1)S(1)}, s32[]{:S(2)}) async-start(s8[16777216]{0:T(1024)(128)(4,1)} %bitcast.6), calls=%async_computation.1 | async-start | bytes 8388608
  0.7 7.3 %slice-start.2 = ((s8[16777216]{0:T(1024)(128)(4,1)}), s8[4194304]{0:T(1024)(128)(4,1)S(1)}, s32[]{:S(2)}) async-start(s8[16777216]{0:T(1024)(128)(4,1)} %bitcast.6), calls=%async_computation.2 | async-start | bytes 8388608
  0.7 7.3 %slice-start.3 = ((s8[16777216]{0:T(1024)(128)(4,1)}), s8[4194304]{0:T(1024)(128)(4,1)S(1)}, s32[]{:S(2)}) async-start(s8[16777216]{0:T(1024)(128)(4,1)} %bitcast.6), calls=%async_computation.3 | async-start | bytes 8388608
  6.5 1.4 %collective-permute-start.1 = (bf16[16,2176]{1,0:T(8,128)(2,1)S(1)}, bf16[16,2176]{1,0:T(8,128)(2,1)S(1)}, u32[]{:S(2)}, u32[]{:S(2)}) collective-permute-start(bf16[16,2176]{1,0:T(8,128)(2,1)S(1)} %get-tuple-element.15), channel_id=1, source_target_pairs={{0,8},{8,0},{1,9},{9,1},{2,10},{10,2},{3,11},{11,3},{4,12},{12,4},... | collective-permute-start | bytes 208904 | tf_op jit(solution)/shard_map/ppermute | solution.py:460
  8.8 9.6 %collective-permute-start.3 = (bf16[32,2176]{1,0:T(8,128)(2,1)S(1)}, bf16[32,2176]{1,0:T(8,128)(2,1)S(1)}, u32[]{:S(2)}, u32[]{:S(2)}) collective-permute-start(bf16[32,2176]{1,0:T(8,128)(2,1)S(1)} %message.5), channel_id=1, source_target_pairs={{0,3},{1,2},{2,1},{3,0},{4,7},{5,6},{6,5},{7,4},{8,11},{9,10},{10,... | collective-permute-start | bytes 417800 | tf_op jit(solution)/shard_map/ppermute | solution.py:468
  13.6 1.5 %copy-start = (bf16[4,64,1024]{2,1,0:T(8,128)(2,1)S(1)}, bf16[4,64,1024]{2,1,0:T(8,128)(2,1)}, u32[]{:S(2)}) copy-start(bf16[4,64,1024]{2,1,0:T(8,128)(2,1)} %up_ref.1) | copy-start | bytes 1572868
  13.6 2.0 %copy-start.1 = (s32[32,8]{0,1:T(8,128)S(1)}, s32[32,8]{0,1:T(8,128)}, u32[]{:S(2)}) copy-start(s32[32,8]{0,1:T(8,128)} %param.19) | copy-start | bytes 3076
  13.6 2.0 %copy-start.2 = (s32[32]{0:T(128)S(1)}, s32[32]{0:T(128)}, u32[]{:S(2)}) copy-start(s32[32]{0:T(128)} %order_ref.5) | copy-start | bytes 388
  13.7 2.0 %copy-start.3 = (s32[32]{0:T(128)S(1)}, s32[32]{0:T(128)}, u32[]{:S(2)}) copy-start(s32[32]{0:T(128)} %lengths_ref.5) | copy-start | bytes 388
  13.7 6.2 %collective-permute-start.4 = (bf16[32,2176]{1,0:T(8,128)(2,1)S(1)}, bf16[32,2176]{1,0:T(8,128)(2,1)S(1)}, u32[]{:S(2)}, u32[]{:S(2)}) collective-permute-start(bf16[32,2176]{1,0:T(8,128)(2,1)S(1)} %message.6), channel_id=1, source_target_pairs={{0,2},{1,3},{2,0},{3,1},{4,6},{5,7},{6,4},{7,5},{8,10},{9,11},{10,... | collective-permute-start | bytes 417800 | tf_op jit(solution)/shard_map/ppermute | solution.py:468
  15.0 5.2 %collective-permute-start.5 = (bf16[32,2176]{1,0:T(8,128)(2,1)S(1)}, bf16[32,2176]{1,0:T(8,128)(2,1)S(1)}, u32[]{:S(2)}, u32[]{:S(2)}) collective-permute-start(bf16[32,2176]{1,0:T(8,128)(2,1)S(1)} %message.7), channel_id=1, source_target_pairs={{0,1},{1,0},{2,3},{3,2},{4,5},{5,4},{6,7},{7,6},{8,9},{9,8},{10,11... | collective-permute-start | bytes 417800 | tf_op jit(solution)/shard_map/ppermute | solution.py:468
  15.1 7.9 %collective-permute-start = (bf16[128,64,256]{2,1,0:T(8,128)(2,1)S(1)}, bf16[128,64,256]{2,1,0:T(8,128)(2,1)S(1)}, u32[]{:S(2)}, u32[]{:S(2)}) collective-permute-start(bf16[128,64,256]{2,1,0:T(8,128)(2,1)S(1)} %get-tuple-element.13.pool_v), channel_id=1, source_target_pairs={{0,8},{8,0},{1,9},{9,1},{2,10},{10,2},{3,11},{11,3},{4,12},{12,4},... | collective-permute-start | bytes 12582920 | tf_op jit(solution)/shard_map/ppermute | solution.py:484
  15.1 10.4 %collective-permute-start.2 = (bf16[4,64,1024]{2,1,0:T(8,128)(2,1)S(1)}, bf16[4,64,1024]{2,1,0:T(8,128)(2,1)S(1)}, u32[]{:S(2)}, u32[]{:S(2)}) collective-permute-start(bf16[4,64,1024]{2,1,0:T(8,128)(2,1)S(1)} %copy-done), channel_id=1, source_target_pairs={{0,8},{8,0},{1,9},{9,1},{2,10},{10,2},{3,11},{11,3},{4,12},{12,4},... | collective-permute-start | bytes 1572872 | tf_op jit(solution)/shard_map/ppermute | solution.py:453
  20.2 5.3 %collective-permute-start.6 = (bf16[32,1152]{1,0:T(8,128)(2,1)S(1)}, bf16[32,1152]{1,0:T(8,128)(2,1)S(1)}, u32[]{:S(2)}, u32[]{:S(2)}) collective-permute-start(bf16[32,1152]{1,0:T(8,128)(2,1)S(1)} %get-tuple-element.22), channel_id=1, source_target_pairs={{0,4},{1,5},{2,6},{3,7},{4,0},{5,1},{6,2},{7,3},{8,12},{9,13},{10,... | collective-permute-start | bytes 221192 | tf_op jit(solution)/shard_map/ppermute | solution.py:468

commit v6 on v5

--- a/solution.py
+++ b/solution.py
@@ -13,8 +13,6 @@
 LANES = 128
 QUAD = 4
 PARTNERS = ((3, 3), (2, 2), (1, 1))
-LATE = 0
-HOME = (0,)
 ATTEND_FLOPS = 40_000_000_000
 MERGE_FLOPS = 50_000_000_000
 VMEM_BYTES = 56 * 1024 * 1024
@@ -78,6 +76,7 @@
     scores_v,
     probs_v,
     attended_v,
+    back_v,
     found,
     target,
     small_sem,
@@ -108,11 +107,9 @@
         )
     ]
     pool_copy = pltpu.make_async_copy(pool_ref, pool_v, pool_sem)
-    small_copies[0].start()
-    small_copies[1].start()
     pool_copy.start()
-    small_copies[2].start()
-    small_copies[3].start()
+    for copy in small_copies:
+        copy.start()
 
     for place in range(places):
         rank_rows(order_ref, found, target, me, me if place == 0 else 1 - me, rows, place * half)
@@ -144,68 +141,20 @@
     group = steps * half
     row = iota((2 * group, 1), 0)
     step_of, place_of = div(row, rows), mod(row, rows)
-    side_of, rank_of = div(row, group), mod(row, half)
     wanted = jnp.zeros_like(row)
-    new_adapter = jnp.zeros_like(row)
+    slot_of = jnp.zeros_like(row)
     counts = [jnp.int32(0), jnp.int32(0)]
     for j in range(rows):
         request = order_ref[me * rows + j]
         away = jnp.where(div(request, rows) == me, 0, 1)
         count = jnp.where(away == 0, counts[0], counts[1])
         counts = [counts[0] + 1 - away, counts[1] + away]
-        wanted = jnp.where(place_of == j, away * group + count, wanted)
-        here = (side_of == away) & (rank_of == count)
-        new_adapter = jnp.where(here, adapter_ref[request], new_adapter)
+        here = place_of == j
+        wanted = jnp.where(here, away * group + count, wanted)
+        slot_of = jnp.where(here, away * slots + adapter_ref[request], slot_of)
     wanted = wanted + step_of * half
     turn_ref[...] = one_hot(iota(turn_ref.shape, 1) == wanted)
-    slot_ref[...] = one_hot(iota(slot_ref.shape, 1) == new_adapter).astype(f32)
-
-    pool_copy.wait()
-
-    def block_rows(row, lo):
-        return jnp.concatenate(
-            [pool_v[table_ref[b, first + row], :, lo : lo + head] for b in range(table_blocks)],
-            axis=0,
-        )
-
-    position = iota((block_size, width), 0)
-    for row in range(rows):
-        length = lengths_ref[first + row]
-        full = div(length, block_size)
-
-        @pl.when(full < table_blocks)
-        def _(row=row, length=length, full=full):
-            block = table_ref[full, first + row]
-            kept = jnp.where(
-                position < length - full * block_size, pool_v[block].astype(f32), 0.0
-            )
-            pool_v[block] = kept.astype(bf16)
-
-    column = iota((sh, positions), 1)
-    for row in range(rows):
-        part = dot(query_rows[row * sh : (row + 1) * sh], block_rows(row, 0), ((1,), (1,)))
-        part = jnp.where(column < lengths_ref[first + row], part * scale, f32(-1e30))
-        scores_v[row * sh : (row + 1) * sh, :] = part
-
-    scores = scores_v[...]
-    top = jnp.max(scores, axis=1, keepdims=True)
-    for value in fresh_scores:
-        top = jnp.maximum(top, value)
-    weights = jnp.exp(scores - top)
-    fresh_weights = [jnp.exp(value - top) for value in fresh_scores]
-    totals = jnp.sum(weights, axis=1, keepdims=True)
-    for value in fresh_weights:
-        totals = totals + value
-    probs_v[...] = weights / totals
-
-    for row in range(rows):
-        span = slice(row * sh, (row + 1) * sh)
-        attended_v[span, :] = dot(probs_v[span, :].astype(bf16), block_rows(row, head))
-    attended = attended_v[...]
-    for value, row in zip(fresh_weights, fresh_rows):
-        share = (value / totals).astype(bf16).astype(f32)
-        attended = attended + share * row[:, head:]
-    attended = attended.astype(bf16)
+    slot_ref[...] = one_hot(iota(slot_ref.shape, 1) == slot_of).astype(f32)
 
     row_index = iota((places * steps * half, 1), 0)
     source = jnp.zeros_like(row_index)
@@ -218,11 +167,60 @@
             adapter = jnp.where(here, adapter_ref[first + local], adapter)
     step_index = div(mod(row_index, steps * half), half)
     columns = iota((places * steps * half, total), 1)
-    pieces = []
     for h in range(heads):
         wanted = source * sh + step_index * heads + h
-        pieces.append(dot(one_hot(columns == wanted), attended))
-    mixed = jnp.concatenate(pieces, axis=1).astype(bf16)
+        span = slice(h * places * steps * half, (h + 1) * places * steps * half)
+        back_v[span, :] = one_hot(columns == wanted)
+
+    small_copies[3].wait()
+    wanted = step_index * rows + source
+    stream = dot(
+        one_hot(iota((steps * rows, steps * rows), 1) == wanted),
+        residual_ref[...].reshape(steps * rows, features),
+    ).astype(bf16)
+    for place, ref in enumerate((stay_ref, leave_ref)):
+        span = slice(place * steps * half, (place + 1) * steps * half)
+        ref[:, features + LANES :] = stream[span]
+
+    pool_copy.wait()
+
+    def block_rows(row, lo):
+        return jnp.concatenate(
+            [pool_v[table_ref[b, first + row], :, lo : lo + head] for b in range(table_blocks)],
+            axis=0,
+        )
+
+    column = iota((sh, positions), 1)
+    for row in range(rows):
+        part = dot(query_rows[row * sh : (row + 1) * sh], block_rows(row, 0), ((1,), (1,)))
+        part = jnp.where(column < lengths_ref[first + row], part * scale, f32(-1e30))
+        scores_v[row * sh : (row + 1) * sh, :] = part
+
+    scores = scores_v[...]
+    top = jnp.max(scores, axis=1, keepdims=True)
+    for value in fresh_scores:
+        top = jnp.maximum(top, value)
+    weights = jnp.exp(scores - top)
+    fresh_weights = [jnp.exp(value - top) for value in fresh_scores]
+    totals = jnp.sum(weights, axis=1, keepdims=True)
+    for value in fresh_weights:
+        totals = totals + value
+    probs_v[...] = weights / totals
+
+    for row in range(rows):
+        span = slice(row * sh, (row + 1) * sh)
+        attended_v[span, :] = dot(probs_v[span, :].astype(bf16), block_rows(row, head))
+    attended = attended_v[...]
+    for value, row in zip(fresh_weights, fresh_rows):
+        share = (value / totals).astype(bf16).astype(f32)
+        attended = attended + share * row[:, head:]
+    attended = attended.astype(bf16)
+
+    turned = dot(back_v[...], attended)
+    count = places * steps * half
+    mixed = jnp.concatenate(
+        [turned[h * count : (h + 1) * count] for h in range(heads)], axis=1
+    ).astype(bf16)
 
     small_copies[2].wait()
     wide = dot(mixed, down_ref[...].reshape(slots * rank, features), ((1,), (1,)))
@@ -235,64 +233,86 @@
         [shrink, jnp.zeros((places * steps * half, LANES - rank), f32)], axis=1
     ).astype(bf16)
 
-    small_copies[3].wait()
-    wanted = step_index * rows + source
-    stream = dot(
-        one_hot(iota((steps * rows, steps * rows), 1) == wanted),
-        residual_ref[...].reshape(steps * rows, features),
-    ).astype(bf16)
     group = steps * half
     for place, ref in enumerate((stay_ref, leave_ref)):
         span = slice(place * group, (place + 1) * group)
         ref[:, :features] = mixed[span]
         ref[:, features : features + LANES] = shrink[span]
-        ref[:, features + LANES :] = stream[span]
-
-
-def message_kernel(stay_ref, arrived_ref, weight_ref, message_ref, *, partners, spans):
+
+
+def sort_kernel(turn_ref, stay_ref, came_ref, out_ref):
+    out_ref[...] = dot(
+        turn_ref[...], jnp.concatenate([stay_ref[...], came_ref[...]], axis=0)
+    ).astype(bf16)
+
+
+def sort_call(turn, stay, came):
+    vmem = pl.BlockSpec(memory_space=pltpu.VMEM)
+    return pl.pallas_call(
+        sort_kernel,
+        out_shape=pltpu.VMEM((turn.shape[0], stay.shape[1]), bf16),
+        in_specs=[vmem] * 3,
+        out_specs=vmem,
+        compiler_params=pltpu.CompilerParams(vmem_limit_bytes=SMALL_BYTES),
+        name="sort",
+    )(turn, stay, came)
+
+
+def message_kernel(rows_ref, came_ref, weight_ref, message_ref, *, partners):
     out_width = weight_ref.shape[1] // lax.axis_size("tensor")
     features = weight_ref.shape[0]
+    spans = message_ref.shape[1] // out_width
     here = lax.axis_index("tensor")
     partner = jnp.where(lax.axis_index("replica") == 0, partners[0], partners[1])
-    mixed = jnp.concatenate([stay_ref[:, :features], arrived_ref[:, :features]], axis=0)
-    for n, span in enumerate(spans):
+    mixed = rows_ref[:, :features]
+    for span in range(spans):
         start = pl.multiple_of((here ^ (span * QUAD + partner)) * out_width, out_width)
         part = dot(mixed, weight_ref[:, pl.ds(start, out_width)])
-        message_ref[:, n * out_width : (n + 1) * out_width] = part.astype(message_ref.dtype)
-    if message_ref.shape[1] > len(spans) * out_width:
-        group = stay_ref.shape[0]
-        for side, ref in enumerate((stay_ref, arrived_ref)):
-            shrink = ref[:, features : features + LANES].astype(message_ref.dtype)
-            message_ref[side * group : (side + 1) * group, len(spans) * out_width :] = shrink
+        message_ref[:, span * out_width : (span + 1) * out_width] = part.astype(message_ref.dtype)
+    shrink = rows_ref[:, features : features + LANES]
+    message_ref[:, spans * out_width :] = shrink.astype(message_ref.dtype)
 
 
 def place_kernel(order_ref, lengths_ref, table_ref, pool_v, *refs, stayed):
-    placed_ref, zero_v, sem = refs[-3:]
+    placed_ref, zero_v, edge_v, sem = refs[-4:]
     rows, table_blocks, block_size, _ = placed_ref.shape
     me = lax.axis_index("replica")
     zero_v[...] = jnp.zeros_like(zero_v)
-
-    def step(j, carry):
+    position = iota(zero_v.shape, 0)
+
+    def step(j, count):
         request = order_ref[me * rows + j]
         length = lengths_ref[request]
-
-        @pl.when((div(request, rows) == me) == stayed)
+        full = div(length, block_size)
+        hit = (div(request, rows) == me) == stayed
+
+        @pl.when(hit)
         def _():
+            @pl.when(full < table_blocks)
+            def _():
+                block = table_ref[jnp.minimum(full, table_blocks - 1), request]
+                kept = position < length - full * block_size
+                edge_v[count] = jnp.where(kept, pool_v[block].astype(f32), 0.0).astype(bf16)
+
             for b in range(table_blocks):
                 target = placed_ref.at[j, b]
 
-                @pl.when(b * block_size < length)
+                @pl.when(b < full)
                 def _():
                     source = pool_v.at[table_ref[b, request]]
                     pltpu.make_async_copy(source, target, sem).start()
 
-                @pl.when(b * block_size >= length)
+                @pl.when(b == full)
+                def _():
+                    pltpu.make_async_copy(edge_v.at[count], target, sem).start()
+
+                @pl.when(b > full)
                 def _():
                     pltpu.make_async_copy(zero_v, target, sem).start()
 
-        return carry
-
-    lax.fori_loop(0, rows, step, 0)
+        return count + hit.astype(jnp.int32)
+
+    lax.fori_loop(0, rows, step, jnp.int32(0))
     part = placed_ref.at[pl.ds(0, rows // 2)]
     pltpu.make_async_copy(part, part, sem).wait()
 
@@ -316,7 +336,7 @@
             pltpu.VMEM((steps * rows // 2, 2 * features + LANES), bf16),
             pltpu.VMEM((steps * rows // 2, 2 * features + LANES), bf16),
             pltpu.VMEM((steps * rows, steps * rows), bf16),
-            pltpu.VMEM((steps * rows, down.shape[0]), f32),
+            pltpu.VMEM((steps * rows, 2 * down.shape[0]), f32),
             pltpu.VMEM(pool.shape, bf16),
         ),
         in_specs=[smem] * 4 + [hbm] * 5,
@@ -329,6 +349,7 @@
             pltpu.VMEM((score_rows, positions), f32),
             pltpu.VMEM((score_rows, positions), f32),
             pltpu.VMEM((score_rows, width // 2), f32),
+            pltpu.VMEM((features // (width // 2) * steps * rows, score_rows), bf16),
             pltpu.SMEM((rows,), jnp.int32),
             pltpu.SMEM((rows,), jnp.int32),
             pltpu.SemaphoreType.DMA((4,)),
@@ -342,18 +363,18 @@
     )(*(in_hbm(x) for x in (order, lengths, table, adapters, queries, fresh, down, residual, pool)))
 
 
-def message_call(stay, arrived, weight, partners, spans, dtype):
-    out_width = weight.shape[1] // lax.axis_size("tensor")
-    columns = len(spans) * out_width + (0 if spans == HOME else LANES)
+def message_call(rows, came, weight, partners, dtype):
+    tensor = lax.axis_size("tensor")
+    columns = tensor // QUAD * weight.shape[1] // tensor
     vmem = pl.BlockSpec(memory_space=pltpu.VMEM)
     return pl.pallas_call(
-        functools.partial(message_kernel, partners=partners, spans=spans),
-        out_shape=pltpu.VMEM((2 * stay.shape[0], columns), dtype),
+        functools.partial(message_kernel, partners=partners),
+        out_shape=pltpu.VMEM((rows.shape[0], columns + LANES), dtype),
         in_specs=[vmem] * 3,
         out_specs=vmem,
         compiler_params=pltpu.CompilerParams(vmem_limit_bytes=SMALL_BYTES),
         name="message",
-    )(stay, arrived, weight)
+    )(rows, came, weight)
 
 
 def place_call(order, lengths, table, pool, rows, placed=None):
@@ -366,7 +387,11 @@
         out_shape=jax.ShapeDtypeStruct((rows, table.shape[0]) + pool.shape[1:], bf16),
         in_specs=[smem] * 3 + [vmem] + [hbm] * len(before),
         out_specs=hbm,
-        scratch_shapes=[pltpu.VMEM(pool.shape[1:], bf16), pltpu.SemaphoreType.DMA],
+        scratch_shapes=[
+            pltpu.VMEM(pool.shape[1:], bf16),
+            pltpu.VMEM((rows // 2,) + pool.shape[1:], bf16),
+            pltpu.SemaphoreType.DMA,
+        ],
         input_output_aliases={4: 0} if before else {},
         compiler_params=pltpu.CompilerParams(vmem_limit_bytes=SMALL_BYTES),
         cost_estimate=pl.CostEstimate(flops=0, bytes_accessed=2 * pool.size, transcendentals=0),
@@ -403,12 +428,9 @@
     )(*messages)
 
 
-def finish_kernel(
-    turn_ref, slot_ref, up_ref, other_up_ref, stay_ref, arrived_ref, shrink_ref, *rest, home_count
-):
+def finish_kernel(slot_ref, up_ref, other_up_ref, rows_ref, shrink_ref, *rest, home_count):
     home_refs, across_refs, out_ref = rest[:home_count], rest[home_count:-1], rest[-1]
     slots, rank, features = up_ref.shape
-    group = stay_ref.shape[0]
     total, shrink = home_refs[0][:, :features], shrink_ref[:, :rank]
     for ref in home_refs[1:]:
         total = total + ref[:, :features].astype(f32)
@@ -416,17 +438,14 @@
         total = total + ref[:, :features].astype(f32)
         shrink = shrink + ref[:, features : features + rank].astype(f32)
     shrink = shrink.astype(bf16).astype(f32)
-    wide = jnp.concatenate(
-        [shrink * slot_ref[:, n : n + 1] for n in range(slots)], axis=1
-    ).astype(bf16)
-    finished = []
-    for side, (up, stream) in enumerate(((up_ref, stay_ref), (other_up_ref, arrived_ref))):
-        span = slice(side * group, (side + 1) * group)
-        raised = dot(wide[span], up[...].reshape(slots * rank, features))
-        residual = stream[:, features + LANES :].astype(f32)
-        finished.append(residual + total[span] + adapter_scale * raised)
-    finished = jnp.concatenate(finished, axis=0).astype(bf16)
-    out_ref[...] = dot(turn_ref[...], finished).astype(bf16).reshape(out_ref.shape)
+    result = total + rows_ref[:, features + LANES :].astype(f32)
+    for side, up in enumerate((up_ref, other_up_ref)):
+        wide = jnp.concatenate(
+            [shrink * slot_ref[:, side * slots + n : side * slots + n + 1] for n in range(slots)],
+            axis=1,
+        ).astype(bf16)
+        result = result + adapter_scale * dot(wide, up[...].reshape(slots * rank, features))
+    out_ref[...] = result.astype(bf16).reshape(out_ref.shape)
 
 
 def shards(
@@ -458,6 +477,7 @@
         *integers, queries, fresh, adapter_down_weight, residual, pool
     )
     came = lax.ppermute(leave, "replica", swap)
+    rows_in_order = sort_call(turn, stay, came)
     spans = tensor // QUAD
     def trade(message, partners):
         pairs = [
@@ -467,20 +487,12 @@
         ]
         return lax.ppermute(message, ("replica", "tensor"), pairs)
 
-    def message(came, partners, chosen, dtype=bf16):
-        return message_call(stay, came, output_weight, partners, chosen, dtype)
-
-    every = tuple(range(spans))
-    early = len(PARTNERS) - LATE
-    sent = [
-        message(came, partners, every if n < early else every[1:])
-        for n, partners in enumerate(PARTNERS)
+    collected = [
+        trade(message_call(rows_in_order, came, output_weight, partners, bf16), partners)
+        for partners in PARTNERS
     ]
-    collected = [trade(*item) for item in zip(sent, PARTNERS)]
-    own = message(came, (0, 0), every, f32)
-    came_later, *_ = lax.optimization_barrier((came, *sent))
-    home = [own] + collected[:early]
-    home += [trade(message(came_later, partners, HOME), partners) for partners in PARTNERS[early:]]
+    own = message_call(rows_in_order, came, output_weight, (0, 0), f32)
+    home = [own] + collected
     other_pool = lax.ppermute(pool, "replica", swap)
     placed = place_call(*integers[:3], pool, rows)
     placed, own = lax.optimization_barrier((placed, own))
@@ -488,16 +500,16 @@
     *across, shrink = merge_call([own] + collected, spans)
     across = [trade(piece, (n * QUAD, n * QUAD)) for n, piece in enumerate(across, 1)]
     placed_cache = place_call(*integers[:3], other_pool, rows, placed)
-    placed_cache, turn = lax.optimization_barrier((placed_cache, turn))
+    placed_cache, slot = lax.optimization_barrier((placed_cache, slot))
     vmem = pl.BlockSpec(memory_space=pltpu.VMEM)
     layer_out = pl.pallas_call(
         functools.partial(finish_kernel, home_count=len(home)),
         out_shape=jax.ShapeDtypeStruct((steps, rows, features), bf16),
-        in_specs=[vmem] * (7 + len(home) + len(across)),
+        in_specs=[vmem] * (5 + len(home) + len(across)),
         out_specs=vmem,
         compiler_params=pltpu.CompilerParams(vmem_limit_bytes=SMALL_BYTES),
         name="finish",
-    )(turn, slot, adapter_up_weight, other_up, stay, came, shrink, *home, *across)
+    )(slot, adapter_up_weight, other_up, rows_in_order, shrink, *home, *across)
     return (layer_out, placed_cache.reshape(rows, table_blocks, 1, block_size, width))
 
 

time: 26.8 us -> 26.6 us (level)
  Pallas kernels: 14.2 us -> 13.9 us
  local copies, waits for them, and re-layouts: 0.05 us -> 0.33 us
    pallas_call x1, Pallas kernels: 5.85 us -> 5.39 us  [attend_call(): pl.pallas_call(attend_kernel, out_shape=(pltpu.VMEM((steps * rows // 2, 2...]
    unnamed x16, local copies, waits for them, and re-layouts: 0.05 us -> 0.33 us
    pallas_call x4 -> x5, Pallas kernels: 3.3 us -> 3.42 us  [the longest x4 3.25 us: message_call(): pl.pallas_call(functools.partial(message_kernel, partners=partners), out_...]
  transfers between devices with their start and end apart: 7 -> 7, of which waited for: 4 -> 4; matrix products, arithmetic and copies ran while one was open for 0% -> 0% of each run, Pallas kernels for 24% -> 25%
where the time goes in v6:
time: 26.6 us; the launch traced here: 26.4 us
  Pallas kernels  13.9 us (52%)
  starting transfers between devices  8.36 us (31%)
  waiting for transfers between devices  3.13 us (12%)
  between operations  0.75 us (3%)
  local copies, waits for them, and re-layouts  0.33 us (1%)
    ppermute x4, starting transfers between devices, trade(): return lax.ppermute(message, ('replica', 'tensor'), pairs)  7.33 us
    pallas_call x1, Pallas kernels, attend_call(): pl.pallas_call(attend_kernel, out_shape=(pltpu.VMEM((steps * rows // 2, 2...  5.39 us
    pallas_call x2, Pallas kernels, place_call(): pl.pallas_call(functools.partial(place_kernel, stayed=placed is None), ou...  3.99 us
    pallas_call x4, Pallas kernels, message_call(): pl.pallas_call(functools.partial(message_kernel, partners=partners), out_...  3.25 us
    ppermute x4, waiting for transfers between devices, trade(): return lax.ppermute(message, ('replica', 'tensor'), pairs)  2.22 us
    pallas_call x1, Pallas kernels, shards(): pl.pallas_call(functools.partial(finish_kernel, home_count=len(home)), ou...  1.03 us
    ppermute x1, waiting for transfers between devices, shards(): came = lax.ppermute(leave, 'replica', swap)  0.91 us
  transfers between devices with their start and end apart: 7, of which 4 were waited for; matrix products, arithmetic and copies ran while one was open for 0% of the time, Pallas kernels for 25%

profile of v6, /device:TPU:0, one launch (start us, length us, event | category | flops | bytes accessed | tf_op | source)
XLA Modules:
  0.0 26.4 jit_solution(5549537775646106076)
XLA Ops:
  0.6 0.0 slice-start
  0.6 0.0 slice-start.1
  0.7 0.0 slice-start.2
  0.7 0.0 slice-start.3
  0.7 5.4 %attend.1 = (bf16[16,2176]{1,0:T(8,128)(2,1)S(1)}, bf16[16,2176]{1,0:T(8,128)(2,1)S(1)}, bf16[32,32]{1,0:T(8,128)(2,1)S(1)}, f32[32,8]{1,0:T(8,128)S(1)}, bf16[128,64,256]{2,1,0:T(8,128)(2,1)S(1)}) custom-call(s32[32]{0:T(128)} %order_ref.5, s32[32]{0:T(128)} %lengths_ref.5, s32[8,32]{1,0:T(8,128)} %bitcast.8, s32[32]{0:T(128)} %adapter_ref.1, ...), custom_call_target="tpu_custom_call" | custom-call | flops 40000000000 | bytes 8388608 | tf_op jit(solution)/shard_map/attend/pallas_call | solution.py:333
  6.1 0.5 %collective-permute-start.1 = (bf16[16,2176]{1,0:T(8,128)(2,1)S(1)}, bf16[16,2176]{1,0:T(8,128)(2,1)S(1)}, u32[]{:S(2)}, u32[]{:S(2)}) collective-permute-start(bf16[16,2176]{1,0:T(8,128)(2,1)S(1)} %get-tuple-element.16), channel_id=1, source_target_pairs={{0,8},{8,0},{1,9},{9,1},{2,10},{10,2},{3,11},{11,3},{4,12},{12,4},... | collective-permute-start | bytes 208904 | tf_op jit(solution)/shard_map/ppermute | solution.py:479
  6.6 0.9 %collective-permute-done.1.came_ref = bf16[16,2176]{1,0:T(8,128)(2,1)S(1)} collective-permute-done((bf16[16,2176]{1,0:T(8,128)(2,1)S(1)}, bf16[16,2176]{1,0:T(8,128)(2,1)S(1)}, u32[]{:S(2)}, u32[]{:S(2)}) %collective-permute-start.1) | collective-permute-done | bytes 69664 | tf_op jit(solution)/shard_map/ppermute | solution.py:479
  7.5 0.2 sort.1.rows_ref
  7.7 0.0 slice-done
  7.7 0.3 %slice-done.3 = s8[4194304]{0:T(1024)(128)(4,1)S(1)} async-done(((s8[16777216]{0:T(1024)(128)(4,1)}), s8[4194304]{0:T(1024)(128)(4,1)S(1)}, s32[]{:S(2)}) %slice-start.3) | async-done | bytes 4194328
  8.0 0.8 %message.5 = bf16[32,2176]{1,0:T(8,128)(2,1)S(1)} custom-call(bf16[32,2176]{1,0:T(8,128)(2,1)S(1)} %sort.1.rows_ref, bf16[16,2176]{1,0:T(8,128)(2,1)S(1)} %collective-permute-done.1.came_ref, bf16[1024,8192]{1,0:T(8,128)(2,1)S(1)} %bitcast.7), custom_call_target="tpu_custom_call" | custom-call | tf_op jit(solution)/shard_map/message/pallas_call | solution.py:370
  8.8 4.0 %collective-permute-start.3 = (bf16[32,2176]{1,0:T(8,128)(2,1)S(1)}, bf16[32,2176]{1,0:T(8,128)(2,1)S(1)}, u32[]{:S(2)}, u32[]{:S(2)}) collective-permute-start(bf16[32,2176]{1,0:T(8,128)(2,1)S(1)} %message.5), channel_id=1, source_target_pairs={{0,3},{1,2},{2,1},{3,0},{4,7},{5,6},{6,5},{7,4},{8,11},{9,10},{10,... | collective-permute-start | bytes 417800 | tf_op jit(solution)/shard_map/ppermute | solution.py:488
  12.8 0.8 %message.6 = bf16[32,2176]{1,0:T(8,128)(2,1)S(1)} custom-call(bf16[32,2176]{1,0:T(8,128)(2,1)S(1)} %sort.1.rows_ref, bf16[16,2176]{1,0:T(8,128)(2,1)S(1)} %collective-permute-done.1.came_ref, bf16[1024,8192]{1,0:T(8,128)(2,1)S(1)} %bitcast.7), custom_call_target="tpu_custom_call" | custom-call | tf_op jit(solution)/shard_map/message/pallas_call | solution.py:370
  13.6 0.0 copy-start.1
  13.6 0.0 copy-start.2
  13.6 0.0 copy-start.3
  13.6 0.5 %collective-permute-start.4 = (bf16[32,2176]{1,0:T(8,128)(2,1)S(1)}, bf16[32,2176]{1,0:T(8,128)(2,1)S(1)}, u32[]{:S(2)}, u32[]{:S(2)}) collective-permute-start(bf16[32,2176]{1,0:T(8,128)(2,1)S(1)} %message.6), channel_id=1, source_target_pairs={{0,2},{1,3},{2,0},{3,1},{4,6},{5,7},{6,4},{7,5},{8,10},{9,11},{10,... | collective-permute-start | bytes 417800 | tf_op jit(solution)/shard_map/ppermute | solution.py:488
  14.2 0.8 %message.7 = bf16[32,2176]{1,0:T(8,128)(2,1)S(1)} custom-call(bf16[32,2176]{1,0:T(8,128)(2,1)S(1)} %sort.1.rows_ref, bf16[16,2176]{1,0:T(8,128)(2,1)S(1)} %collective-permute-done.1.came_ref, bf16[1024,8192]{1,0:T(8,128)(2,1)S(1)} %bitcast.7), custom_call_target="tpu_custom_call" | custom-call | tf_op jit(solution)/shard_map/message/pallas_call | solution.py:370
  15.0 0.1 collective-permute-start.5
  15.1 0.0 collective-permute-start
  15.1 0.5 %collective-permute-start.2 = (bf16[4,64,1024]{2,1,0:T(8,128)(2,1)S(1)}, bf16[4,64,1024]{2,1,0:T(8,128)(2,1)S(1)}, u32[]{:S(2)}, u32[]{:S(2)}) collective-permute-start(bf16[4,64,1024]{2,1,0:T(8,128)(2,1)S(1)} %copy-done), channel_id=1, source_target_pairs={{0,8},{8,0},{1,9},{9,1},{2,10},{10,2},{3,11},{11,3},{4,12},{12,4},... | collective-permute-start | bytes 1572872 | tf_op jit(solution)/shard_map/ppermute | solution.py:472
  15.6 2.0 %place.2.refs_0_ = bf16[16,8,64,256]{3,2,1,0:T(8,128)(2,1)} custom-call(s32[32]{0:T(128)S(1)} %copy-done.2, s32[32]{0:T(128)S(1)} %copy-done.3, s32[8,32]{1,0:T(8,128)S(1)} %bitcast.9, bf16[128,64,256]{2,1,0:T(8,128)(2,1)S(1)} %get-tuple-element.13.pool_v), custom_call_target="tpu_custom_call" | custom-call | bytes 4194304 | tf_op jit(solution)/shard_map/place/pallas_call | solution.py:385
  17.6 0.8 %message.4.refs_0_.rest_0_ = f32[32,2176]{1,0:T(8,128)S(1)} custom-call(bf16[32,2176]{1,0:T(8,128)(2,1)S(1)} %sort.1.rows_ref, bf16[16,2176]{1,0:T(8,128)(2,1)S(1)} %collective-permute-done.1.came_ref, bf16[1024,8192]{1,0:T(8,128)(2,1)S(1)} %bitcast.7), custom_call_target="tpu_custom_call" | custom-call | tf_op jit(solution)/shard_map/message/pallas_call | solution.py:370
  18.4 0.0 collective-permute-done.3.refs_1_.rest_1_
  18.4 1.2 %collective-permute-done.4.refs_2_.rest_2_ = bf16[32,2176]{1,0:T(8,128)(2,1)S(1)} collective-permute-done((bf16[32,2176]{1,0:T(8,128)(2,1)S(1)}, bf16[32,2176]{1,0:T(8,128)(2,1)S(1)}, u32[]{:S(2)}, u32[]{:S(2)}) %collective-permute-start.4) | collective-permute-done | bytes 139296 | tf_op jit(solution)/shard_map/ppermute | solution.py:488
  19.6 0.4 %collective-permute-done.5.refs_3_.rest_3_ = bf16[32,2176]{1,0:T(8,128)(2,1)S(1)} collective-permute-done((bf16[32,2176]{1,0:T(8,128)(2,1)S(1)}, bf16[32,2176]{1,0:T(8,128)(2,1)S(1)}, u32[]{:S(2)}, u32[]{:S(2)}) %collective-permute-start.5) | collective-permute-done | bytes 139296 | tf_op jit(solution)/shard_map/ppermute | solution.py:488
  20.1 2.7 %collective-permute-start.6 = (bf16[32,1152]{1,0:T(8,128)(2,1)S(1)}, bf16[32,1152]{1,0:T(8,128)(2,1)S(1)}, u32[]{:S(2)}, u32[]{:S(2)}) collective-permute-start(bf16[32,1152]{1,0:T(8,128)(2,1)S(1)} %get-tuple-element.22), channel_id=1, source_target_pairs={{0,4},{1,5},{2,6},{3,7},{4,0},{5,1},{6,2},{7,3},{8,12},{9,13},{10,... | collective-permute-start | bytes 221192 | tf_op jit(solution)/shard_map/ppermute | solution.py:488
  22.8 0.0 collective-permute-done.pool_v
  22.8 2.0 %place.3 = bf16[16,8,64,256]{3,2,1,0:T(8,128)(2,1)} custom-call(s32[32]{0:T(128)S(1)} %copy-done.2, s32[32]{0:T(128)S(1)} %copy-done.3, s32[8,32]{1,0:T(8,128)S(1)} %bitcast.10, bf16[128,64,256]{2,1,0:T(8,128)(2,1)S(1)} %collective-permute-done.pool_v, bf16[16,8,64,256]{3,2,1,0:T(8,128)(2,1)} %place.2.refs_0_), custom_call_target="tpu_custom_call", output_to_operand_aliasing={{}: (4, {})} | custom-call | bytes 4194304 | tf_op jit(solution)/shard_map/place/pallas_call | solution.py:385
  24.8 0.6 %collective-permute-done.6.rest_4_ = bf16[32,1152]{1,0:T(8,128)(2,1)S(1)} collective-permute-done((bf16[32,1152]{1,0:T(8,128)(2,1)S(1)}, bf16[32,1152]{1,0:T(8,128)(2,1)S(1)}, u32[]{:S(2)}, u32[]{:S(2)}) %collective-permute-start.6) | collective-permute-done | bytes 73760 | tf_op jit(solution)/shard_map/ppermute | solution.py:488
  25.4 0.0 collective-permute-done.2.other_up_ref
  25.4 1.0 %finish.1 = bf16[2,16,1024]{2,1,0:T(8,128)(2,1)} custom-call(f32[32,8]{1,0:T(8,128)S(1)} %get-tuple-element.19.slot_ref, bf16[4,64,1024]{2,1,0:T(8,128)(2,1)S(1)} %copy-done, bf16[4,64,1024]{2,1,0:T(8,128)(2,1)S(1)} %collective-permute-done.2.other_up_ref, bf16[32,2176]{1,0:T(8,128)(2,1)S(1)} %sort.1.rows_ref, f32[32,128]{1,0:T(8,128)S(1)} %get-tuple-element.21.shrink_ref, ...), custom_call_target="tpu_custom_call" | custom-call | tf_op jit(solution)/shard_map/finish/pallas_call | solution.py:505
  (9 shorter events, 0.1 us)
Async XLA Ops:
  0.6 7.0 %slice-start = ((s8[16777216]{0:T(1024)(128)(4,1)}), s8[4194304]{0:T(1024)(128)(4,1)S(1)}, s32[]{:S(2)}) async-start(s8[16777216]{0:T(1024)(128)(4,1)} %bitcast.6), calls=%async_computation | async-start | bytes 8388608
  0.6 7.0 %slice-start.1 = ((s8[16777216]{0:T(1024)(128)(4,1)}), s8[4194304]{0:T(1024)(128)(4,1)S(1)}, s32[]{:S(2)}) async-start(s8[16777216]{0:T(1024)(128)(4,1)} %bitcast.6), calls=%async_computation.1 | async-start | bytes 8388608
  0.7 7.0 %slice-start.2 = ((s8[16777216]{0:T(1024)(128)(4,1)}), s8[4194304]{0:T(1024)(128)(4,1)S(1)}, s32[]{:S(2)}) async-start(s8[16777216]{0:T(1024)(128)(4,1)} %bitcast.6), calls=%async_computation.2 | async-start | bytes 8388608
  0.7 7.3 %slice-start.3 = ((s8[16777216]{0:T(1024)(128)(4,1)}), s8[4194304]{0:T(1024)(128)(4,1)S(1)}, s32[]{:S(2)}) async-start(s8[16777216]{0:T(1024)(128)(4,1)} %bitcast.6), calls=%async_computation.3 | async-start | bytes 8388608
  6.1 1.4 %collective-permute-start.1 = (bf16[16,2176]{1,0:T(8,128)(2,1)S(1)}, bf16[16,2176]{1,0:T(8,128)(2,1)S(1)}, u32[]{:S(2)}, u32[]{:S(2)}) collective-permute-start(bf16[16,2176]{1,0:T(8,128)(2,1)S(1)} %get-tuple-element.16), channel_id=1, source_target_pairs={{0,8},{8,0},{1,9},{9,1},{2,10},{10,2},{3,11},{11,3},{4,12},{12,4},... | collective-permute-start | bytes 208904 | tf_op jit(solution)/shard_map/ppermute | solution.py:479
  8.8 9.6 %collective-permute-start.3 = (bf16[32,2176]{1,0:T(8,128)(2,1)S(1)}, bf16[32,2176]{1,0:T(8,128)(2,1)S(1)}, u32[]{:S(2)}, u32[]{:S(2)}) collective-permute-start(bf16[32,2176]{1,0:T(8,128)(2,1)S(1)} %message.5), channel_id=1, source_target_pairs={{0,3},{1,2},{2,1},{3,0},{4,7},{5,6},{6,5},{7,4},{8,11},{9,10},{10,... | collective-permute-start | bytes 417800 | tf_op jit(solution)/shard_map/ppermute | solution.py:488
  13.6 1.5 %copy-start = (bf16[4,64,1024]{2,1,0:T(8,128)(2,1)S(1)}, bf16[4,64,1024]{2,1,0:T(8,128)(2,1)}, u32[]{:S(2)}) copy-start(bf16[4,64,1024]{2,1,0:T(8,128)(2,1)} %up_ref.1) | copy-start | bytes 1572868
  13.6 2.0 %copy-start.1 = (s32[32,8]{0,1:T(8,128)S(1)}, s32[32,8]{0,1:T(8,128)}, u32[]{:S(2)}) copy-start(s32[32,8]{0,1:T(8,128)} %param.19) | copy-start | bytes 3076
  13.6 2.0 %copy-start.2 = (s32[32]{0:T(128)S(1)}, s32[32]{0:T(128)}, u32[]{:S(2)}) copy-start(s32[32]{0:T(128)} %order_ref.5) | copy-start | bytes 388
  13.6 2.0 %copy-start.3 = (s32[32]{0:T(128)S(1)}, s32[32]{0:T(128)}, u32[]{:S(2)}) copy-start(s32[32]{0:T(128)} %lengths_ref.5) | copy-start | bytes 388
  13.6 6.0 %collective-permute-start.4 = (bf16[32,2176]{1,0:T(8,128)(2,1)S(1)}, bf16[32,2176]{1,0:T(8,128)(2,1)S(1)}, u32[]{:S(2)}, u32[]{:S(2)}) collective-permute-start(bf16[32,2176]{1,0:T(8,128)(2,1)S(1)} %message.6), channel_id=1, source_target_pairs={{0,2},{1,3},{2,0},{3,1},{4,6},{5,7},{6,4},{7,5},{8,10},{9,11},{10,... | collective-permute-start | bytes 417800 | tf_op jit(solution)/shard_map/ppermute | solution.py:488
  15.0 5.1 %collective-permute-start.5 = (bf16[32,2176]{1,0:T(8,128)(2,1)S(1)}, bf16[32,2176]{1,0:T(8,128)(2,1)S(1)}, u32[]{:S(2)}, u32[]{:S(2)}) collective-permute-start(bf16[32,2176]{1,0:T(8,128)(2,1)S(1)} %message.7), channel_id=1, source_target_pairs={{0,1},{1,0},{2,3},{3,2},{4,5},{5,4},{6,7},{7,6},{8,9},{9,8},{10,11... | collective-permute-start | bytes 417800 | tf_op jit(solution)/shard_map/ppermute | solution.py:488
  15.1 7.7 %collective-permute-start = (bf16[128,64,256]{2,1,0:T(8,128)(2,1)S(1)}, bf16[128,64,256]{2,1,0:T(8,128)(2,1)S(1)}, u32[]{:S(2)}, u32[]{:S(2)}) collective-permute-start(bf16[128,64,256]{2,1,0:T(8,128)(2,1)S(1)} %get-tuple-element.13.pool_v), channel_id=1, source_target_pairs={{0,8},{8,0},{1,9},{9,1},{2,10},{10,2},{3,11},{11,3},{4,12},{12,4},... | collective-permute-start | bytes 12582920 | tf_op jit(solution)/shard_map/ppermute | solution.py:496
  15.1 10.3 %collective-permute-start.2 = (bf16[4,64,1024]{2,1,0:T(8,128)(2,1)S(1)}, bf16[4,64,1024]{2,1,0:T(8,128)(2,1)S(1)}, u32[]{:S(2)}, u32[]{:S(2)}) collective-permute-start(bf16[4,64,1024]{2,1,0:T(8,128)(2,1)S(1)} %copy-done), channel_id=1, source_target_pairs={{0,8},{8,0},{1,9},{9,1},{2,10},{10,2},{3,11},{11,3},{4,12},{12,4},... | collective-permute-start | bytes 1572872 | tf_op jit(solution)/shard_map/ppermute | solution.py:472
  20.1 5.3 %collective-permute-start.6 = (bf16[32,1152]{1,0:T(8,128)(2,1)S(1)}, bf16[32,1152]{1,0:T(8,128)(2,1)S(1)}, u32[]{:S(2)}, u32[]{:S(2)}) collective-permute-start(bf16[32,1152]{1,0:T(8,128)(2,1)S(1)} %get-tuple-element.22), channel_id=1, source_target_pairs={{0,4},{1,5},{2,6},{3,7},{4,0},{5,1},{6,2},{7,3},{8,12},{9,13},{10,... | collective-permute-start | bytes 221192 | tf_op jit(solution)/shard_map/ppermute | solution.py:488

commit v7 on v6

--- a/solution.py
+++ b/solution.py
@@ -261,16 +261,20 @@
 def message_kernel(rows_ref, came_ref, weight_ref, message_ref, *, partners):
     out_width = weight_ref.shape[1] // lax.axis_size("tensor")
     features = weight_ref.shape[0]
-    spans = message_ref.shape[1] // out_width
+    spans = message_ref.shape[1] // (2 * out_width)
     here = lax.axis_index("tensor")
     partner = jnp.where(lax.axis_index("replica") == 0, partners[0], partners[1])
+    half = message_ref.shape[0]
     mixed = rows_ref[:, :features]
     for span in range(spans):
         start = pl.multiple_of((here ^ (span * QUAD + partner)) * out_width, out_width)
-        part = dot(mixed, weight_ref[:, pl.ds(start, out_width)])
-        message_ref[:, span * out_width : (span + 1) * out_width] = part.astype(message_ref.dtype)
-    shrink = rows_ref[:, features : features + LANES]
-    message_ref[:, spans * out_width :] = shrink.astype(message_ref.dtype)
+        part = dot(mixed, weight_ref[:, pl.ds(start, out_width)]).astype(message_ref.dtype)
+        for side in range(2):
+            column = (2 * span + side) * out_width
+            message_ref[:, column : column + out_width] = part[side * half : (side + 1) * half]
+    rank = LANES // 2
+    shrink = rows_ref[:, features : features + rank].astype(message_ref.dtype)
+    message_ref[:, 2 * spans * out_width :] = jnp.concatenate([shrink[:half], shrink[half:]], axis=1)
 
 
 def place_kernel(order_ref, lengths_ref, table_ref, pool_v, *refs, stayed):
@@ -365,11 +369,11 @@
 
 def message_call(rows, came, weight, partners, dtype):
     tensor = lax.axis_size("tensor")
-    columns = tensor // QUAD * weight.shape[1] // tensor
+    columns = 2 * (tensor // QUAD) * (weight.shape[1] // tensor)
     vmem = pl.BlockSpec(memory_space=pltpu.VMEM)
     return pl.pallas_call(
         functools.partial(message_kernel, partners=partners),
-        out_shape=pltpu.VMEM((rows.shape[0], columns + LANES), dtype),
+        out_shape=pltpu.VMEM((rows.shape[0] // 2, columns + LANES), dtype),
         in_specs=[vmem] * 3,
         out_specs=vmem,
         compiler_params=pltpu.CompilerParams(vmem_limit_bytes=SMALL_BYTES),
@@ -399,26 +403,26 @@
     )(order, lengths, table, pool, *before)
 
 
-def merge_kernel(*refs, spans, out_width):
+def merge_kernel(*refs, spans):
     messages, outs, shrink_ref = refs[:-spans], refs[-spans:-1], refs[-1]
-    columns = (spans - 1) * out_width + LANES
-    total = messages[0][:, out_width:]
+    width = (messages[0].shape[1] - LANES) // spans
+    total = messages[0][:, width:]
     for ref in messages[1:]:
-        total = total + ref[:, ref.shape[1] - columns :].astype(f32)
-    shrink = total[:, (spans - 1) * out_width :]
+        total = total + ref[:, width:].astype(f32)
+    shrink = total[:, (spans - 1) * width :]
     shrink_ref[...] = shrink
     for n, ref in enumerate(outs):
-        ref[:, :out_width] = total[:, n * out_width : (n + 1) * out_width].astype(bf16)
-        ref[:, out_width:] = shrink.astype(bf16)
+        ref[:, :width] = total[:, n * width : (n + 1) * width].astype(bf16)
+        ref[:, width:] = shrink.astype(bf16)
 
 
 def merge_call(messages, spans):
     rows, columns = messages[0].shape
     vmem = pl.BlockSpec(memory_space=pltpu.VMEM)
-    out_width = (columns - LANES) // spans
+    width = (columns - LANES) // spans
     return pl.pallas_call(
-        functools.partial(merge_kernel, spans=spans, out_width=out_width),
-        out_shape=[pltpu.VMEM((rows, out_width + LANES), bf16)] * (spans - 1)
+        functools.partial(merge_kernel, spans=spans),
+        out_shape=[pltpu.VMEM((rows, width + LANES), bf16)] * (spans - 1)
         + [pltpu.VMEM((rows, LANES), f32)],
         in_specs=[vmem] * len(messages),
         out_specs=[vmem] * spans,
@@ -431,12 +435,15 @@
 def finish_kernel(slot_ref, up_ref, other_up_ref, rows_ref, shrink_ref, *rest, home_count):
     home_refs, across_refs, out_ref = rest[:home_count], rest[home_count:-1], rest[-1]
     slots, rank, features = up_ref.shape
-    total, shrink = home_refs[0][:, :features], shrink_ref[:, :rank]
+    width = 2 * features
+    total, shrink = home_refs[0][:, :width], shrink_ref[...]
     for ref in home_refs[1:]:
-        total = total + ref[:, :features].astype(f32)
+        total = total + ref[:, :width].astype(f32)
     for ref in across_refs:
-        total = total + ref[:, :features].astype(f32)
-        shrink = shrink + ref[:, features : features + rank].astype(f32)
+        total = total + ref[:, :width].astype(f32)
+        shrink = shrink + ref[:, width:].astype(f32)
+    total = jnp.concatenate([total[:, :features], total[:, features:]], axis=0)
+    shrink = jnp.concatenate([shrink[:, :rank], shrink[:, LANES // 2 : LANES // 2 + rank]], axis=0)
     shrink = shrink.astype(bf16).astype(f32)
     result = total + rows_ref[:, features + LANES :].astype(f32)
     for side, up in enumerate((up_ref, other_up_ref)):

time: 26.6 us -> 26.5 us (level)
  no operation moved by 1% of the time
where the time goes in v7:
time: 26.5 us; the launch traced here: 26.4 us
  Pallas kernels  13.9 us (52%)
  starting transfers between devices  8.32 us (31%)
  waiting for transfers between devices  3.06 us (12%)
  between operations  0.75 us (3%)
  local copies, waits for them, and re-layouts  0.33 us (1%)
    ppermute x4, starting transfers between devices, trade(): return lax.ppermute(message, ('replica', 'tensor'), pairs)  7.3 us
    pallas_call x1, Pallas kernels, attend_call(): pl.pallas_call(attend_kernel, out_shape=(pltpu.VMEM((steps * rows // 2, 2...  5.39 us
    pallas_call x2, Pallas kernels, place_call(): pl.pallas_call(functools.partial(place_kernel, stayed=placed is None), ou...  4 us
    pallas_call x4, Pallas kernels, message_call(): pl.pallas_call(functools.partial(message_kernel, partners=partners), out_...  3.29 us
    ppermute x4, waiting for transfers between devices, trade(): return lax.ppermute(message, ('replica', 'tensor'), pairs)  2.15 us
    pallas_call x1, Pallas kernels, shards(): pl.pallas_call(functools.partial(finish_kernel, home_count=len(home)), ou...  1.03 us
    ppermute x1, waiting for transfers between devices, shards(): came = lax.ppermute(leave, 'replica', swap)  0.91 us
  transfers between devices with their start and end apart: 7, of which 4 were waited for; matrix products, arithmetic and copies ran while one was open for 0% of the time, Pallas kernels for 25%

profile of v7, /device:TPU:0, one launch (start us, length us, event | category | flops | bytes accessed | tf_op | source)
XLA Modules:
  0.0 26.4 jit_solution(8814591776115950761)
XLA Ops:
  0.6 0.0 slice-start
  0.6 0.0 slice-start.1
  0.7 0.0 slice-start.2
  0.7 0.0 slice-start.3
  0.7 5.4 %attend.1 = (bf16[16,2176]{1,0:T(8,128)(2,1)S(1)}, bf16[16,2176]{1,0:T(8,128)(2,1)S(1)}, bf16[32,32]{1,0:T(8,128)(2,1)S(1)}, f32[32,8]{1,0:T(8,128)S(1)}, bf16[128,64,256]{2,1,0:T(8,128)(2,1)S(1)}) custom-call(s32[32]{0:T(128)} %order_ref.5, s32[32]{0:T(128)} %lengths_ref.5, s32[8,32]{1,0:T(8,128)} %bitcast.8, s32[32]{0:T(128)} %adapter_ref.1, ...), custom_call_target="tpu_custom_call" | custom-call | flops 40000000000 | bytes 8388608 | tf_op jit(solution)/shard_map/attend/pallas_call | solution.py:337
  6.1 0.5 %collective-permute-start.1 = (bf16[16,2176]{1,0:T(8,128)(2,1)S(1)}, bf16[16,2176]{1,0:T(8,128)(2,1)S(1)}, u32[]{:S(2)}, u32[]{:S(2)}) collective-permute-start(bf16[16,2176]{1,0:T(8,128)(2,1)S(1)} %get-tuple-element.16), channel_id=1, source_target_pairs={{0,8},{8,0},{1,9},{9,1},{2,10},{10,2},{3,11},{11,3},{4,12},{12,4},... | collective-permute-start | bytes 208904 | tf_op jit(solution)/shard_map/ppermute | solution.py:486
  6.6 0.9 %collective-permute-done.1.came_ref = bf16[16,2176]{1,0:T(8,128)(2,1)S(1)} collective-permute-done((bf16[16,2176]{1,0:T(8,128)(2,1)S(1)}, bf16[16,2176]{1,0:T(8,128)(2,1)S(1)}, u32[]{:S(2)}, u32[]{:S(2)}) %collective-permute-start.1) | collective-permute-done | bytes 69664 | tf_op jit(solution)/shard_map/ppermute | solution.py:486
  7.5 0.2 sort.1.rows_ref
  7.7 0.3 %slice-done.3 = s8[4194304]{0:T(1024)(128)(4,1)S(1)} async-done(((s8[16777216]{0:T(1024)(128)(4,1)}), s8[4194304]{0:T(1024)(128)(4,1)S(1)}, s32[]{:S(2)}) %slice-start.3) | async-done | bytes 4194328
  8.0 0.8 %message.5 = bf16[16,4224]{1,0:T(8,128)(2,1)S(1)} custom-call(bf16[32,2176]{1,0:T(8,128)(2,1)S(1)} %sort.1.rows_ref, bf16[16,2176]{1,0:T(8,128)(2,1)S(1)} %collective-permute-done.1.came_ref, bf16[1024,8192]{1,0:T(8,128)(2,1)S(1)} %bitcast.7), custom_call_target="tpu_custom_call" | custom-call | tf_op jit(solution)/shard_map/message/pallas_call | solution.py:374
  8.8 4.0 %collective-permute-start.3 = (bf16[16,4224]{1,0:T(8,128)(2,1)S(1)}, bf16[16,4224]{1,0:T(8,128)(2,1)S(1)}, u32[]{:S(2)}, u32[]{:S(2)}) collective-permute-start(bf16[16,4224]{1,0:T(8,128)(2,1)S(1)} %message.5), channel_id=1, source_target_pairs={{0,3},{1,2},{2,1},{3,0},{4,7},{5,6},{6,5},{7,4},{8,11},{9,10},{10,... | collective-permute-start | bytes 405512 | tf_op jit(solution)/shard_map/ppermute | solution.py:495
  12.8 0.8 %message.6 = bf16[16,4224]{1,0:T(8,128)(2,1)S(1)} custom-call(bf16[32,2176]{1,0:T(8,128)(2,1)S(1)} %sort.1.rows_ref, bf16[16,2176]{1,0:T(8,128)(2,1)S(1)} %collective-permute-done.1.came_ref, bf16[1024,8192]{1,0:T(8,128)(2,1)S(1)} %bitcast.7), custom_call_target="tpu_custom_call" | custom-call | tf_op jit(solution)/shard_map/message/pallas_call | solution.py:374
  13.6 0.0 copy-start.1
  13.6 0.0 copy-start.2
  13.7 0.0 copy-start.3
  13.7 0.5 %collective-permute-start.4 = (bf16[16,4224]{1,0:T(8,128)(2,1)S(1)}, bf16[16,4224]{1,0:T(8,128)(2,1)S(1)}, u32[]{:S(2)}, u32[]{:S(2)}) collective-permute-start(bf16[16,4224]{1,0:T(8,128)(2,1)S(1)} %message.6), channel_id=1, source_target_pairs={{0,2},{1,3},{2,0},{3,1},{4,6},{5,7},{6,4},{7,5},{8,10},{9,11},{10,... | collective-permute-start | bytes 405512 | tf_op jit(solution)/shard_map/ppermute | solution.py:495
  14.2 0.8 %message.7 = bf16[16,4224]{1,0:T(8,128)(2,1)S(1)} custom-call(bf16[32,2176]{1,0:T(8,128)(2,1)S(1)} %sort.1.rows_ref, bf16[16,2176]{1,0:T(8,128)(2,1)S(1)} %collective-permute-done.1.came_ref, bf16[1024,8192]{1,0:T(8,128)(2,1)S(1)} %bitcast.7), custom_call_target="tpu_custom_call" | custom-call | tf_op jit(solution)/shard_map/message/pallas_call | solution.py:374
  15.0 0.1 collective-permute-start.5
  15.1 0.0 collective-permute-start
  15.1 0.5 %collective-permute-start.2 = (bf16[4,64,1024]{2,1,0:T(8,128)(2,1)S(1)}, bf16[4,64,1024]{2,1,0:T(8,128)(2,1)S(1)}, u32[]{:S(2)}, u32[]{:S(2)}) collective-permute-start(bf16[4,64,1024]{2,1,0:T(8,128)(2,1)S(1)} %copy-done), channel_id=1, source_target_pairs={{0,8},{8,0},{1,9},{9,1},{2,10},{10,2},{3,11},{11,3},{4,12},{12,4},... | collective-permute-start | bytes 1572872 | tf_op jit(solution)/shard_map/ppermute | solution.py:479
  15.7 0.0 copy-done.1
  15.7 2.0 %place.2.refs_0_ = bf16[16,8,64,256]{3,2,1,0:T(8,128)(2,1)} custom-call(s32[32]{0:T(128)S(1)} %copy-done.2, s32[32]{0:T(128)S(1)} %copy-done.3, s32[8,32]{1,0:T(8,128)S(1)} %bitcast.9, bf16[128,64,256]{2,1,0:T(8,128)(2,1)S(1)} %get-tuple-element.13.pool_v), custom_call_target="tpu_custom_call" | custom-call | bytes 4194304 | tf_op jit(solution)/shard_map/place/pallas_call | solution.py:389
  17.7 0.8 %message.4.refs_0_.rest_0_ = f32[16,4224]{1,0:T(8,128)S(1)} custom-call(bf16[32,2176]{1,0:T(8,128)(2,1)S(1)} %sort.1.rows_ref, bf16[16,2176]{1,0:T(8,128)(2,1)S(1)} %collective-permute-done.1.came_ref, bf16[1024,8192]{1,0:T(8,128)(2,1)S(1)} %bitcast.7), custom_call_target="tpu_custom_call" | custom-call | tf_op jit(solution)/shard_map/message/pallas_call | solution.py:374
  18.5 0.0 collective-permute-done.3.refs_1_.rest_1_
  18.5 1.0 %collective-permute-done.4.refs_2_.rest_2_ = bf16[16,4224]{1,0:T(8,128)(2,1)S(1)} collective-permute-done((bf16[16,4224]{1,0:T(8,128)(2,1)S(1)}, bf16[16,4224]{1,0:T(8,128)(2,1)S(1)}, u32[]{:S(2)}, u32[]{:S(2)}) %collective-permute-start.4) | collective-permute-done | bytes 135200 | tf_op jit(solution)/shard_map/ppermute | solution.py:495
  19.4 0.6 %collective-permute-done.5.refs_3_.rest_3_ = bf16[16,4224]{1,0:T(8,128)(2,1)S(1)} collective-permute-done((bf16[16,4224]{1,0:T(8,128)(2,1)S(1)}, bf16[16,4224]{1,0:T(8,128)(2,1)S(1)}, u32[]{:S(2)}, u32[]{:S(2)}) %collective-permute-start.5) | collective-permute-done | bytes 135200 | tf_op jit(solution)/shard_map/ppermute | solution.py:495
  20.1 2.6 %collective-permute-start.6 = (bf16[16,2176]{1,0:T(8,128)(2,1)S(1)}, bf16[16,2176]{1,0:T(8,128)(2,1)S(1)}, u32[]{:S(2)}, u32[]{:S(2)}) collective-permute-start(bf16[16,2176]{1,0:T(8,128)(2,1)S(1)} %get-tuple-element.22), channel_id=1, source_target_pairs={{0,4},{1,5},{2,6},{3,7},{4,0},{5,1},{6,2},{7,3},{8,12},{9,13},{10,... | collective-permute-start | bytes 208904 | tf_op jit(solution)/shard_map/ppermute | solution.py:495
  22.7 0.0 collective-permute-done.pool_v
  22.7 2.0 %place.3 = bf16[16,8,64,256]{3,2,1,0:T(8,128)(2,1)} custom-call(s32[32]{0:T(128)S(1)} %copy-done.2, s32[32]{0:T(128)S(1)} %copy-done.3, s32[8,32]{1,0:T(8,128)S(1)} %bitcast.10, bf16[128,64,256]{2,1,0:T(8,128)(2,1)S(1)} %collective-permute-done.pool_v, bf16[16,8,64,256]{3,2,1,0:T(8,128)(2,1)} %place.2.refs_0_), custom_call_target="tpu_custom_call", output_to_operand_aliasing={{}: (4, {})} | custom-call | bytes 4194304 | tf_op jit(solution)/shard_map/place/pallas_call | solution.py:389
  24.8 0.6 %collective-permute-done.6.rest_4_ = bf16[16,2176]{1,0:T(8,128)(2,1)S(1)} collective-permute-done((bf16[16,2176]{1,0:T(8,128)(2,1)S(1)}, bf16[16,2176]{1,0:T(8,128)(2,1)S(1)}, u32[]{:S(2)}, u32[]{:S(2)}) %collective-permute-start.6) | collective-permute-done | bytes 69664 | tf_op jit(solution)/shard_map/ppermute | solution.py:495
  25.3 0.0 collective-permute-done.2.other_up_ref
  25.4 1.0 %finish.1 = bf16[2,16,1024]{2,1,0:T(8,128)(2,1)} custom-call(f32[32,8]{1,0:T(8,128)S(1)} %get-tuple-element.19.slot_ref, bf16[4,64,1024]{2,1,0:T(8,128)(2,1)S(1)} %copy-done, bf16[4,64,1024]{2,1,0:T(8,128)(2,1)S(1)} %collective-permute-done.2.other_up_ref, bf16[32,2176]{1,0:T(8,128)(2,1)S(1)} %sort.1.rows_ref, f32[16,128]{1,0:T(8,128)S(1)} %get-tuple-element.21.shrink_ref, ...), custom_call_target="tpu_custom_call" | custom-call | tf_op jit(solution)/shard_map/finish/pallas_call | solution.py:512
  (9 shorter events, 0.1 us)
Async XLA Ops:
  0.6 7.0 %slice-start = ((s8[16777216]{0:T(1024)(128)(4,1)}), s8[4194304]{0:T(1024)(128)(4,1)S(1)}, s32[]{:S(2)}) async-start(s8[16777216]{0:T(1024)(128)(4,1)} %bitcast.6), calls=%async_computation | async-start | bytes 8388608
  0.6 7.0 %slice-start.1 = ((s8[16777216]{0:T(1024)(128)(4,1)}), s8[4194304]{0:T(1024)(128)(4,1)S(1)}, s32[]{:S(2)}) async-start(s8[16777216]{0:T(1024)(128)(4,1)} %bitcast.6), calls=%async_computation.1 | async-start | bytes 8388608
  0.7 7.0 %slice-start.2 = ((s8[16777216]{0:T(1024)(128)(4,1)}), s8[4194304]{0:T(1024)(128)(4,1)S(1)}, s32[]{:S(2)}) async-start(s8[16777216]{0:T(1024)(128)(4,1)} %bitcast.6), calls=%async_computation.2 | async-start | bytes 8388608
  0.7 7.3 %slice-start.3 = ((s8[16777216]{0:T(1024)(128)(4,1)}), s8[4194304]{0:T(1024)(128)(4,1)S(1)}, s32[]{:S(2)}) async-start(s8[16777216]{0:T(1024)(128)(4,1)} %bitcast.6), calls=%async_computation.3 | async-start | bytes 8388608
  6.1 1.4 %collective-permute-start.1 = (bf16[16,2176]{1,0:T(8,128)(2,1)S(1)}, bf16[16,2176]{1,0:T(8,128)(2,1)S(1)}, u32[]{:S(2)}, u32[]{:S(2)}) collective-permute-start(bf16[16,2176]{1,0:T(8,128)(2,1)S(1)} %get-tuple-element.16), channel_id=1, source_target_pairs={{0,8},{8,0},{1,9},{9,1},{2,10},{10,2},{3,11},{11,3},{4,12},{12,4},... | collective-permute-start | bytes 208904 | tf_op jit(solution)/shard_map/ppermute | solution.py:486
  8.8 9.7 %collective-permute-start.3 = (bf16[16,4224]{1,0:T(8,128)(2,1)S(1)}, bf16[16,4224]{1,0:T(8,128)(2,1)S(1)}, u32[]{:S(2)}, u32[]{:S(2)}) collective-permute-start(bf16[16,4224]{1,0:T(8,128)(2,1)S(1)} %message.5), channel_id=1, source_target_pairs={{0,3},{1,2},{2,1},{3,0},{4,7},{5,6},{6,5},{7,4},{8,11},{9,10},{10,... | collective-permute-start | bytes 405512 | tf_op jit(solution)/shard_map/ppermute | solution.py:495
  13.6 1.5 %copy-start = (bf16[4,64,1024]{2,1,0:T(8,128)(2,1)S(1)}, bf16[4,64,1024]{2,1,0:T(8,128)(2,1)}, u32[]{:S(2)}) copy-start(bf16[4,64,1024]{2,1,0:T(8,128)(2,1)} %up_ref.1) | copy-start | bytes 1572868
  13.6 2.0 %copy-start.1 = (s32[32,8]{0,1:T(8,128)S(1)}, s32[32,8]{0,1:T(8,128)}, u32[]{:S(2)}) copy-start(s32[32,8]{0,1:T(8,128)} %param.19) | copy-start | bytes 3076
  13.6 2.0 %copy-start.2 = (s32[32]{0:T(128)S(1)}, s32[32]{0:T(128)}, u32[]{:S(2)}) copy-start(s32[32]{0:T(128)} %order_ref.5) | copy-start | bytes 388
  13.7 2.0 %copy-start.3 = (s32[32]{0:T(128)S(1)}, s32[32]{0:T(128)}, u32[]{:S(2)}) copy-start(s32[32]{0:T(128)} %lengths_ref.5) | copy-start | bytes 388
  13.7 5.8 %collective-permute-start.4 = (bf16[16,4224]{1,0:T(8,128)(2,1)S(1)}, bf16[16,4224]{1,0:T(8,128)(2,1)S(1)}, u32[]{:S(2)}, u32[]{:S(2)}) collective-permute-start(bf16[16,4224]{1,0:T(8,128)(2,1)S(1)} %message.6), channel_id=1, source_target_pairs={{0,2},{1,3},{2,0},{3,1},{4,6},{5,7},{6,4},{7,5},{8,10},{9,11},{10,... | collective-permute-start | bytes 405512 | tf_op jit(solution)/shard_map/ppermute | solution.py:495
  15.0 5.0 %collective-permute-start.5 = (bf16[16,4224]{1,0:T(8,128)(2,1)S(1)}, bf16[16,4224]{1,0:T(8,128)(2,1)S(1)}, u32[]{:S(2)}, u32[]{:S(2)}) collective-permute-start(bf16[16,4224]{1,0:T(8,128)(2,1)S(1)} %message.7), channel_id=1, source_target_pairs={{0,1},{1,0},{2,3},{3,2},{4,5},{5,4},{6,7},{7,6},{8,9},{9,8},{10,11... | collective-permute-start | bytes 405512 | tf_op jit(solution)/shard_map/ppermute | solution.py:495
  15.1 7.6 %collective-permute-start = (bf16[128,64,256]{2,1,0:T(8,128)(2,1)S(1)}, bf16[128,64,256]{2,1,0:T(8,128)(2,1)S(1)}, u32[]{:S(2)}, u32[]{:S(2)}) collective-permute-start(bf16[128,64,256]{2,1,0:T(8,128)(2,1)S(1)} %get-tuple-element.13.pool_v), channel_id=1, source_target_pairs={{0,8},{8,0},{1,9},{9,1},{2,10},{10,2},{3,11},{11,3},{4,12},{12,4},... | collective-permute-start | bytes 12582920 | tf_op jit(solution)/shard_map/ppermute | solution.py:503
  15.1 10.2 %collective-permute-start.2 = (bf16[4,64,1024]{2,1,0:T(8,128)(2,1)S(1)}, bf16[4,64,1024]{2,1,0:T(8,128)(2,1)S(1)}, u32[]{:S(2)}, u32[]{:S(2)}) collective-permute-start(bf16[4,64,1024]{2,1,0:T(8,128)(2,1)S(1)} %copy-done), channel_id=1, source_target_pairs={{0,8},{8,0},{1,9},{9,1},{2,10},{10,2},{3,11},{11,3},{4,12},{12,4},... | collective-permute-start | bytes 1572872 | tf_op jit(solution)/shard_map/ppermute | solution.py:479
  20.1 5.3 %collective-permute-start.6 = (bf16[16,2176]{1,0:T(8,128)(2,1)S(1)}, bf16[16,2176]{1,0:T(8,128)(2,1)S(1)}, u32[]{:S(2)}, u32[]{:S(2)}) collective-permute-start(bf16[16,2176]{1,0:T(8,128)(2,1)S(1)} %get-tuple-element.22), channel_id=1, source_target_pairs={{0,4},{1,5},{2,6},{3,7},{4,0},{5,1},{6,2},{7,3},{8,12},{9,13},{10,... | collective-permute-start | bytes 208904 | tf_op jit(solution)/shard_map/ppermute | solution.py:495

commit v8 on v7

--- a/solution.py
+++ b/solution.py
@@ -154,7 +154,7 @@
         slot_of = jnp.where(here, away * slots + adapter_ref[request], slot_of)
     wanted = wanted + step_of * half
     turn_ref[...] = one_hot(iota(turn_ref.shape, 1) == wanted)
-    slot_ref[...] = one_hot(iota(slot_ref.shape, 1) == slot_of).astype(f32)
+    slot_ref[...] = one_hot(div(iota(slot_ref.shape, 1), rank) == slot_of).astype(f32)
 
     row_index = iota((places * steps * half, 1), 0)
     source = jnp.zeros_like(row_index)
@@ -340,7 +340,7 @@
             pltpu.VMEM((steps * rows // 2, 2 * features + LANES), bf16),
             pltpu.VMEM((steps * rows // 2, 2 * features + LANES), bf16),
             pltpu.VMEM((steps * rows, steps * rows), bf16),
-            pltpu.VMEM((steps * rows, 2 * down.shape[0]), f32),
+            pltpu.VMEM((steps * rows, 2 * down.shape[0] * down.shape[1]), f32),
             pltpu.VMEM(pool.shape, bf16),
         ),
         in_specs=[smem] * 4 + [hbm] * 5,
@@ -432,26 +432,53 @@
     )(*messages)
 
 
-def finish_kernel(slot_ref, up_ref, other_up_ref, rows_ref, shrink_ref, *rest, home_count):
-    home_refs, across_refs, out_ref = rest[:home_count], rest[home_count:-1], rest[-1]
+def base_kernel(rows_ref, *rest):
+    home_refs, base_ref = rest[:-1], rest[-1]
+    features = base_ref.shape[1]
+    width = 2 * features
+    total = home_refs[0][:, :width]
+    for ref in home_refs[1:]:
+        total = total + ref[:, :width].astype(f32)
+    total = jnp.concatenate([total[:, :features], total[:, features:]], axis=0)
+    base_ref[...] = total + rows_ref[:, features + LANES :].astype(f32)
+
+
+def base_call(rows, home, features):
+    vmem = pl.BlockSpec(memory_space=pltpu.VMEM)
+    return pl.pallas_call(
+        base_kernel,
+        out_shape=pltpu.VMEM((rows.shape[0], features), f32),
+        in_specs=[vmem] * (1 + len(home)),
+        out_specs=vmem,
+        compiler_params=pltpu.CompilerParams(vmem_limit_bytes=SMALL_BYTES),
+        name="base",
+    )(rows, *home)
+
+
+def finish_kernel(slot_ref, up_ref, other_up_ref, base_ref, shrink_ref, *rest):
+    across_refs, out_ref = rest[:-1], rest[-1]
     slots, rank, features = up_ref.shape
     width = 2 * features
-    total, shrink = home_refs[0][:, :width], shrink_ref[...]
-    for ref in home_refs[1:]:
-        total = total + ref[:, :width].astype(f32)
+    shrink = shrink_ref[...]
     for ref in across_refs:
-        total = total + ref[:, :width].astype(f32)
         shrink = shrink + ref[:, width:].astype(f32)
-    total = jnp.concatenate([total[:, :features], total[:, features:]], axis=0)
-    shrink = jnp.concatenate([shrink[:, :rank], shrink[:, LANES // 2 : LANES // 2 + rank]], axis=0)
+    turned = pltpu.roll(shrink, LANES // 2, 1)
+    left = iota(shrink.shape, 1) < LANES // 2
+    shrink = jnp.concatenate(
+        [jnp.where(left, shrink, turned), jnp.where(left, turned, shrink)], axis=0
+    )
     shrink = shrink.astype(bf16).astype(f32)
-    result = total + rows_ref[:, features + LANES :].astype(f32)
+    span = slots * rank
+    wide = jnp.concatenate([shrink] * (2 * span // LANES), axis=1) * slot_ref[...]
+    wide = wide.astype(bf16)
+    result = base_ref[...]
+    for ref in across_refs:
+        result = result + jnp.concatenate(
+            [ref[:, :features], ref[:, features:width]], axis=0
+        ).astype(f32)
     for side, up in enumerate((up_ref, other_up_ref)):
-        wide = jnp.concatenate(
-            [shrink * slot_ref[:, side * slots + n : side * slots + n + 1] for n in range(slots)],
-            axis=1,
-        ).astype(bf16)
-        result = result + adapter_scale * dot(wide, up[...].reshape(slots * rank, features))
+        raised = dot(wide[:, side * span : (side + 1) * span], up[...].reshape(span, features))
+        result = result + adapter_scale * raised
     out_ref[...] = result.astype(bf16).reshape(out_ref.shape)
 
 
@@ -507,16 +534,17 @@
     *across, shrink = merge_call([own] + collected, spans)
     across = [trade(piece, (n * QUAD, n * QUAD)) for n, piece in enumerate(across, 1)]
     placed_cache = place_call(*integers[:3], other_pool, rows, placed)
-    placed_cache, slot = lax.optimization_barrier((placed_cache, slot))
+    placed_cache, own = lax.optimization_barrier((placed_cache, own))
+    base = base_call(rows_in_order, [own] + collected, features)
     vmem = pl.BlockSpec(memory_space=pltpu.VMEM)
     layer_out = pl.pallas_call(
-        functools.partial(finish_kernel, home_count=len(home)),
+        finish_kernel,
         out_shape=jax.ShapeDtypeStruct((steps, rows, features), bf16),
-        in_specs=[vmem] * (5 + len(home) + len(across)),
+        in_specs=[vmem] * (5 + len(across)),
         out_specs=vmem,
         compiler_params=pltpu.CompilerParams(vmem_limit_bytes=SMALL_BYTES),
         name="finish",
-    )(slot, adapter_up_weight, other_up, rows_in_order, shrink, *home, *across)
+    )(slot, adapter_up_weight, other_up, base, shrink, *across)
     return (layer_out, placed_cache.reshape(rows, table_blocks, 1, block_size, width))
 
 

time: 26.5 us -> 26.5 us (level)
    pallas_call x1 -> x2, Pallas kernels: 1.03 us -> 1.01 us  [the longest x1 0.97 us: shards(): pl.pallas_call(finish_kernel, out_shape=jax.ShapeDtypeStruct((steps, rows...]
where the time goes in v8:
time: 26.5 us; the launch traced here: 26.3 us
  Pallas kernels  13.9 us (52%)
  starting transfers between devices  8.32 us (31%)
  waiting for transfers between devices  3.01 us (11%)
  between operations  0.76 us (3%)
  local copies, waits for them, and re-layouts  0.33 us (1%)
    ppermute x4, starting transfers between devices, trade(): return lax.ppermute(message, ('replica', 'tensor'), pairs)  7.3 us
    pallas_call x1, Pallas kernels, attend_call(): pl.pallas_call(attend_kernel, out_shape=(pltpu.VMEM((steps * rows // 2, 2...  5.39 us
    pallas_call x2, Pallas kernels, place_call(): pl.pallas_call(functools.partial(place_kernel, stayed=placed is None), ou...  4 us
    pallas_call x4, Pallas kernels, message_call(): pl.pallas_call(functools.partial(message_kernel, partners=partners), out_...  3.29 us
    ppermute x4, waiting for transfers between devices, trade(): return lax.ppermute(message, ('replica', 'tensor'), pairs)  2.1 us
    pallas_call x1, Pallas kernels, shards(): pl.pallas_call(finish_kernel, out_shape=jax.ShapeDtypeStruct((steps, rows...  0.97 us
    ppermute x1, waiting for transfers between devices, shards(): came = lax.ppermute(leave, 'replica', swap)  0.91 us
  transfers between devices with their start and end apart: 7, of which 4 were waited for; matrix products, arithmetic and copies ran while one was open for 0% of the time, Pallas kernels for 25%

profile of v8, /device:TPU:0, one launch (start us, length us, event | category | flops | bytes accessed | tf_op | source)
XLA Modules:
  0.0 26.3 jit_solution(16702463847971265828)
XLA Ops:
  0.6 0.0 slice-start
  0.6 0.0 slice-start.1
  0.7 0.0 slice-start.2
  0.7 0.0 slice-start.3
  0.7 5.4 %attend.1 = (bf16[16,2176]{1,0:T(8,128)(2,1)S(1)}, bf16[16,2176]{1,0:T(8,128)(2,1)S(1)}, bf16[32,32]{1,0:T(8,128)(2,1)S(1)}, f32[32,512]{1,0:T(8,128)S(1)}, bf16[128,64,256]{2,1,0:T(8,128)(2,1)S(1)}) custom-call(s32[32]{0:T(128)} %order_ref.5, s32[32]{0:T(128)} %lengths_ref.5, s32[8,32]{1,0:T(8,128)} %bitcast.8, s32[32]{0:T(128)} %adapter_ref.1, ...), custom_call_target="tpu_custom_call" | custom-call | flops 40000000000 | bytes 8388608 | tf_op jit(solution)/shard_map/attend/pallas_call | solution.py:337
  6.1 0.5 %collective-permute-start.1 = (bf16[16,2176]{1,0:T(8,128)(2,1)S(1)}, bf16[16,2176]{1,0:T(8,128)(2,1)S(1)}, u32[]{:S(2)}, u32[]{:S(2)}) collective-permute-start(bf16[16,2176]{1,0:T(8,128)(2,1)S(1)} %get-tuple-element.16), channel_id=1, source_target_pairs={{0,8},{8,0},{1,9},{9,1},{2,10},{10,2},{3,11},{11,3},{4,12},{12,4},... | collective-permute-start | bytes 208904 | tf_op jit(solution)/shard_map/ppermute | solution.py:513
  6.6 0.9 %collective-permute-done.1.came_ref = bf16[16,2176]{1,0:T(8,128)(2,1)S(1)} collective-permute-done((bf16[16,2176]{1,0:T(8,128)(2,1)S(1)}, bf16[16,2176]{1,0:T(8,128)(2,1)S(1)}, u32[]{:S(2)}, u32[]{:S(2)}) %collective-permute-start.1) | collective-permute-done | bytes 69664 | tf_op jit(solution)/shard_map/ppermute | solution.py:513
  7.5 0.2 sort.1.rows_ref
  7.7 0.3 %slice-done.3 = s8[4194304]{0:T(1024)(128)(4,1)S(1)} async-done(((s8[16777216]{0:T(1024)(128)(4,1)}), s8[4194304]{0:T(1024)(128)(4,1)S(1)}, s32[]{:S(2)}) %slice-start.3) | async-done | bytes 4194328
  8.0 0.8 %message.5 = bf16[16,4224]{1,0:T(8,128)(2,1)S(1)} custom-call(bf16[32,2176]{1,0:T(8,128)(2,1)S(1)} %sort.1.rows_ref, bf16[16,2176]{1,0:T(8,128)(2,1)S(1)} %collective-permute-done.1.came_ref, bf16[1024,8192]{1,0:T(8,128)(2,1)S(1)} %bitcast.7), custom_call_target="tpu_custom_call" | custom-call | tf_op jit(solution)/shard_map/message/pallas_call | solution.py:374
  8.8 4.0 %collective-permute-start.3 = (bf16[16,4224]{1,0:T(8,128)(2,1)S(1)}, bf16[16,4224]{1,0:T(8,128)(2,1)S(1)}, u32[]{:S(2)}, u32[]{:S(2)}) collective-permute-start(bf16[16,4224]{1,0:T(8,128)(2,1)S(1)} %message.5), channel_id=1, source_target_pairs={{0,3},{1,2},{2,1},{3,0},{4,7},{5,6},{6,5},{7,4},{8,11},{9,10},{10,... | collective-permute-start | bytes 405512 | tf_op jit(solution)/shard_map/ppermute | solution.py:522
  12.8 0.8 %message.6 = bf16[16,4224]{1,0:T(8,128)(2,1)S(1)} custom-call(bf16[32,2176]{1,0:T(8,128)(2,1)S(1)} %sort.1.rows_ref, bf16[16,2176]{1,0:T(8,128)(2,1)S(1)} %collective-permute-done.1.came_ref, bf16[1024,8192]{1,0:T(8,128)(2,1)S(1)} %bitcast.7), custom_call_target="tpu_custom_call" | custom-call | tf_op jit(solution)/shard_map/message/pallas_call | solution.py:374
  13.6 0.0 copy-start.1
  13.6 0.0 copy-start.2
  13.7 0.0 copy-start.3
  13.7 0.5 %collective-permute-start.4 = (bf16[16,4224]{1,0:T(8,128)(2,1)S(1)}, bf16[16,4224]{1,0:T(8,128)(2,1)S(1)}, u32[]{:S(2)}, u32[]{:S(2)}) collective-permute-start(bf16[16,4224]{1,0:T(8,128)(2,1)S(1)} %message.6), channel_id=1, source_target_pairs={{0,2},{1,3},{2,0},{3,1},{4,6},{5,7},{6,4},{7,5},{8,10},{9,11},{10,... | collective-permute-start | bytes 405512 | tf_op jit(solution)/shard_map/ppermute | solution.py:522
  14.2 0.8 %message.7 = bf16[16,4224]{1,0:T(8,128)(2,1)S(1)} custom-call(bf16[32,2176]{1,0:T(8,128)(2,1)S(1)} %sort.1.rows_ref, bf16[16,2176]{1,0:T(8,128)(2,1)S(1)} %collective-permute-done.1.came_ref, bf16[1024,8192]{1,0:T(8,128)(2,1)S(1)} %bitcast.7), custom_call_target="tpu_custom_call" | custom-call | tf_op jit(solution)/shard_map/message/pallas_call | solution.py:374
  15.0 0.1 collective-permute-start.5
  15.1 0.0 collective-permute-start.2
  15.1 0.5 %collective-permute-start = (bf16[4,64,1024]{2,1,0:T(8,128)(2,1)S(1)}, bf16[4,64,1024]{2,1,0:T(8,128)(2,1)S(1)}, u32[]{:S(2)}, u32[]{:S(2)}) collective-permute-start(bf16[4,64,1024]{2,1,0:T(8,128)(2,1)S(1)} %copy-done), channel_id=1, source_target_pairs={{0,8},{8,0},{1,9},{9,1},{2,10},{10,2},{3,11},{11,3},{4,12},{12,4},... | collective-permute-start | bytes 1572872 | tf_op jit(solution)/shard_map/ppermute | solution.py:506
  15.7 0.0 copy-done.1
  15.7 2.0 %place.2.refs_0_ = bf16[16,8,64,256]{3,2,1,0:T(8,128)(2,1)} custom-call(s32[32]{0:T(128)S(1)} %copy-done.2, s32[32]{0:T(128)S(1)} %copy-done.3, s32[8,32]{1,0:T(8,128)S(1)} %bitcast.9, bf16[128,64,256]{2,1,0:T(8,128)(2,1)S(1)} %get-tuple-element.17.pool_v), custom_call_target="tpu_custom_call" | custom-call | bytes 4194304 | tf_op jit(solution)/shard_map/place/pallas_call | solution.py:389
  17.7 0.8 %message.4.rest_0_.refs_0_ = f32[16,4224]{1,0:T(8,128)S(1)} custom-call(bf16[32,2176]{1,0:T(8,128)(2,1)S(1)} %sort.1.rows_ref, bf16[16,2176]{1,0:T(8,128)(2,1)S(1)} %collective-permute-done.1.came_ref, bf16[1024,8192]{1,0:T(8,128)(2,1)S(1)} %bitcast.7), custom_call_target="tpu_custom_call" | custom-call | tf_op jit(solution)/shard_map/message/pallas_call | solution.py:374
  18.5 0.0 collective-permute-done.3.rest_1_.refs_1_
  18.5 0.9 %collective-permute-done.4.rest_2_.refs_2_ = bf16[16,4224]{1,0:T(8,128)(2,1)S(1)} collective-permute-done((bf16[16,4224]{1,0:T(8,128)(2,1)S(1)}, bf16[16,4224]{1,0:T(8,128)(2,1)S(1)}, u32[]{:S(2)}, u32[]{:S(2)}) %collective-permute-start.4) | collective-permute-done | bytes 135200 | tf_op jit(solution)/shard_map/ppermute | solution.py:522
  19.4 0.6 %collective-permute-done.5.rest_3_.refs_3_ = bf16[16,4224]{1,0:T(8,128)(2,1)S(1)} collective-permute-done((bf16[16,4224]{1,0:T(8,128)(2,1)S(1)}, bf16[16,4224]{1,0:T(8,128)(2,1)S(1)}, u32[]{:S(2)}, u32[]{:S(2)}) %collective-permute-start.5) | collective-permute-done | bytes 135200 | tf_op jit(solution)/shard_map/ppermute | solution.py:522
  20.1 2.6 %collective-permute-start.6 = (bf16[16,2176]{1,0:T(8,128)(2,1)S(1)}, bf16[16,2176]{1,0:T(8,128)(2,1)S(1)}, u32[]{:S(2)}, u32[]{:S(2)}) collective-permute-start(bf16[16,2176]{1,0:T(8,128)(2,1)S(1)} %get-tuple-element.22), channel_id=1, source_target_pairs={{0,4},{1,5},{2,6},{3,7},{4,0},{5,1},{6,2},{7,3},{8,12},{9,13},{10,... | collective-permute-start | bytes 208904 | tf_op jit(solution)/shard_map/ppermute | solution.py:522
  22.7 0.0 collective-permute-done.2.pool_v
  22.7 2.0 %place.3 = bf16[16,8,64,256]{3,2,1,0:T(8,128)(2,1)} custom-call(s32[32]{0:T(128)S(1)} %copy-done.2, s32[32]{0:T(128)S(1)} %copy-done.3, s32[8,32]{1,0:T(8,128)S(1)} %bitcast.10, bf16[128,64,256]{2,1,0:T(8,128)(2,1)S(1)} %collective-permute-done.2.pool_v, bf16[16,8,64,256]{3,2,1,0:T(8,128)(2,1)} %place.2.refs_0_), custom_call_target="tpu_custom_call", output_to_operand_aliasing={{}: (4, {})} | custom-call | bytes 4194304 | tf_op jit(solution)/shard_map/place/pallas_call | solution.py:389
  24.7 0.6 %collective-permute-done.6.rest_0_ = bf16[16,2176]{1,0:T(8,128)(2,1)S(1)} collective-permute-done((bf16[16,2176]{1,0:T(8,128)(2,1)S(1)}, bf16[16,2176]{1,0:T(8,128)(2,1)S(1)}, u32[]{:S(2)}, u32[]{:S(2)}) %collective-permute-start.6) | collective-permute-done | bytes 69664 | tf_op jit(solution)/shard_map/ppermute | solution.py:522
  25.3 0.0 collective-permute-done.other_up_ref
  25.3 1.0 %finish.1 = bf16[2,16,1024]{2,1,0:T(8,128)(2,1)} custom-call(f32[32,512]{1,0:T(8,128)S(1)} %get-tuple-element.13.slot_ref, bf16[4,64,1024]{2,1,0:T(8,128)(2,1)S(1)} %copy-done, bf16[4,64,1024]{2,1,0:T(8,128)(2,1)S(1)} %collective-permute-done.other_up_ref, f32[32,1024]{1,0:T(8,128)S(1)} %base.1.base_ref, f32[16,128]{1,0:T(8,128)S(1)} %get-tuple-element.21.shrink_ref, ...), custom_call_target="tpu_custom_call" | custom-call | tf_op jit(solution)/shard_map/finish/pallas_call | solution.py:540
  (10 shorter events, 0.1 us)
Async XLA Ops:
  0.6 7.0 %slice-start = ((s8[16777216]{0:T(1024)(128)(4,1)}), s8[4194304]{0:T(1024)(128)(4,1)S(1)}, s32[]{:S(2)}) async-start(s8[16777216]{0:T(1024)(128)(4,1)} %bitcast.6), calls=%async_computation | async-start | bytes 8388608
  0.6 7.0 %slice-start.1 = ((s8[16777216]{0:T(1024)(128)(4,1)}), s8[4194304]{0:T(1024)(128)(4,1)S(1)}, s32[]{:S(2)}) async-start(s8[16777216]{0:T(1024)(128)(4,1)} %bitcast.6), calls=%async_computation.1 | async-start | bytes 8388608
  0.7 7.0 %slice-start.2 = ((s8[16777216]{0:T(1024)(128)(4,1)}), s8[4194304]{0:T(1024)(128)(4,1)S(1)}, s32[]{:S(2)}) async-start(s8[16777216]{0:T(1024)(128)(4,1)} %bitcast.6), calls=%async_computation.2 | async-start | bytes 8388608
  0.7 7.3 %slice-start.3 = ((s8[16777216]{0:T(1024)(128)(4,1)}), s8[4194304]{0:T(1024)(128)(4,1)S(1)}, s32[]{:S(2)}) async-start(s8[16777216]{0:T(1024)(128)(4,1)} %bitcast.6), calls=%async_computation.3 | async-start | bytes 8388608
  6.1 1.4 %collective-permute-start.1 = (bf16[16,2176]{1,0:T(8,128)(2,1)S(1)}, bf16[16,2176]{1,0:T(8,128)(2,1)S(1)}, u32[]{:S(2)}, u32[]{:S(2)}) collective-permute-start(bf16[16,2176]{1,0:T(8,128)(2,1)S(1)} %get-tuple-element.16), channel_id=1, source_target_pairs={{0,8},{8,0},{1,9},{9,1},{2,10},{10,2},{3,11},{11,3},{4,12},{12,4},... | collective-permute-start | bytes 208904 | tf_op jit(solution)/shard_map/ppermute | solution.py:513
  8.8 9.7 %collective-permute-start.3 = (bf16[16,4224]{1,0:T(8,128)(2,1)S(1)}, bf16[16,4224]{1,0:T(8,128)(2,1)S(1)}, u32[]{:S(2)}, u32[]{:S(2)}) collective-permute-start(bf16[16,4224]{1,0:T(8,128)(2,1)S(1)} %message.5), channel_id=1, source_target_pairs={{0,3},{1,2},{2,1},{3,0},{4,7},{5,6},{6,5},{7,4},{8,11},{9,10},{10,... | collective-permute-start | bytes 405512 | tf_op jit(solution)/shard_map/ppermute | solution.py:522
  13.6 1.5 %copy-start = (bf16[4,64,1024]{2,1,0:T(8,128)(2,1)S(1)}, bf16[4,64,1024]{2,1,0:T(8,128)(2,1)}, u32[]{:S(2)}) copy-start(bf16[4,64,1024]{2,1,0:T(8,128)(2,1)} %up_ref.1) | copy-start | bytes 1572868
  13.6 2.0 %copy-start.1 = (s32[32,8]{0,1:T(8,128)S(1)}, s32[32,8]{0,1:T(8,128)}, u32[]{:S(2)}) copy-start(s32[32,8]{0,1:T(8,128)} %param.19) | copy-start | bytes 3076
  13.6 2.0 %copy-start.2 = (s32[32]{0:T(128)S(1)}, s32[32]{0:T(128)}, u32[]{:S(2)}) copy-start(s32[32]{0:T(128)} %order_ref.5) | copy-start | bytes 388
  13.7 2.0 %copy-start.3 = (s32[32]{0:T(128)S(1)}, s32[32]{0:T(128)}, u32[]{:S(2)}) copy-start(s32[32]{0:T(128)} %lengths_ref.5) | copy-start | bytes 388
  13.7 5.8 %collective-permute-start.4 = (bf16[16,4224]{1,0:T(8,128)(2,1)S(1)}, bf16[16,4224]{1,0:T(8,128)(2,1)S(1)}, u32[]{:S(2)}, u32[]{:S(2)}) collective-permute-start(bf16[16,4224]{1,0:T(8,128)(2,1)S(1)} %message.6), channel_id=1, source_target_pairs={{0,2},{1,3},{2,0},{3,1},{4,6},{5,7},{6,4},{7,5},{8,10},{9,11},{10,... | collective-permute-start | bytes 405512 | tf_op jit(solution)/shard_map/ppermute | solution.py:522
  15.0 5.0 %collective-permute-start.5 = (bf16[16,4224]{1,0:T(8,128)(2,1)S(1)}, bf16[16,4224]{1,0:T(8,128)(2,1)S(1)}, u32[]{:S(2)}, u32[]{:S(2)}) collective-permute-start(bf16[16,4224]{1,0:T(8,128)(2,1)S(1)} %message.7), channel_id=1, source_target_pairs={{0,1},{1,0},{2,3},{3,2},{4,5},{5,4},{6,7},{7,6},{8,9},{9,8},{10,11... | collective-permute-start | bytes 405512 | tf_op jit(solution)/shard_map/ppermute | solution.py:522
  15.1 7.6 %collective-permute-start.2 = (bf16[128,64,256]{2,1,0:T(8,128)(2,1)S(1)}, bf16[128,64,256]{2,1,0:T(8,128)(2,1)S(1)}, u32[]{:S(2)}, u32[]{:S(2)}) collective-permute-start(bf16[128,64,256]{2,1,0:T(8,128)(2,1)S(1)} %get-tuple-element.17.pool_v), channel_id=1, source_target_pairs={{0,8},{8,0},{1,9},{9,1},{2,10},{10,2},{3,11},{11,3},{4,12},{12,4},... | collective-permute-start | bytes 12582920 | tf_op jit(solution)/shard_map/ppermute | solution.py:530
  15.1 10.2 %collective-permute-start = (bf16[4,64,1024]{2,1,0:T(8,128)(2,1)S(1)}, bf16[4,64,1024]{2,1,0:T(8,128)(2,1)S(1)}, u32[]{:S(2)}, u32[]{:S(2)}) collective-permute-start(bf16[4,64,1024]{2,1,0:T(8,128)(2,1)S(1)} %copy-done), channel_id=1, source_target_pairs={{0,8},{8,0},{1,9},{9,1},{2,10},{10,2},{3,11},{11,3},{4,12},{12,4},... | collective-permute-start | bytes 1572872 | tf_op jit(solution)/shard_map/ppermute | solution.py:506
  20.1 5.3 %collective-permute-start.6 = (bf16[16,2176]{1,0:T(8,128)(2,1)S(1)}, bf16[16,2176]{1,0:T(8,128)(2,1)S(1)}, u32[]{:S(2)}, u32[]{:S(2)}) collective-permute-start(bf16[16,2176]{1,0:T(8,128)(2,1)S(1)} %get-tuple-element.22), channel_id=1, source_target_pairs={{0,4},{1,5},{2,6},{3,7},{4,0},{5,1},{6,2},{7,3},{8,12},{9,13},{10,... | collective-permute-start | bytes 208904 | tf_op jit(solution)/shard_map/ppermute | solution.py:522
